TPU v7x, 256 devices: a whole 4x4x8 slice. The times are simulated.
256 devices in a mesh: query: 8 (over x, y_hi), corpus: 32 (over y_lo, z, core).
Axes of the slice: x: 4, y: 4 (y_hi: 2, y_lo: 2; y = y_hi * 2 + y_lo), z: 8, core: 2. Of those that a mesh axis runs over, the one named last changes fastest.
Arguments:
- teacher_query: bfloat16 [32768, 1024], P('query'), may hold values from -70 to 70
- student_query: bfloat16 [32768, 384], P('query'), may hold values from -110 to 110
- teacher_passages: bfloat16 [16384, 1024], P(('query', 'corpus')), may hold values from -40 to 40
- student_passages: bfloat16 [16384, 384], P(('query', 'corpus')), may hold values from -40 to 40
Outputs:
- divergence: float32 [32768], P(('query', 'corpus'))
- grad_query: float32 [32768, 384], P(('query', 'corpus'))
- grad_passage: float32 [16384, 384], P(('query', 'corpus'))
All inputs are finite; a program needn't handle non-finite values.
Results may differ from a plain program's by a relative error of at most 0.0044.
Values may be sent and summed in bfloat16 or wider, within the bound.
A program may use at most 128 MiB of HBM per device.

v0:
```python
import functools
import math

import jax
import jax.numpy as jnp
from jax import lax
from jax.experimental import pallas as pl
from jax.experimental.pallas import tpu as pltpu
from jax.sharding import PartitionSpec as P

NX, NYH, NYL, NZ, NCORE = 4, 2, 2, 8, 2
OWN = 64
ROWS = 128
DT, DS = 1024, 384
BATCHES = 4
BATCH = 256
GROUP = NYL * ROWS
OWNERS = NYL * NZ
HALF = OWN // 2
ZF = 192
YF = DS - ZF
LOG2E = math.log2(math.e)
LN2 = math.log(2.0)
F32, BF16 = jnp.float32, jnp.bfloat16
MESH = pl.DeviceIdType.MESH

SELF, LEFT, RIGHT, FAR = 0, 1, 2, 3


def place(h, where, core):
    if where == SELF:
        return 0, core * 2 + h
    if where == FAR:
        return 3, core * 2 + h
    return 1 + h, core * 2 + (where - LEFT)


def nn(a, b):
    return lax.dot_general(a, b, (((1,), (0,)), ((), ())), preferred_element_type=F32)


class Messages:
    def __init__(self):
        self.numbers = {}

    def __call__(self, name):
        return self.numbers.setdefault(name, len(self.numbers))


MESSAGES = 80
VMEM_BYTES = 60 * 1024 * 1024


def kernel(
    tq_hbm, sq_hbm, tp_hbm, sp_hbm,
    gq_out, gp_out, div_out,
    tq, sq, tqt, sqt, pbuf, spt, tw, sw, gt, stat, gq,
    stat_send, stat_recv, res_recv,
    z_send_r, z_recv_r, z_send_l, z_recv_l, z_pair_send, z_pair_recv,
    y_pair_send, y_pair_recv, y_send_r, y_recv_r, y_send_l, y_recv_l,
    gp, gps_send, gps_recv, gp1_send, gp1_recv, gp2_send, gp2_recv, gp3_send, gp3_recv,
    load_sem, send_sem, recv_sem, st_send_sem, st_recv_sem, rs_send_sem, rs_recv_sem,
):
    t_scale = DT ** (-0.5) * LOG2E
    s_scale = DS ** (-0.5) * LOG2E
    factor = DS ** (-0.5)
    q = lax.axis_index("query")
    c = lax.axis_index("corpus")
    x, yh = q // NYH, q % NYH
    yl, z, k = c // (NZ * NCORE), (c // NCORE) % NZ, c % NCORE
    me = yl * NZ + z

    def at(x_, yh_, yl_, z_, k_):
        return (x_ * NYH + yh_, (yl_ * NZ + z_) * NCORE + k_)

    right, left = at((x + 1) % NX, yh, yl, z, k), at((x + NX - 1) % NX, yh, yl, z, k)
    across = at(x, 1 - yh, yl, z, k)
    sibling = at(x, yh, yl, z, 1 - k)
    up, down = at(x, yh, yl, (z + 1) % NZ, k), at(x, yh, yl, (z + NZ - 1) % NZ, k)
    y_mate = at(x, yh, 1 - yl, z, k)

    def owner(m):
        return at(x, yh, m // NZ, m % NZ, k)

    def slot(h, where, core, half=None):
        b, s = place(h, where, core)
        if half is None:
            return pbuf.at[b, s]
        return pbuf.at[b, s, pl.ds(half * HALF, HALF)]

    loads = [
        pltpu.make_async_copy(tp_hbm, pbuf.at[0, 0, :, pl.ds(0, DT)], load_sem.at[0]),
        pltpu.make_async_copy(sp_hbm, pbuf.at[0, 0, :, pl.ds(DT, DS)], load_sem.at[1]),
    ]
    for y in range(NYL):
        loads.append(pltpu.make_async_copy(tq_hbm.at[y, :, k], tq.at[:, y], load_sem.at[2 + y]))
        loads.append(pltpu.make_async_copy(sq_hbm.at[y, :, k], sq.at[:, y], load_sem.at[4 + y]))
    for load in loads:
        load.start()

    barrier = pltpu.get_barrier_semaphore()
    for device in (right, left, across, sibling):
        pl.semaphore_signal(barrier, inc=1, device_id=device, device_id_type=MESH)

    def greet(i, carry):
        pl.semaphore_signal(barrier, inc=1, device_id=owner((me + i) % OWNERS), device_id_type=MESH)
        return carry

    lax.fori_loop(1, OWNERS, greet, 0)
    pl.semaphore_wait(barrier, 4 + OWNERS - 1)
    loads[0].wait()
    loads[1].wait()

    number = Messages()
    sent = []

    def message(src, dst, name, device):
        i = number(name)
        return pltpu.make_async_remote_copy(
            src_ref=src, dst_ref=dst, send_sem=send_sem.at[i], recv_sem=recv_sem.at[i],
            device_id=device, device_id_type=MESH,
        )

    def send(src, dst, name, device):
        copy = message(src, dst, name, device)
        copy.start()
        sent.append(copy)

    def received(ref, name):
        message(ref, ref, name, sibling).wait_recv()

    def to_sides(h):
        for first in (0, 1):
            half = first
            send(slot(h, SELF, 0, half), slot(h, LEFT, 0, half), ("p", h, LEFT, half), right)
            half = 1 - first
            send(slot(h, SELF, 0, half), slot(h, RIGHT, 0, half), ("p", h, RIGHT, half), left)

    def to_sibling(h, where):
        send(slot(h, where, 0), slot(h, where, 1), ("sib", h, where), sibling)

    def side_halves_on(h):
        received(slot(h, LEFT, 0, 0), ("p", h, LEFT, 0))
        send(slot(h, LEFT, 0, 0), slot(h, FAR, 0, 0), ("p", h, FAR, 0), right)
        received(slot(h, RIGHT, 0, 1), ("p", h, RIGHT, 1))
        send(slot(h, RIGHT, 0, 1), slot(h, FAR, 0, 1), ("p", h, FAR, 1), left)

    def sides_to_sibling(h):
        received(slot(h, LEFT, 0, 1), ("p", h, LEFT, 1))
        to_sibling(h, LEFT)
        received(slot(h, RIGHT, 0, 0), ("p", h, RIGHT, 0))
        to_sibling(h, RIGHT)

    def far_to_sibling(h):
        received(slot(h, FAR, 0, 0), ("p", h, FAR, 0))
        received(slot(h, FAR, 0, 1), ("p", h, FAR, 1))
        to_sibling(h, FAR)

    def from_sibling(h, where):
        received(slot(h, where, 1), ("sib", h, where))

    for half in (0, 1):
        send(slot(0, SELF, 0, half), slot(1, SELF, 0, half), ("p", 1, SELF, half), across)
    to_sides(0)
    to_sibling(0, SELF)

    def scores(b, first, count):
        def tile(n, carry):
            passages = pbuf[b].reshape(BATCH, DT + DS)
            t = nn(passages[:, :DT], tqt[n]) * t_scale
            s = nn(passages[:, DT:], sqt[n]) * s_scale
            t_max = jnp.max(t, axis=0, keepdims=True)
            s_max = jnp.max(s, axis=0, keepdims=True)
            t_weight = jnp.exp2(t - t_max)
            s_weight = jnp.exp2(s - s_max)
            tw[n, b] = t_weight
            sw[n, b] = s_weight
            t_sum = jnp.sum(t_weight, axis=0, keepdims=True)
            s_sum = jnp.sum(s_weight, axis=0, keepdims=True)
            cross = jnp.sum(t_weight * (t - s), axis=0, keepdims=True)
            stat[n, b] = jnp.concatenate([t_max, t_sum, s_max, s_sum, cross, cross, cross, cross], axis=0)
            return carry

        lax.fori_loop(first, first + count, tile, 0, unroll=2)

    def turn(b):
        spt[b] = pbuf[b].reshape(BATCH, DT + DS)[:, DT:].T

    def turn_queries(first, count):
        def body(n, carry):
            tqt[n] = tq[n].reshape(GROUP, DT).T
            sqt[n] = sq[n].reshape(GROUP, DS).T
            return carry

        lax.fori_loop(first, first + count, body, 0)

    for load in loads[2:]:
        load.wait()
    turn_queries(0, 4)
    side_halves_on(0)
    turn_queries(4, 4)
    sides_to_sibling(0)
    for half in (0, 1):
        received(slot(1, SELF, 0, half), ("p", 1, SELF, half))
    to_sides(1)
    to_sibling(1, SELF)
    from_sibling(0, LEFT)
    from_sibling(0, RIGHT)
    scores(1, 0, 4)
    far_to_sibling(0)
    scores(1, 4, 4)
    side_halves_on(1)
    from_sibling(0, SELF)
    from_sibling(1, SELF)
    scores(0, 0, 4)
    sides_to_sibling(1)
    scores(0, 4, 4)
    from_sibling(1, LEFT)
    from_sibling(1, RIGHT)
    scores(2, 0, 4)
    far_to_sibling(1)
    scores(2, 4, 4)
    from_sibling(0, FAR)
    from_sibling(1, FAR)

    def joined(parts):
        t_max = functools.reduce(jnp.maximum, [p[0:1] for p in parts])
        s_max = functools.reduce(jnp.maximum, [p[2:3] for p in parts])
        t_in = [jnp.exp2(p[0:1] - t_max) for p in parts]
        s_in = [jnp.exp2(p[2:3] - s_max) for p in parts]
        t_sum = functools.reduce(jnp.add, [p[1:2] * w for p, w in zip(parts, t_in)])
        s_sum = functools.reduce(jnp.add, [p[3:4] * w for p, w in zip(parts, s_in)])
        cross = functools.reduce(jnp.add, [p[4:5] * w for p, w in zip(parts, t_in)])
        return t_max, t_sum, s_max, s_sum, cross

    def stat_copy(m_to, m_slot):
        return pltpu.make_async_remote_copy(
            src_ref=stat_send.at[m_to], dst_ref=stat_recv.at[m_slot],
            send_sem=st_send_sem.at[m_to], recv_sem=st_recv_sem.at[m_slot],
            device_id=owner(m_to), device_id_type=MESH,
        )

    def res_copy(m_to, m_slot):
        return pltpu.make_async_remote_copy(
            src_ref=res_recv.at[m_slot], dst_ref=res_recv.at[m_slot],
            send_sem=rs_send_sem.at[m_to], recv_sem=rs_recv_sem.at[m_slot],
            device_id=owner(m_to), device_id_type=MESH,
        )

    def each_other(step):
        def body(i, carry):
            step((me + i) % OWNERS)
            return carry

        lax.fori_loop(1, OWNERS, body, 0)

    for first in (0, 4):
        scores(3, first, 4)
        for n in range(first, first + 4):
            t_max, t_sum, s_max, s_sum, cross = joined([stat[n, b] for b in range(BATCHES)])
            whole = jnp.concatenate([t_max, t_sum, s_max, s_sum, cross, cross, cross, cross], axis=0)
            for y in range(NYL):
                stat_send[y * NZ + n] = whole[:, y * ROWS:(y + 1) * ROWS]

        def leave(i, carry):
            m = (i // 4) * NZ + first + i % 4

            @pl.when(m != me)
            def _():
                stat_copy(m, me).start()

            return carry

        lax.fori_loop(0, 8, leave, 0)
    stat_recv[me] = stat_send[me]
    for b in range(BATCHES):
        turn(b)

    each_other(lambda m: stat_copy(m, m).wait_recv())
    t_max, t_sum, s_max, s_sum, cross = joined([stat_recv[m] for m in range(OWNERS)])
    t_in, s_in = factor / t_sum, factor / s_sum
    res_recv[me] = jnp.concatenate([t_max, t_in, s_max, s_in, t_in, t_in, t_in, t_in], axis=0)
    each_other(lambda m: res_copy(m, me).start())
    div_out[...] = cross * LN2 / t_sum - (t_max * LN2 + jnp.log(t_sum)) + (s_max * LN2 + jnp.log(s_sum))
    each_other(lambda m: res_copy(m, m).wait_recv())

    def group(away):
        return (z + NZ + away) % NZ

    def query_part(away):
        n = group(away)
        res = jnp.concatenate([res_recv[n], res_recv[NZ + n]], axis=1)
        total = None
        for b in range(BATCHES):
            st = stat[n, b]
            t_in = jnp.exp2(st[0:1] - res[0:1]) * res[1:2]
            s_in = jnp.exp2(st[2:3] - res[2:3]) * res[3:4]
            grad = (sw[n, b] * s_in - tw[n, b] * t_in).astype(BF16)
            lanes = pl.ds(pl.multiple_of(n * GROUP, GROUP), GROUP)
            gt[0, b, :, lanes] = grad[:BATCH // 2]
            gt[1, b, :, lanes] = grad[BATCH // 2:]
            term = nn(spt[b], grad)
            total = term if total is None else total + term
        gq[n, 0] = total[:, :ROWS]
        gq[n, 1] = total[:, ROWS:]
        i = away + 3
        y_pair_send[i] = gq[n, 1 - yl, ZF:].astype(BF16)
        send(y_pair_send.at[i], y_pair_recv.at[i], ("y pair", i), y_mate)

    def z_part(away):
        return gq[group(away), :, :ZF]

    def y_part(away):
        i = away + 3
        received(y_pair_recv.at[i], ("y pair", i))
        return gq[group(away), yl, ZF:] + y_pair_recv[i].astype(F32)

    ZH, YH = ZF // 2, YF // 2

    def z_start():
        far = z_part(4).astype(BF16)
        z_send_r[0] = far
        send(z_send_r.at[0, :, pl.ds(0, ZH)], z_recv_r.at[0, :, pl.ds(0, ZH)], ("zr", 0), up)
        send(z_send_r.at[0, :, pl.ds(ZH, ZH)], z_recv_l.at[0, :, pl.ds(ZH, ZH)], ("zl", 0), down)

    def y_start():
        y_send_r[0] = y_part(4).astype(BF16)
        send(y_send_r.at[0, pl.ds(0, YH)], y_recv_r.at[0, pl.ds(0, YH)], ("yr", 0), up)
        send(y_send_r.at[0, pl.ds(YH, YH)], y_recv_l.at[0, pl.ds(YH, YH)], ("yl", 0), down)

    def z_step(step):
        if step == 1:
            mine = z_part(3)
            received(z_recv_r.at[0, :, pl.ds(0, ZH)], ("zr", 0))
            z_send_r[1, :, :ZH] = (mine[:, :ZH] + z_recv_r[0, :, :ZH].astype(F32)).astype(BF16)
            z_send_r[1, :, ZH:] = mine[:, ZH:].astype(BF16)
        else:
            received(z_recv_r.at[step - 1], ("zr", step - 1))
            z_send_r[step] = (z_part(4 - step) + z_recv_r[step - 1].astype(F32)).astype(BF16)
        send(z_send_r.at[step], z_recv_r.at[step], ("zr", step), up)
        if step == 1:
            mine = z_part(-3)
            received(z_recv_l.at[0, :, pl.ds(ZH, ZH)], ("zl", 0))
            z_send_l[1, :, :ZH] = mine[:, :ZH].astype(BF16)
            z_send_l[1, :, ZH:] = (mine[:, ZH:] + z_recv_l[0, :, ZH:].astype(F32)).astype(BF16)
        else:
            received(z_recv_l.at[step - 1], ("zl", step - 1))
            z_send_l[step] = (z_part(step - 4) + z_recv_l[step - 1].astype(F32)).astype(BF16)
        send(z_send_l.at[step], z_recv_l.at[step], ("zl", step), down)

    def y_step(step):
        mine = y_part(4 - step)
        if step == 1:
            received(y_recv_r.at[0, pl.ds(0, YH)], ("yr", 0))
            y_send_r[1, :YH] = (mine[:YH] + y_recv_r[0, :YH].astype(F32)).astype(BF16)
            y_send_r[1, YH:] = mine[YH:].astype(BF16)
        else:
            received(y_recv_r.at[step - 1], ("yr", step - 1))
            y_send_r[step] = (mine + y_recv_r[step - 1].astype(F32)).astype(BF16)
        send(y_send_r.at[step], y_recv_r.at[step], ("yr", step), up)
        mine = y_part(step - 4)
        if step == 1:
            received(y_recv_l.at[0, pl.ds(YH, YH)], ("yl", 0))
            y_send_l[1, :YH] = mine[:YH].astype(BF16)
            y_send_l[1, YH:] = (mine[YH:] + y_recv_l[0, YH:].astype(F32)).astype(BF16)
        else:
            received(y_recv_l.at[step - 1], ("yl", step - 1))
            y_send_l[step] = (mine + y_recv_l[step - 1].astype(F32)).astype(BF16)
        send(y_send_l.at[step], y_recv_l.at[step], ("yl", step), down)

    def passage_part(core):
        grads = gt[core].reshape(BATCHES * BATCH // 2, NZ * GROUP)
        return nn(grads, sq[...].reshape(NZ * GROUP, DS)).reshape(BATCHES, 2, OWN, DS)

    def gp_of(h, where):
        b, s = place(h, where, 0)
        return gp[b, s]

    query_part(4)
    z_start()
    query_part(3)
    query_part(-3)
    z_step(1)
    y_start()
    query_part(2)
    query_part(-2)
    query_part(1)
    query_part(-1)
    query_part(0)
    gps_send[...] = passage_part(1).astype(BF16)
    send(gps_send, gps_recv, "gp sibling", sibling)
    z_step(2)
    y_step(1)
    gp[...] = passage_part(0)
    z_step(3)
    received(gps_recv, "gp sibling")
    gp[...] = gp[...] + gps_recv[...].astype(F32)
    for h in range(NYH):
        gp1_send[h] = gp_of(h, FAR).astype(BF16)
    send(gp1_send.at[0], gp1_recv.at[0], ("gp", RIGHT, 1), right)
    send(gp1_send.at[1], gp1_recv.at[1], ("gp", LEFT, 1), left)
    y_step(2)
    received(gp1_recv.at[0], ("gp", RIGHT, 1))
    gp2_send[0, 0] = (gp_of(0, RIGHT) + gp1_recv[0].astype(F32)).astype(BF16)
    gp2_send[0, 1] = gp_of(1, RIGHT).astype(BF16)
    send(gp2_send.at[0], gp2_recv.at[0], ("gp", RIGHT, 2), right)
    received(gp1_recv.at[1], ("gp", LEFT, 1))
    gp2_send[1, 0] = gp_of(0, LEFT).astype(BF16)
    gp2_send[1, 1] = (gp_of(1, LEFT) + gp1_recv[1].astype(F32)).astype(BF16)
    send(gp2_send.at[1], gp2_recv.at[1], ("gp", LEFT, 2), left)
    y_step(3)
    received(z_recv_r.at[3], ("zr", 3))
    received(z_recv_l.at[3], ("zl", 3))
    for y in range(NYL):
        gq[z, y, :ZF] = gq[z, y, :ZF] + z_recv_r[3, y].astype(F32) + z_recv_l[3, y].astype(F32)
    z_pair_send[...] = gq[z, 1 - yl, :ZF].astype(BF16)
    send(z_pair_send, z_pair_recv, "z pair", y_mate)
    received(gp2_recv.at[0], ("gp", RIGHT, 2))
    received(gp2_recv.at[1], ("gp", LEFT, 2))

    def x_total(h):
        return gp_of(h, SELF) + gp2_recv[0, h].astype(F32) + gp2_recv[1, h].astype(F32)

    gp3_send[...] = x_total(1).astype(BF16)
    send(gp3_send, gp3_recv, "gp across", across)

    mine = y_part(0)
    received(y_recv_r.at[3], ("yr", 3))
    received(y_recv_l.at[3], ("yl", 3))
    gq_out[:, ZF:] = (mine + y_recv_r[3].astype(F32) + y_recv_l[3].astype(F32)).T
    received(z_pair_recv, "z pair")
    gq_out[:, :ZF] = (gq[z, yl, :ZF] + z_pair_recv[...].astype(F32)).T
    received(gp3_recv, "gp across")
    gp_out[...] = x_total(0) + gp3_recv[...].astype(F32)

    for copy in sent:
        copy.wait_send()
    each_other(lambda m: stat_copy(m, me).wait_send())
    each_other(lambda m: res_copy(m, me).wait_send())


def deliver(gq_in, gp_in, div_in, gq_out, gp_out, div_out, gq, gp, div, in_sem, out_sem):
    parts = ((gq_in, gq, gq_out), (gp_in, gp, gp_out), (div_in, div, div_out))
    ins = [pltpu.make_async_copy(src, mid, in_sem.at[i]) for i, (src, mid, _) in enumerate(parts)]
    outs = [pltpu.make_async_copy(mid, dst, out_sem.at[i]) for i, (_, mid, dst) in enumerate(parts)]
    for copy in ins:
        copy.start()
    for arrive, leave in zip(ins, outs):
        arrive.wait()
        leave.start()
    for copy in outs:
        copy.wait()


def local(teacher_query, student_query, teacher_passages, student_passages):
    blocks = NYL, NZ, NCORE, ROWS
    hbm = pl.BlockSpec(memory_space=pl.ANY)
    vmem = pl.BlockSpec(memory_space=pltpu.VMEM)
    outs = (
        jax.ShapeDtypeStruct((ROWS, DS), F32),
        jax.ShapeDtypeStruct((OWN, DS), F32),
        jax.ShapeDtypeStruct((1, ROWS), F32),
    )
    results = pl.pallas_call(
        kernel,
        out_shape=outs,
        in_specs=[hbm] * 4,
        out_specs=(vmem,) * 3,
        scratch_shapes=[
            pltpu.VMEM((NZ, NYL, ROWS, DT), BF16),
            pltpu.VMEM((NZ, NYL, ROWS, DS), BF16),
            pltpu.VMEM((NZ, DT, GROUP), BF16),
            pltpu.VMEM((NZ, DS, GROUP), BF16),
            pltpu.VMEM((BATCHES, BATCH // OWN, OWN, DT + DS), BF16),
            pltpu.VMEM((BATCHES, DS, BATCH), BF16),
            pltpu.VMEM((NZ, BATCHES, BATCH, GROUP), F32),
            pltpu.VMEM((NZ, BATCHES, BATCH, GROUP), F32),
            pltpu.VMEM((NCORE, BATCHES, BATCH // 2, NZ * GROUP), BF16),
            pltpu.VMEM((NZ, BATCHES, 8, GROUP), F32),
            pltpu.VMEM((NZ, NYL, DS, ROWS), F32),
            pltpu.VMEM((OWNERS, 8, ROWS), F32),
            pltpu.VMEM((OWNERS, 8, ROWS), F32),
            pltpu.VMEM((OWNERS, 8, ROWS), F32),
            pltpu.VMEM((4, NYL, ZF, ROWS), BF16),
            pltpu.VMEM((4, NYL, ZF, ROWS), BF16),
            pltpu.VMEM((4, NYL, ZF, ROWS), BF16),
            pltpu.VMEM((4, NYL, ZF, ROWS), BF16),
            pltpu.VMEM((ZF, ROWS), BF16),
            pltpu.VMEM((ZF, ROWS), BF16),
            pltpu.VMEM((NZ, YF, ROWS), BF16),
            pltpu.VMEM((NZ, YF, ROWS), BF16),
            pltpu.VMEM((4, YF, ROWS), BF16),
            pltpu.VMEM((4, YF, ROWS), BF16),
            pltpu.VMEM((4, YF, ROWS), BF16),
            pltpu.VMEM((4, YF, ROWS), BF16),
            pltpu.VMEM((BATCHES, 2, OWN, DS), F32),
            pltpu.VMEM((BATCHES, 2, OWN, DS), BF16),
            pltpu.VMEM((BATCHES, 2, OWN, DS), BF16),
            pltpu.VMEM((NYH, OWN, DS), BF16),
            pltpu.VMEM((NYH, OWN, DS), BF16),
            pltpu.VMEM((2, NYH, OWN, DS), BF16),
            pltpu.VMEM((2, NYH, OWN, DS), BF16),
            pltpu.VMEM((OWN, DS), BF16),
            pltpu.VMEM((OWN, DS), BF16),
            pltpu.SemaphoreType.DMA((6,)),
            pltpu.SemaphoreType.DMA((MESSAGES,)),
            pltpu.SemaphoreType.DMA((MESSAGES,)),
            pltpu.SemaphoreType.DMA((OWNERS,)),
            pltpu.SemaphoreType.DMA((OWNERS,)),
            pltpu.SemaphoreType.DMA((OWNERS,)),
            pltpu.SemaphoreType.DMA((OWNERS,)),
        ],
        compiler_params=pltpu.CompilerParams(
            collective_id=0, has_side_effects=True, vmem_limit_bytes=VMEM_BYTES
        ),
    )(
        teacher_query.reshape(*blocks, DT),
        student_query.reshape(*blocks, DS),
        teacher_passages,
        student_passages,
    )
    grad_query, grad_passage, divergence = pl.pallas_call(
        deliver,
        out_shape=outs,
        in_specs=[hbm] * 3,
        out_specs=(hbm,) * 3,
        scratch_shapes=[
            *(pltpu.VMEM(out.shape, out.dtype) for out in outs),
            pltpu.SemaphoreType.DMA((3,)),
            pltpu.SemaphoreType.DMA((3,)),
        ],
        compiler_params=pltpu.CompilerParams(vmem_limit_bytes=VMEM_BYTES),
    )(*results)
    return divergence.reshape(ROWS), grad_query, grad_passage


def solution(mesh):
    return jax.shard_map(
        local,
        mesh=mesh,
        in_specs=(
            P("query", None),
            P("query", None),
            P(("query", "corpus"), None),
            P(("query", "corpus"), None),
        ),
        out_specs=(
            P(("query", "corpus")),
            P(("query", "corpus"), None),
            P(("query", "corpus"), None),
        ),
        check_vma=False,
    )
```

profile of v0, /device:TPU:2, one launch (start us, length us, event | category | flops | bytes accessed | tf_op | source)
XLA Modules:
  0.0 71.4 jit_solution(2898783814833521583)
XLA Ops:
  0.6 69.1 %shard_map.67 = (f32[128,384]{1,0:T(8,128)}, f32[64,384]{1,0:T(8,128)}, f32[1,128]{1,0:T(1,128)}) custom-call(bf16[2,8,2,128,1024]{4,3,2,1,0:T(8,128)(2,1)} %bitcast.3, bf16[2,8,2,128,384]{4,3,2,1,0:T(8,128)(2,1)} %bitcast.4, bf16[64,1024]{1,0:T(8,128)(2,1)} %tp_hbm.1, bf16[64,384]{1,0:T(8,128)(2,1)} %sp_hbm.1), custom_call_target="tpu_custom_call" | custom-call | tf_op jit(solution)/shard_map/pallas_call | solution.py:464
  69.7 1.7 %shard_map.68 = (f32[128,384]{1,0:T(8,128)}, f32[64,384]{1,0:T(8,128)}, f32[1,128]{1,0:T(1,128)}) custom-call(f32[128,384]{1,0:T(8,128)} %get-tuple-element.9.gq_in, f32[64,384]{1,0:T(8,128)} %get-tuple-element.10.gp_in, f32[1,128]{1,0:T(1,128)} %get-tuple-element.11.div_in), custom_call_target="tpu_custom_call" | custom-call | tf_op jit(solution)/shard_map/pallas_call | solution.py:522
where the time goes:
time: 71.5 us; the launch traced here: 71.4 us
  Pallas kernels  70.8 us (99%)
    pallas_call x1, Pallas kernels, local(): pl.pallas_call(kernel, out_shape=outs, in_specs=[hbm] * 4, out_specs=(vme...  69.1 us
    pallas_call x1, Pallas kernels, local(): pl.pallas_call(deliver, out_shape=outs, in_specs=[hbm] * 3, out_specs=(hb...  1.69 us

commit v1 on v0

--- a/solution.py
+++ b/solution.py
@@ -74,7 +74,7 @@
         return (x_ * NYH + yh_, (yl_ * NZ + z_) * NCORE + k_)
 
     right, left = at((x + 1) % NX, yh, yl, z, k), at((x + NX - 1) % NX, yh, yl, z, k)
-    across = at(x, 1 - yh, yl, z, k)
+    across = at(x, 1 - yh, 1 - yl, z, k)
     sibling = at(x, yh, yl, z, 1 - k)
     up, down = at(x, yh, yl, (z + 1) % NZ, k), at(x, yh, yl, (z + NZ - 1) % NZ, k)
     y_mate = at(x, yh, 1 - yl, z, k)
@@ -126,6 +126,11 @@
         copy.start()
         sent.append(copy)
 
+    def flush():
+        for copy in sent:
+            copy.wait_send()
+        sent.clear()
+
     def received(ref, name):
         message(ref, ref, name, sibling).wait_recv()
 
@@ -139,22 +144,30 @@
     def to_sibling(h, where):
         send(slot(h, where, 0), slot(h, where, 1), ("sib", h, where), sibling)
 
-    def side_halves_on(h):
-        received(slot(h, LEFT, 0, 0), ("p", h, LEFT, 0))
-        send(slot(h, LEFT, 0, 0), slot(h, FAR, 0, 0), ("p", h, FAR, 0), right)
-        received(slot(h, RIGHT, 0, 1), ("p", h, RIGHT, 1))
-        send(slot(h, RIGHT, 0, 1), slot(h, FAR, 0, 1), ("p", h, FAR, 1), left)
-
-    def sides_to_sibling(h):
-        received(slot(h, LEFT, 0, 1), ("p", h, LEFT, 1))
+    def side_halves_on():
+        received(slot(0, LEFT, 0, 0), ("p", 0, LEFT, 0))
+        send(slot(0, LEFT, 0, 0), slot(0, FAR, 0, 0), ("p", 0, FAR, 0), right)
+        received(slot(0, RIGHT, 0, 1), ("p", 0, RIGHT, 1))
+        send(slot(0, RIGHT, 0, 1), slot(0, FAR, 0, 1), ("p", 0, FAR, 1), left)
+
+    def sides_to_sibling(h, rest):
+        for half in rest:
+            received(slot(h, LEFT, 0, half), ("p", h, LEFT, half))
         to_sibling(h, LEFT)
-        received(slot(h, RIGHT, 0, 0), ("p", h, RIGHT, 0))
+        for half in rest:
+            received(slot(h, RIGHT, 0, 1 - half), ("p", h, RIGHT, 1 - half))
         to_sibling(h, RIGHT)
 
-    def far_to_sibling(h):
-        received(slot(h, FAR, 0, 0), ("p", h, FAR, 0))
-        received(slot(h, FAR, 0, 1), ("p", h, FAR, 1))
-        to_sibling(h, FAR)
+    def far_across():
+        for half in (0, 1):
+            received(slot(0, FAR, 0, half), ("p", 0, FAR, half))
+            send(slot(0, FAR, 0, half), slot(1, FAR, 0, half), ("p", 1, FAR, half), across)
+        to_sibling(0, FAR)
+
+    def far_from_across():
+        for half in (0, 1):
+            received(slot(1, FAR, 0, half), ("p", 1, FAR, half))
+        to_sibling(1, FAR)
 
     def from_sibling(h, where):
         received(slot(h, where, 1), ("sib", h, where))
@@ -184,7 +197,11 @@
         lax.fori_loop(first, first + count, tile, 0, unroll=2)
 
     def turn(b):
-        spt[b] = pbuf[b].reshape(BATCH, DT + DS)[:, DT:].T
+        turned = pbuf[b].reshape(BATCH, DT + DS)[:, DT:].T
+        part = BATCH // NCORE
+        for core in range(NCORE):
+            start = (core * BATCHES + b) * part
+            spt[:, start:start + part] = turned[:, core * part:(core + 1) * part]
 
     def turn_queries(first, count):
         def body(n, carry):
@@ -197,29 +214,27 @@
     for load in loads[2:]:
         load.wait()
     turn_queries(0, 4)
-    side_halves_on(0)
+    side_halves_on()
     turn_queries(4, 4)
-    sides_to_sibling(0)
     for half in (0, 1):
         received(slot(1, SELF, 0, half), ("p", 1, SELF, half))
     to_sides(1)
     to_sibling(1, SELF)
+    sides_to_sibling(0, (1,))
     from_sibling(0, LEFT)
     from_sibling(0, RIGHT)
-    scores(1, 0, 4)
-    far_to_sibling(0)
-    scores(1, 4, 4)
-    side_halves_on(1)
+    scores(1, 0, 2)
+    far_across()
+    scores(1, 2, 6)
     from_sibling(0, SELF)
     from_sibling(1, SELF)
     scores(0, 0, 4)
-    sides_to_sibling(1)
+    sides_to_sibling(1, (0, 1))
     scores(0, 4, 4)
+    far_from_across()
     from_sibling(1, LEFT)
     from_sibling(1, RIGHT)
-    scores(2, 0, 4)
-    far_to_sibling(1)
-    scores(2, 4, 4)
+    scores(2, 0, 8)
     from_sibling(0, FAR)
     from_sibling(1, FAR)
 
@@ -275,32 +290,36 @@
     stat_recv[me] = stat_send[me]
     for b in range(BATCHES):
         turn(b)
-
+    flush()
     each_other(lambda m: stat_copy(m, m).wait_recv())
     t_max, t_sum, s_max, s_sum, cross = joined([stat_recv[m] for m in range(OWNERS)])
     t_in, s_in = factor / t_sum, factor / s_sum
     res_recv[me] = jnp.concatenate([t_max, t_in, s_max, s_in, t_in, t_in, t_in, t_in], axis=0)
     each_other(lambda m: res_copy(m, me).start())
     div_out[...] = cross * LN2 / t_sum - (t_max * LN2 + jnp.log(t_sum)) + (s_max * LN2 + jnp.log(s_sum))
+    each_other(lambda m: stat_copy(m, me).wait_send())
     each_other(lambda m: res_copy(m, m).wait_recv())
 
     def group(away):
         return (z + NZ + away) % NZ
 
-    def query_part(away):
+    def lanes(away):
+        return pl.ds(pl.multiple_of(group(away) * GROUP, GROUP), GROUP)
+
+    def form(away):
         n = group(away)
         res = jnp.concatenate([res_recv[n], res_recv[NZ + n]], axis=1)
-        total = None
         for b in range(BATCHES):
             st = stat[n, b]
             t_in = jnp.exp2(st[0:1] - res[0:1]) * res[1:2]
             s_in = jnp.exp2(st[2:3] - res[2:3]) * res[3:4]
             grad = (sw[n, b] * s_in - tw[n, b] * t_in).astype(BF16)
-            lanes = pl.ds(pl.multiple_of(n * GROUP, GROUP), GROUP)
-            gt[0, b, :, lanes] = grad[:BATCH // 2]
-            gt[1, b, :, lanes] = grad[BATCH // 2:]
-            term = nn(spt[b], grad)
-            total = term if total is None else total + term
+            gt[0, b, :, lanes(away)] = grad[:BATCH // 2]
+            gt[1, b, :, lanes(away)] = grad[BATCH // 2:]
+
+    def query_part(away):
+        n = group(away)
+        total = nn(spt[...], gt[:, :, :, lanes(away)].reshape(NCORE * BATCHES * BATCH // 2, GROUP))
         gq[n, 0] = total[:, :ROWS]
         gq[n, 1] = total[:, ROWS:]
         i = away + 3
@@ -376,53 +395,74 @@
         b, s = place(h, where, 0)
         return gp[b, s]
 
+    def gp_first():
+        received(gps_recv, "gp sibling")
+        gp[...] = gp[...] + gps_recv[...].astype(F32)
+        for h in range(NYH):
+            gp1_send[h] = gp_of(h, FAR).astype(BF16)
+        send(gp1_send.at[0], gp1_recv.at[0], ("gp", RIGHT, 1), right)
+        send(gp1_send.at[1], gp1_recv.at[1], ("gp", LEFT, 1), left)
+
+    def gp_second():
+        received(gp1_recv.at[0], ("gp", RIGHT, 1))
+        gp2_send[0, 0] = (gp_of(0, RIGHT) + gp1_recv[0].astype(F32)).astype(BF16)
+        gp2_send[0, 1] = gp_of(1, RIGHT).astype(BF16)
+        send(gp2_send.at[0], gp2_recv.at[0], ("gp", RIGHT, 2), right)
+        received(gp1_recv.at[1], ("gp", LEFT, 1))
+        gp2_send[1, 0] = gp_of(0, LEFT).astype(BF16)
+        gp2_send[1, 1] = (gp_of(1, LEFT) + gp1_recv[1].astype(F32)).astype(BF16)
+        send(gp2_send.at[1], gp2_recv.at[1], ("gp", LEFT, 2), left)
+
+    def gp_third():
+        received(gp2_recv.at[0], ("gp", RIGHT, 2))
+        received(gp2_recv.at[1], ("gp", LEFT, 2))
+        gp3_send[...] = x_total(1).astype(BF16)
+        send(gp3_send, gp3_recv, "gp across", across)
+
+    def x_total(h):
+        return gp_of(h, SELF) + gp2_recv[0, h].astype(F32) + gp2_recv[1, h].astype(F32)
+
+    def z_last():
+        received(z_recv_r.at[3], ("zr", 3))
+        received(z_recv_l.at[3], ("zl", 3))
+        for y in range(NYL):
+            gq[z, y, :ZF] = gq[z, y, :ZF] + z_recv_r[3, y].astype(F32) + z_recv_l[3, y].astype(F32)
+        z_pair_send[...] = gq[z, 1 - yl, :ZF].astype(BF16)
+        send(z_pair_send, z_pair_recv, "z pair", y_mate)
+
+    form(4)
     query_part(4)
     z_start()
+    form(3)
     query_part(3)
+    form(-3)
     query_part(-3)
+    form(2)
+    form(-2)
     z_step(1)
     y_start()
+    form(1)
+    form(-1)
+    form(0)
+    gps_send[...] = passage_part(1).astype(BF16)
+    send(gps_send, gps_recv, "gp sibling", sibling)
     query_part(2)
     query_part(-2)
-    query_part(1)
-    query_part(-1)
-    query_part(0)
-    gps_send[...] = passage_part(1).astype(BF16)
-    send(gps_send, gps_recv, "gp sibling", sibling)
     z_step(2)
     y_step(1)
     gp[...] = passage_part(0)
+    gp_first()
+    query_part(1)
+    query_part(-1)
     z_step(3)
-    received(gps_recv, "gp sibling")
-    gp[...] = gp[...] + gps_recv[...].astype(F32)
-    for h in range(NYH):
-        gp1_send[h] = gp_of(h, FAR).astype(BF16)
-    send(gp1_send.at[0], gp1_recv.at[0], ("gp", RIGHT, 1), right)
-    send(gp1_send.at[1], gp1_recv.at[1], ("gp", LEFT, 1), left)
     y_step(2)
-    received(gp1_recv.at[0], ("gp", RIGHT, 1))
-    gp2_send[0, 0] = (gp_of(0, RIGHT) + gp1_recv[0].astype(F32)).astype(BF16)
-    gp2_send[0, 1] = gp_of(1, RIGHT).astype(BF16)
-    send(gp2_send.at[0], gp2_recv.at[0], ("gp", RIGHT, 2), right)
-    received(gp1_recv.at[1], ("gp", LEFT, 1))
-    gp2_send[1, 0] = gp_of(0, LEFT).astype(BF16)
-    gp2_send[1, 1] = (gp_of(1, LEFT) + gp1_recv[1].astype(F32)).astype(BF16)
-    send(gp2_send.at[1], gp2_recv.at[1], ("gp", LEFT, 2), left)
+    gp_second()
+    query_part(0)
+    each_other(lambda m: res_copy(m, me).wait_send())
+    z_last()
     y_step(3)
-    received(z_recv_r.at[3], ("zr", 3))
-    received(z_recv_l.at[3], ("zl", 3))
-    for y in range(NYL):
-        gq[z, y, :ZF] = gq[z, y, :ZF] + z_recv_r[3, y].astype(F32) + z_recv_l[3, y].astype(F32)
-    z_pair_send[...] = gq[z, 1 - yl, :ZF].astype(BF16)
-    send(z_pair_send, z_pair_recv, "z pair", y_mate)
-    received(gp2_recv.at[0], ("gp", RIGHT, 2))
-    received(gp2_recv.at[1], ("gp", LEFT, 2))
-
-    def x_total(h):
-        return gp_of(h, SELF) + gp2_recv[0, h].astype(F32) + gp2_recv[1, h].astype(F32)
-
-    gp3_send[...] = x_total(1).astype(BF16)
-    send(gp3_send, gp3_recv, "gp across", across)
+    gp_third()
+    flush()
 
     mine = y_part(0)
     received(y_recv_r.at[3], ("yr", 3))
@@ -432,11 +472,6 @@
     gq_out[:, :ZF] = (gq[z, yl, :ZF] + z_pair_recv[...].astype(F32)).T
     received(gp3_recv, "gp across")
     gp_out[...] = x_total(0) + gp3_recv[...].astype(F32)
-
-    for copy in sent:
-        copy.wait_send()
-    each_other(lambda m: stat_copy(m, me).wait_send())
-    each_other(lambda m: res_copy(m, me).wait_send())
 
 
 def deliver(gq_in, gp_in, div_in, gq_out, gp_out, div_out, gq, gp, div, in_sem, out_sem):
@@ -472,7 +507,7 @@
             pltpu.VMEM((NZ, DT, GROUP), BF16),
             pltpu.VMEM((NZ, DS, GROUP), BF16),
             pltpu.VMEM((BATCHES, BATCH // OWN, OWN, DT + DS), BF16),
-            pltpu.VMEM((BATCHES, DS, BATCH), BF16),
+            pltpu.VMEM((DS, BATCHES * BATCH), BF16),
             pltpu.VMEM((NZ, BATCHES, BATCH, GROUP), F32),
             pltpu.VMEM((NZ, BATCHES, BATCH, GROUP), F32),
             pltpu.VMEM((NCORE, BATCHES, BATCH // 2, NZ * GROUP), BF16),

time: 71.5 us -> 68.9 us (0.964)
  Pallas kernels: 70.8 us -> 67.6 us
    pallas_call x1, Pallas kernels: 69.1 us -> 65.9 us  [local(): pl.pallas_call(kernel, out_shape=outs, in_specs=[hbm] * 4, out_specs=(vme...]
where the time goes in v1:
time: 68.9 us; the launch traced here: 68.2 us
  Pallas kernels  67.6 us (98%)
    pallas_call x1, Pallas kernels, local(): pl.pallas_call(kernel, out_shape=outs, in_specs=[hbm] * 4, out_specs=(vme...  65.9 us
    pallas_call x1, Pallas kernels, local(): pl.pallas_call(deliver, out_shape=outs, in_specs=[hbm] * 3, out_specs=(hb...  1.69 us

profile of v1, /device:TPU:2, one launch (start us, length us, event | category | flops | bytes accessed | tf_op | source)
XLA Modules:
  0.0 68.2 jit_solution(3048158902840574090)
XLA Ops:
  0.6 65.9 %shard_map.67 = (f32[128,384]{1,0:T(8,128)}, f32[64,384]{1,0:T(8,128)}, f32[1,128]{1,0:T(1,128)}) custom-call(bf16[2,8,2,128,1024]{4,3,2,1,0:T(8,128)(2,1)} %bitcast.3, bf16[2,8,2,128,384]{4,3,2,1,0:T(8,128)(2,1)} %bitcast.4, bf16[64,1024]{1,0:T(8,128)(2,1)} %tp_hbm.1, bf16[64,384]{1,0:T(8,128)(2,1)} %sp_hbm.1), custom_call_target="tpu_custom_call" | custom-call | tf_op jit(solution)/shard_map/pallas_call | solution.py:499
  66.6 1.7 %shard_map.68 = (f32[128,384]{1,0:T(8,128)}, f32[64,384]{1,0:T(8,128)}, f32[1,128]{1,0:T(1,128)}) custom-call(f32[128,384]{1,0:T(8,128)} %get-tuple-element.9.gq_in, f32[64,384]{1,0:T(8,128)} %get-tuple-element.10.gp_in, f32[1,128]{1,0:T(1,128)} %get-tuple-element.11.div_in), custom_call_target="tpu_custom_call" | custom-call | tf_op jit(solution)/shard_map/pallas_call | solution.py:557

commit v2 on v1

--- a/solution.py
+++ b/solution.py
@@ -29,10 +29,10 @@
 
 def place(h, where, core):
     if where == SELF:
-        return 0, core * 2 + h
+        return 1, core * 2 + h
     if where == FAR:
         return 3, core * 2 + h
-    return 1 + h, core * 2 + (where - LEFT)
+    return 2 * h, core * 2 + (where - LEFT)
 
 
 def nn(a, b):
@@ -54,12 +54,12 @@
 def kernel(
     tq_hbm, sq_hbm, tp_hbm, sp_hbm,
     gq_out, gp_out, div_out,
-    tq, sq, tqt, sqt, pbuf, spt, tw, sw, gt, stat, gq,
+    tq, sq, tqt, sqt, pbuf, spt, tw, sw, raw_a, raw_b, gt, stat, gq,
     stat_send, stat_recv, res_recv,
     z_send_r, z_recv_r, z_send_l, z_recv_l, z_pair_send, z_pair_recv,
     y_pair_send, y_pair_recv, y_send_r, y_recv_r, y_send_l, y_recv_l,
     gp, gps_send, gps_recv, gp1_send, gp1_recv, gp2_send, gp2_recv, gp3_send, gp3_recv,
-    load_sem, send_sem, recv_sem, st_send_sem, st_recv_sem, rs_send_sem, rs_recv_sem,
+    load_sem, send_sem, recv_sem, yp_send_sem, yp_recv_sem, st_send_sem, st_recv_sem, rs_send_sem, rs_recv_sem,
 ):
     t_scale = DT ** (-0.5) * LOG2E
     s_scale = DS ** (-0.5) * LOG2E
@@ -89,8 +89,8 @@
         return pbuf.at[b, s, pl.ds(half * HALF, HALF)]
 
     loads = [
-        pltpu.make_async_copy(tp_hbm, pbuf.at[0, 0, :, pl.ds(0, DT)], load_sem.at[0]),
-        pltpu.make_async_copy(sp_hbm, pbuf.at[0, 0, :, pl.ds(DT, DS)], load_sem.at[1]),
+        pltpu.make_async_copy(tp_hbm, pbuf.at[1, 0, :, pl.ds(0, DT)], load_sem.at[0]),
+        pltpu.make_async_copy(sp_hbm, pbuf.at[1, 0, :, pl.ds(DT, DS)], load_sem.at[1]),
     ]
     for y in range(NYL):
         loads.append(pltpu.make_async_copy(tq_hbm.at[y, :, k], tq.at[:, y], load_sem.at[2 + y]))
@@ -114,41 +114,41 @@
     number = Messages()
     sent = []
 
-    def message(src, dst, name, device):
+    def message(refs, name, device):
         i = number(name)
+        src, dst = refs()
         return pltpu.make_async_remote_copy(
             src_ref=src, dst_ref=dst, send_sem=send_sem.at[i], recv_sem=recv_sem.at[i],
             device_id=device, device_id_type=MESH,
         )
 
-    def send(src, dst, name, device):
-        copy = message(src, dst, name, device)
-        copy.start()
-        sent.append(copy)
+    def send(refs, name, device):
+        message(refs, name, device).start()
+        sent.append((refs, name, device))
 
     def flush():
-        for copy in sent:
-            copy.wait_send()
+        for args in sent:
+            message(*args).wait_send()
         sent.clear()
 
     def received(ref, name):
-        message(ref, ref, name, sibling).wait_recv()
+        message(lambda: (ref, ref), name, sibling).wait_recv()
 
     def to_sides(h):
         for first in (0, 1):
             half = first
-            send(slot(h, SELF, 0, half), slot(h, LEFT, 0, half), ("p", h, LEFT, half), right)
+            send(lambda half=half, h=h: (slot(h, SELF, 0, half), slot(h, LEFT, 0, half)), ("p", h, LEFT, half), right)
             half = 1 - first
-            send(slot(h, SELF, 0, half), slot(h, RIGHT, 0, half), ("p", h, RIGHT, half), left)
+            send(lambda half=half, h=h: (slot(h, SELF, 0, half), slot(h, RIGHT, 0, half)), ("p", h, RIGHT, half), left)
 
     def to_sibling(h, where):
-        send(slot(h, where, 0), slot(h, where, 1), ("sib", h, where), sibling)
+        send(lambda h=h, where=where: (slot(h, where, 0), slot(h, where, 1)), ("sib", h, where), sibling)
 
     def side_halves_on():
         received(slot(0, LEFT, 0, 0), ("p", 0, LEFT, 0))
-        send(slot(0, LEFT, 0, 0), slot(0, FAR, 0, 0), ("p", 0, FAR, 0), right)
+        send(lambda: (slot(0, LEFT, 0, 0), slot(0, FAR, 0, 0)), ("p", 0, FAR, 0), right)
         received(slot(0, RIGHT, 0, 1), ("p", 0, RIGHT, 1))
-        send(slot(0, RIGHT, 0, 1), slot(0, FAR, 0, 1), ("p", 0, FAR, 1), left)
+        send(lambda: (slot(0, RIGHT, 0, 1), slot(0, FAR, 0, 1)), ("p", 0, FAR, 1), left)
 
     def sides_to_sibling(h, rest):
         for half in rest:
@@ -161,7 +161,7 @@
     def far_across():
         for half in (0, 1):
             received(slot(0, FAR, 0, half), ("p", 0, FAR, half))
-            send(slot(0, FAR, 0, half), slot(1, FAR, 0, half), ("p", 1, FAR, half), across)
+            send(lambda half=half: (slot(0, FAR, 0, half), slot(1, FAR, 0, half)), ("p", 1, FAR, half), across)
         to_sibling(0, FAR)
 
     def far_from_across():
@@ -173,28 +173,30 @@
         received(slot(h, where, 1), ("sib", h, where))
 
     for half in (0, 1):
-        send(slot(0, SELF, 0, half), slot(1, SELF, 0, half), ("p", 1, SELF, half), across)
+        send(lambda half=half: (slot(0, SELF, 0, half), slot(1, SELF, 0, half)), ("p", 1, SELF, half), across)
     to_sides(0)
     to_sibling(0, SELF)
 
-    def scores(b, first, count):
-        def tile(n, carry):
-            passages = pbuf[b].reshape(BATCH, DT + DS)
-            t = nn(passages[:, :DT], tqt[n]) * t_scale
-            s = nn(passages[:, DT:], sqt[n]) * s_scale
-            t_max = jnp.max(t, axis=0, keepdims=True)
-            s_max = jnp.max(s, axis=0, keepdims=True)
-            t_weight = jnp.exp2(t - t_max)
-            s_weight = jnp.exp2(s - s_max)
-            tw[n, b] = t_weight
-            sw[n, b] = s_weight
-            t_sum = jnp.sum(t_weight, axis=0, keepdims=True)
-            s_sum = jnp.sum(s_weight, axis=0, keepdims=True)
-            cross = jnp.sum(t_weight * (t - s), axis=0, keepdims=True)
-            stat[n, b] = jnp.concatenate([t_max, t_sum, s_max, s_sum, cross, cross, cross, cross], axis=0)
-            return carry
-
-        lax.fori_loop(first, first + count, tile, 0, unroll=2)
+    def product(i, raw):
+        b, n = i // NZ, i % NZ
+        passages = pbuf[b].reshape(BATCH, DT + DS)
+        raw[0] = nn(passages[:, :DT], tqt[n])
+        raw[1] = nn(passages[:, DT:], sqt[n])
+
+    def weights(i, raw):
+        b, n = i // NZ, i % NZ
+        t = raw[0] * t_scale
+        s = raw[1] * s_scale
+        t_max = jnp.max(t, axis=0, keepdims=True)
+        s_max = jnp.max(s, axis=0, keepdims=True)
+        t_weight = jnp.exp2(t - t_max)
+        s_weight = jnp.exp2(s - s_max)
+        tw[n, b] = t_weight
+        sw[n, b] = s_weight
+        t_sum = jnp.sum(t_weight, axis=0, keepdims=True)
+        s_sum = jnp.sum(s_weight, axis=0, keepdims=True)
+        cross = jnp.sum(t_weight * (t - s), axis=0, keepdims=True)
+        stat[n, b] = jnp.concatenate([t_max, t_sum, s_max, s_sum, cross, cross, cross, cross], axis=0)
 
     def turn(b):
         turned = pbuf[b].reshape(BATCH, DT + DS)[:, DT:].T
@@ -221,23 +223,6 @@
     to_sides(1)
     to_sibling(1, SELF)
     sides_to_sibling(0, (1,))
-    from_sibling(0, LEFT)
-    from_sibling(0, RIGHT)
-    scores(1, 0, 2)
-    far_across()
-    scores(1, 2, 6)
-    from_sibling(0, SELF)
-    from_sibling(1, SELF)
-    scores(0, 0, 4)
-    sides_to_sibling(1, (0, 1))
-    scores(0, 4, 4)
-    far_from_across()
-    from_sibling(1, LEFT)
-    from_sibling(1, RIGHT)
-    scores(2, 0, 8)
-    from_sibling(0, FAR)
-    from_sibling(1, FAR)
-
     def joined(parts):
         t_max = functools.reduce(jnp.maximum, [p[0:1] for p in parts])
         s_max = functools.reduce(jnp.maximum, [p[2:3] for p in parts])
@@ -269,15 +254,14 @@
 
         lax.fori_loop(1, OWNERS, body, 0)
 
-    for first in (0, 4):
-        scores(3, first, 4)
+    def leave(first):
         for n in range(first, first + 4):
             t_max, t_sum, s_max, s_sum, cross = joined([stat[n, b] for b in range(BATCHES)])
             whole = jnp.concatenate([t_max, t_sum, s_max, s_sum, cross, cross, cross, cross], axis=0)
             for y in range(NYL):
                 stat_send[y * NZ + n] = whole[:, y * ROWS:(y + 1) * ROWS]
 
-        def leave(i, carry):
+        def body(i, carry):
             m = (i // 4) * NZ + first + i % 4
 
             @pl.when(m != me)
@@ -286,7 +270,52 @@
 
             return carry
 
-        lax.fori_loop(0, 8, leave, 0)
+        lax.fori_loop(0, 8, body, 0)
+
+    from_sibling(0, LEFT)
+    from_sibling(0, RIGHT)
+    product(0, raw_a)
+
+    def score_step(j, carry):
+        @pl.when(j == 1)
+        def _():
+            far_across()
+
+        @pl.when(j == 3)
+        def _():
+            from_sibling(0, SELF)
+            from_sibling(1, SELF)
+
+        @pl.when(j == 6)
+        def _():
+            sides_to_sibling(1, (0, 1))
+
+        @pl.when(j == 7)
+        def _():
+            from_sibling(1, LEFT)
+            from_sibling(1, RIGHT)
+
+        @pl.when(j == 9)
+        def _():
+            far_from_across()
+
+        @pl.when(j == 11)
+        def _():
+            from_sibling(0, FAR)
+            from_sibling(1, FAR)
+
+        @pl.when(j == 14)
+        def _():
+            leave(0)
+
+        product(2 * j + 1, raw_b)
+        weights(2 * j, raw_a)
+        product(jnp.minimum(2 * j + 2, BATCHES * NZ - 1), raw_a)
+        weights(2 * j + 1, raw_b)
+        return carry
+
+    lax.fori_loop(0, BATCHES * NZ // 2, score_step, 0)
+    leave(4)
     stat_recv[me] = stat_send[me]
     for b in range(BATCHES):
         turn(b)
@@ -303,35 +332,44 @@
     def group(away):
         return (z + NZ + away) % NZ
 
-    def lanes(away):
-        return pl.ds(pl.multiple_of(group(away) * GROUP, GROUP), GROUP)
-
-    def form(away):
-        n = group(away)
+    def sequence(i):
+        size = 4 - (i + 1) // 2
+        return group(size * (2 * (i % 2) - 1))
+
+    def lanes(n):
+        return pl.ds(pl.multiple_of(n * GROUP, GROUP), GROUP)
+
+    def form(i):
+        n = sequence(i)
         res = jnp.concatenate([res_recv[n], res_recv[NZ + n]], axis=1)
         for b in range(BATCHES):
             st = stat[n, b]
             t_in = jnp.exp2(st[0:1] - res[0:1]) * res[1:2]
             s_in = jnp.exp2(st[2:3] - res[2:3]) * res[3:4]
             grad = (sw[n, b] * s_in - tw[n, b] * t_in).astype(BF16)
-            gt[0, b, :, lanes(away)] = grad[:BATCH // 2]
-            gt[1, b, :, lanes(away)] = grad[BATCH // 2:]
-
-    def query_part(away):
-        n = group(away)
-        total = nn(spt[...], gt[:, :, :, lanes(away)].reshape(NCORE * BATCHES * BATCH // 2, GROUP))
+            gt[0, b, :, lanes(n)] = grad[:BATCH // 2]
+            gt[1, b, :, lanes(n)] = grad[BATCH // 2:]
+
+    def pair_copy(i):
+        return pltpu.make_async_remote_copy(
+            src_ref=y_pair_send.at[i], dst_ref=y_pair_recv.at[i],
+            send_sem=yp_send_sem.at[i], recv_sem=yp_recv_sem.at[i],
+            device_id=y_mate, device_id_type=MESH,
+        )
+
+    def query_part(i):
+        n = sequence(i)
+        total = nn(spt[...], gt[:, :, :, lanes(n)].reshape(NCORE * BATCHES * BATCH // 2, GROUP))
         gq[n, 0] = total[:, :ROWS]
         gq[n, 1] = total[:, ROWS:]
-        i = away + 3
         y_pair_send[i] = gq[n, 1 - yl, ZF:].astype(BF16)
-        send(y_pair_send.at[i], y_pair_recv.at[i], ("y pair", i), y_mate)
 
     def z_part(away):
         return gq[group(away), :, :ZF]
 
     def y_part(away):
-        i = away + 3
-        received(y_pair_recv.at[i], ("y pair", i))
+        i = (4, 3, -3, 2, -2, 1, -1, 0).index(away)
+        pair_copy(i).wait_recv()
         return gq[group(away), yl, ZF:] + y_pair_recv[i].astype(F32)
 
     ZH, YH = ZF // 2, YF // 2
@@ -339,13 +377,13 @@
     def z_start():
         far = z_part(4).astype(BF16)
         z_send_r[0] = far
-        send(z_send_r.at[0, :, pl.ds(0, ZH)], z_recv_r.at[0, :, pl.ds(0, ZH)], ("zr", 0), up)
-        send(z_send_r.at[0, :, pl.ds(ZH, ZH)], z_recv_l.at[0, :, pl.ds(ZH, ZH)], ("zl", 0), down)
+        send(lambda: (z_send_r.at[0, :, pl.ds(0, ZH)], z_recv_r.at[0, :, pl.ds(0, ZH)]), ("zr", 0), up)
+        send(lambda: (z_send_r.at[0, :, pl.ds(ZH, ZH)], z_recv_l.at[0, :, pl.ds(ZH, ZH)]), ("zl", 0), down)
 
     def y_start():
         y_send_r[0] = y_part(4).astype(BF16)
-        send(y_send_r.at[0, pl.ds(0, YH)], y_recv_r.at[0, pl.ds(0, YH)], ("yr", 0), up)
-        send(y_send_r.at[0, pl.ds(YH, YH)], y_recv_l.at[0, pl.ds(YH, YH)], ("yl", 0), down)
+        send(lambda: (y_send_r.at[0, pl.ds(0, YH)], y_recv_r.at[0, pl.ds(0, YH)]), ("yr", 0), up)
+        send(lambda: (y_send_r.at[0, pl.ds(YH, YH)], y_recv_l.at[0, pl.ds(YH, YH)]), ("yl", 0), down)
 
     def z_step(step):
         if step == 1:
@@ -356,7 +394,7 @@
         else:
             received(z_recv_r.at[step - 1], ("zr", step - 1))
             z_send_r[step] = (z_part(4 - step) + z_recv_r[step - 1].astype(F32)).astype(BF16)
-        send(z_send_r.at[step], z_recv_r.at[step], ("zr", step), up)
+        send(lambda step=step: (z_send_r.at[step], z_recv_r.at[step]), ("zr", step), up)
         if step == 1:
             mine = z_part(-3)
             received(z_recv_l.at[0, :, pl.ds(ZH, ZH)], ("zl", 0))
@@ -365,7 +403,7 @@
         else:
             received(z_recv_l.at[step - 1], ("zl", step - 1))
             z_send_l[step] = (z_part(step - 4) + z_recv_l[step - 1].astype(F32)).astype(BF16)
-        send(z_send_l.at[step], z_recv_l.at[step], ("zl", step), down)
+        send(lambda step=step: (z_send_l.at[step], z_recv_l.at[step]), ("zl", step), down)
 
     def y_step(step):
         mine = y_part(4 - step)
@@ -376,7 +414,7 @@
         else:
             received(y_recv_r.at[step - 1], ("yr", step - 1))
             y_send_r[step] = (mine + y_recv_r[step - 1].astype(F32)).astype(BF16)
-        send(y_send_r.at[step], y_recv_r.at[step], ("yr", step), up)
+        send(lambda step=step: (y_send_r.at[step], y_recv_r.at[step]), ("yr", step), up)
         mine = y_part(step - 4)
         if step == 1:
             received(y_recv_l.at[0, pl.ds(YH, YH)], ("yl", 0))
@@ -385,11 +423,18 @@
         else:
             received(y_recv_l.at[step - 1], ("yl", step - 1))
             y_send_l[step] = (mine + y_recv_l[step - 1].astype(F32)).astype(BF16)
-        send(y_send_l.at[step], y_recv_l.at[step], ("yl", step), down)
-
-    def passage_part(core):
-        grads = gt[core].reshape(BATCHES * BATCH // 2, NZ * GROUP)
-        return nn(grads, sq[...].reshape(NZ * GROUP, DS)).reshape(BATCHES, 2, OWN, DS)
+        send(lambda step=step: (y_send_l.at[step], y_recv_l.at[step]), ("yl", step), down)
+
+    def passage_part(core, to):
+        to[...] = jnp.zeros_like(to)
+
+        def body(n, carry):
+            grads = gt[core, :, :, lanes(n)].reshape(BATCHES * BATCH // 2, GROUP)
+            term = nn(grads, sq[n].reshape(GROUP, DS))
+            to[...] = to[...] + term.reshape(BATCHES, 2, OWN, DS)
+            return carry
+
+        lax.fori_loop(0, NZ, body, 0)
 
     def gp_of(h, where):
         b, s = place(h, where, 0)
@@ -400,24 +445,24 @@
         gp[...] = gp[...] + gps_recv[...].astype(F32)
         for h in range(NYH):
             gp1_send[h] = gp_of(h, FAR).astype(BF16)
-        send(gp1_send.at[0], gp1_recv.at[0], ("gp", RIGHT, 1), right)
-        send(gp1_send.at[1], gp1_recv.at[1], ("gp", LEFT, 1), left)
+        send(lambda: (gp1_send.at[0], gp1_recv.at[0]), ("gp", RIGHT, 1), right)
+        send(lambda: (gp1_send.at[1], gp1_recv.at[1]), ("gp", LEFT, 1), left)
 
     def gp_second():
         received(gp1_recv.at[0], ("gp", RIGHT, 1))
         gp2_send[0, 0] = (gp_of(0, RIGHT) + gp1_recv[0].astype(F32)).astype(BF16)
         gp2_send[0, 1] = gp_of(1, RIGHT).astype(BF16)
-        send(gp2_send.at[0], gp2_recv.at[0], ("gp", RIGHT, 2), right)
+        send(lambda: (gp2_send.at[0], gp2_recv.at[0]), ("gp", RIGHT, 2), right)
         received(gp1_recv.at[1], ("gp", LEFT, 1))
         gp2_send[1, 0] = gp_of(0, LEFT).astype(BF16)
         gp2_send[1, 1] = (gp_of(1, LEFT) + gp1_recv[1].astype(F32)).astype(BF16)
-        send(gp2_send.at[1], gp2_recv.at[1], ("gp", LEFT, 2), left)
+        send(lambda: (gp2_send.at[1], gp2_recv.at[1]), ("gp", LEFT, 2), left)
 
     def gp_third():
         received(gp2_recv.at[0], ("gp", RIGHT, 2))
         received(gp2_recv.at[1], ("gp", LEFT, 2))
         gp3_send[...] = x_total(1).astype(BF16)
-        send(gp3_send, gp3_recv, "gp across", across)
+        send(lambda: (gp3_send, gp3_recv), "gp across", across)
 
     def x_total(h):
         return gp_of(h, SELF) + gp2_recv[0, h].astype(F32) + gp2_recv[1, h].astype(F32)
@@ -428,37 +473,41 @@
         for y in range(NYL):
             gq[z, y, :ZF] = gq[z, y, :ZF] + z_recv_r[3, y].astype(F32) + z_recv_l[3, y].astype(F32)
         z_pair_send[...] = gq[z, 1 - yl, :ZF].astype(BF16)
-        send(z_pair_send, z_pair_recv, "z pair", y_mate)
-
-    form(4)
-    query_part(4)
-    z_start()
-    form(3)
-    query_part(3)
-    form(-3)
-    query_part(-3)
-    form(2)
-    form(-2)
-    z_step(1)
-    y_start()
-    form(1)
-    form(-1)
+        send(lambda: (z_pair_send, z_pair_recv), "z pair", y_mate)
+
     form(0)
-    gps_send[...] = passage_part(1).astype(BF16)
-    send(gps_send, gps_recv, "gp sibling", sibling)
-    query_part(2)
-    query_part(-2)
+
+    def gradient_step(i, carry):
+        query_part(i)
+        form(i + 1)
+        pair_copy(i).start()
+
+        @pl.when(i == 0)
+        def _():
+            z_start()
+
+        @pl.when(i == 5)
+        def _():
+            z_step(1)
+            y_start()
+
+        return carry
+
+    lax.fori_loop(0, NZ - 1, gradient_step, 0)
+    query_part(NZ - 1)
+    pair_copy(NZ - 1).start()
+    passage_part(1, gp)
+    gps_send[...] = gp[...].astype(BF16)
+    send(lambda: (gps_send, gps_recv), "gp sibling", sibling)
     z_step(2)
     y_step(1)
-    gp[...] = passage_part(0)
+    passage_part(0, gp)
     gp_first()
-    query_part(1)
-    query_part(-1)
     z_step(3)
     y_step(2)
     gp_second()
-    query_part(0)
     each_other(lambda m: res_copy(m, me).wait_send())
+    lax.fori_loop(0, NZ, lambda i, carry: (pair_copy(i).wait_send(), carry)[1], 0)
     z_last()
     y_step(3)
     gp_third()
@@ -510,6 +559,8 @@
             pltpu.VMEM((DS, BATCHES * BATCH), BF16),
             pltpu.VMEM((NZ, BATCHES, BATCH, GROUP), F32),
             pltpu.VMEM((NZ, BATCHES, BATCH, GROUP), F32),
+            pltpu.VMEM((2, BATCH, GROUP), F32),
+            pltpu.VMEM((2, BATCH, GROUP), F32),
             pltpu.VMEM((NCORE, BATCHES, BATCH // 2, NZ * GROUP), BF16),
             pltpu.VMEM((NZ, BATCHES, 8, GROUP), F32),
             pltpu.VMEM((NZ, NYL, DS, ROWS), F32),
@@ -540,6 +591,8 @@
             pltpu.SemaphoreType.DMA((6,)),
             pltpu.SemaphoreType.DMA((MESSAGES,)),
             pltpu.SemaphoreType.DMA((MESSAGES,)),
+            pltpu.SemaphoreType.DMA((NZ,)),
+            pltpu.SemaphoreType.DMA((NZ,)),
             pltpu.SemaphoreType.DMA((OWNERS,)),
             pltpu.SemaphoreType.DMA((OWNERS,)),
             pltpu.SemaphoreType.DMA((OWNERS,)),

time: 68.9 us -> 68.4 us (level)
  no operation moved by 1% of the time
where the time goes in v2:
time: 68.4 us; the launch traced here: 67.9 us
  Pallas kernels  67.3 us (98%)
    pallas_call x1, Pallas kernels, local(): pl.pallas_call(kernel, out_shape=outs, in_specs=[hbm] * 4, out_specs=(vme...  65.6 us
    pallas_call x1, Pallas kernels, local(): pl.pallas_call(deliver, out_shape=outs, in_specs=[hbm] * 3, out_specs=(hb...  1.69 us

profile of v2, /device:TPU:2, one launch (start us, length us, event | category | flops | bytes accessed | tf_op | source)
XLA Modules:
  0.0 67.9 jit_solution(11158633256869475963)
XLA Ops:
  0.6 65.6 %shard_map.67 = (f32[128,384]{1,0:T(8,128)}, f32[64,384]{1,0:T(8,128)}, f32[1,128]{1,0:T(1,128)}) custom-call(bf16[2,8,2,128,1024]{4,3,2,1,0:T(8,128)(2,1)} %bitcast.3, bf16[2,8,2,128,384]{4,3,2,1,0:T(8,128)(2,1)} %bitcast.4, bf16[64,1024]{1,0:T(8,128)(2,1)} %tp_hbm.1, bf16[64,384]{1,0:T(8,128)(2,1)} %sp_hbm.1), custom_call_target="tpu_custom_call" | custom-call | tf_op jit(solution)/shard_map/pallas_call | solution.py:548
  66.2 1.7 %shard_map.68 = (f32[128,384]{1,0:T(8,128)}, f32[64,384]{1,0:T(8,128)}, f32[1,128]{1,0:T(1,128)}) custom-call(f32[128,384]{1,0:T(8,128)} %get-tuple-element.9.gq_in, f32[64,384]{1,0:T(8,128)} %get-tuple-element.10.gp_in, f32[1,128]{1,0:T(1,128)} %get-tuple-element.11.div_in), custom_call_target="tpu_custom_call" | custom-call | tf_op jit(solution)/shard_map/pallas_call | solution.py:610

commit v3 on v2

--- a/solution.py
+++ b/solution.py
@@ -16,7 +16,7 @@
 BATCH = 256
 GROUP = NYL * ROWS
 OWNERS = NYL * NZ
-HALF = OWN // 2
+PIECE = OWN // 4
 ZF = 192
 YF = DS - ZF
 LOG2E = math.log2(math.e)
@@ -47,7 +47,7 @@
         return self.numbers.setdefault(name, len(self.numbers))
 
 
-MESSAGES = 80
+MESSAGES = 96
 VMEM_BYTES = 60 * 1024 * 1024
 
 
@@ -56,8 +56,8 @@
     gq_out, gp_out, div_out,
     tq, sq, tqt, sqt, pbuf, spt, tw, sw, raw_a, raw_b, gt, stat, gq,
     stat_send, stat_recv, res_recv,
-    z_send_r, z_recv_r, z_send_l, z_recv_l, z_pair_send, z_pair_recv,
-    y_pair_send, y_pair_recv, y_send_r, y_recv_r, y_send_l, y_recv_l,
+    z_send, z_recv, z_pair_send, z_pair_recv,
+    y_pair_send, y_pair_recv, y_send, y_recv,
     gp, gps_send, gps_recv, gp1_send, gp1_recv, gp2_send, gp2_recv, gp3_send, gp3_recv,
     load_sem, send_sem, recv_sem, yp_send_sem, yp_recv_sem, st_send_sem, st_recv_sem, rs_send_sem, rs_recv_sem,
 ):
@@ -82,11 +82,9 @@
     def owner(m):
         return at(x, yh, m // NZ, m % NZ, k)
 
-    def slot(h, where, core, half=None):
+    def slot(h, where, core, first=0, count=4):
         b, s = place(h, where, core)
-        if half is None:
-            return pbuf.at[b, s]
-        return pbuf.at[b, s, pl.ds(half * HALF, HALF)]
+        return pbuf.at[b, s, pl.ds(first * PIECE, count * PIECE)]
 
     loads = [
         pltpu.make_async_copy(tp_hbm, pbuf.at[1, 0, :, pl.ds(0, DT)], load_sem.at[0]),
@@ -134,54 +132,67 @@
     def received(ref, name):
         message(lambda: (ref, ref), name, sibling).wait_recv()
 
-    def to_sides(h):
-        for first in (0, 1):
-            half = first
-            send(lambda half=half, h=h: (slot(h, SELF, 0, half), slot(h, LEFT, 0, half)), ("p", h, LEFT, half), right)
-            half = 1 - first
-            send(lambda half=half, h=h: (slot(h, SELF, 0, half), slot(h, RIGHT, 0, half)), ("p", h, RIGHT, half), left)
+    def passages(h, where, to_h, to_where, first, count, device):
+        send(
+            lambda: (slot(h, where, 0, first, count), slot(to_h, to_where, 0, first, count)),
+            ("p", to_h, to_where, first, count), device,
+        )
+
+    def arrived(h, where, first, count):
+        received(slot(h, where, 0, first, count), ("p", h, where, first, count))
 
     def to_sibling(h, where):
-        send(lambda h=h, where=where: (slot(h, where, 0), slot(h, where, 1)), ("sib", h, where), sibling)
-
-    def side_halves_on():
-        received(slot(0, LEFT, 0, 0), ("p", 0, LEFT, 0))
-        send(lambda: (slot(0, LEFT, 0, 0), slot(0, FAR, 0, 0)), ("p", 0, FAR, 0), right)
-        received(slot(0, RIGHT, 0, 1), ("p", 0, RIGHT, 1))
-        send(lambda: (slot(0, RIGHT, 0, 1), slot(0, FAR, 0, 1)), ("p", 0, FAR, 1), left)
-
-    def sides_to_sibling(h, rest):
-        for half in rest:
-            received(slot(h, LEFT, 0, half), ("p", h, LEFT, half))
-        to_sibling(h, LEFT)
-        for half in rest:
-            received(slot(h, RIGHT, 0, 1 - half), ("p", h, RIGHT, 1 - half))
-        to_sibling(h, RIGHT)
+        send(lambda: (slot(h, where, 0), slot(h, where, 1)), ("sib", h, where), sibling)
+
+    def far_on(i):
+        arrived(0, LEFT, i, 1)
+        passages(0, LEFT, 0, FAR, i, 1, right)
+        arrived(0, RIGHT, 2 + i, 1)
+        passages(0, RIGHT, 0, FAR, 2 + i, 1, left)
 
     def far_across():
-        for half in (0, 1):
-            received(slot(0, FAR, 0, half), ("p", 0, FAR, half))
-            send(lambda half=half: (slot(0, FAR, 0, half), slot(1, FAR, 0, half)), ("p", 1, FAR, half), across)
+        for i in (0, 2, 1, 3):
+            arrived(0, FAR, i, 1)
+            passages(0, FAR, 1, FAR, i, 1, across)
         to_sibling(0, FAR)
 
     def far_from_across():
-        for half in (0, 1):
-            received(slot(1, FAR, 0, half), ("p", 1, FAR, half))
+        for i in (0, 2, 1, 3):
+            arrived(1, FAR, i, 1)
         to_sibling(1, FAR)
+
+    def across_to_sides(first):
+        arrived(1, SELF, first, 2)
+        passages(1, SELF, 1, LEFT, first, 2, right)
+        passages(1, SELF, 1, RIGHT, first, 2, left)
+
+    def sides_to_sibling(h):
+        for where in (LEFT, RIGHT):
+            if h == 0:
+                arrived(0, where, 2 if where == LEFT else 0, 2)
+            else:
+                arrived(1, where, 0, 2)
+                arrived(1, where, 2, 2)
+            to_sibling(h, where)
 
     def from_sibling(h, where):
         received(slot(h, where, 1), ("sib", h, where))
 
-    for half in (0, 1):
-        send(lambda half=half: (slot(0, SELF, 0, half), slot(1, SELF, 0, half)), ("p", 1, SELF, half), across)
-    to_sides(0)
+    passages(0, SELF, 0, LEFT, 0, 1, right)
+    passages(0, SELF, 0, RIGHT, 2, 1, left)
+    passages(0, SELF, 1, SELF, 0, 2, across)
+    passages(0, SELF, 0, LEFT, 1, 1, right)
+    passages(0, SELF, 0, RIGHT, 3, 1, left)
+    passages(0, SELF, 0, LEFT, 2, 2, right)
+    passages(0, SELF, 0, RIGHT, 0, 2, left)
+    passages(0, SELF, 1, SELF, 2, 2, across)
     to_sibling(0, SELF)
 
     def product(i, raw):
         b, n = i // NZ, i % NZ
-        passages = pbuf[b].reshape(BATCH, DT + DS)
-        raw[0] = nn(passages[:, :DT], tqt[n])
-        raw[1] = nn(passages[:, DT:], sqt[n])
+        batch = pbuf[b].reshape(BATCH, DT + DS)
+        raw[0] = nn(batch[:, :DT], tqt[n])
+        raw[1] = nn(batch[:, DT:], sqt[n])
 
     def weights(i, raw):
         b, n = i // NZ, i % NZ
@@ -216,13 +227,16 @@
     for load in loads[2:]:
         load.wait()
     turn_queries(0, 4)
-    side_halves_on()
-    turn_queries(4, 4)
-    for half in (0, 1):
-        received(slot(1, SELF, 0, half), ("p", 1, SELF, half))
-    to_sides(1)
+    far_on(0)
+    turn_queries(4, 2)
+    far_on(1)
+    across_to_sides(0)
+    turn_queries(6, 2)
+    sides_to_sibling(0)
+    across_to_sides(2)
     to_sibling(1, SELF)
-    sides_to_sibling(0, (1,))
+    far_across()
+
     def joined(parts):
         t_max = functools.reduce(jnp.maximum, [p[0:1] for p in parts])
         s_max = functools.reduce(jnp.maximum, [p[2:3] for p in parts])
@@ -277,27 +291,23 @@
     product(0, raw_a)
 
     def score_step(j, carry):
-        @pl.when(j == 1)
-        def _():
-            far_across()
-
         @pl.when(j == 3)
         def _():
             from_sibling(0, SELF)
             from_sibling(1, SELF)
 
+        @pl.when(j == 5)
+        def _():
+            sides_to_sibling(1)
+
         @pl.when(j == 6)
         def _():
-            sides_to_sibling(1, (0, 1))
+            far_from_across()
 
         @pl.when(j == 7)
         def _():
             from_sibling(1, LEFT)
             from_sibling(1, RIGHT)
-
-        @pl.when(j == 9)
-        def _():
-            far_from_across()
 
         @pl.when(j == 11)
         def _():
@@ -364,66 +374,45 @@
         gq[n, 1] = total[:, ROWS:]
         y_pair_send[i] = gq[n, 1 - yl, ZF:].astype(BF16)
 
-    def z_part(away):
-        return gq[group(away), :, :ZF]
-
-    def y_part(away):
-        i = (4, 3, -3, 2, -2, 1, -1, 0).index(away)
-        pair_copy(i).wait_recv()
-        return gq[group(away), yl, ZF:] + y_pair_recv[i].astype(F32)
-
-    ZH, YH = ZF // 2, YF // 2
-
-    def z_start():
-        far = z_part(4).astype(BF16)
-        z_send_r[0] = far
-        send(lambda: (z_send_r.at[0, :, pl.ds(0, ZH)], z_recv_r.at[0, :, pl.ds(0, ZH)]), ("zr", 0), up)
-        send(lambda: (z_send_r.at[0, :, pl.ds(ZH, ZH)], z_recv_l.at[0, :, pl.ds(ZH, ZH)]), ("zl", 0), down)
-
-    def y_start():
-        y_send_r[0] = y_part(4).astype(BF16)
-        send(lambda: (y_send_r.at[0, pl.ds(0, YH)], y_recv_r.at[0, pl.ds(0, YH)]), ("yr", 0), up)
-        send(lambda: (y_send_r.at[0, pl.ds(YH, YH)], y_recv_l.at[0, pl.ds(YH, YH)]), ("yl", 0), down)
-
-    def z_step(step):
-        if step == 1:
-            mine = z_part(3)
-            received(z_recv_r.at[0, :, pl.ds(0, ZH)], ("zr", 0))
-            z_send_r[1, :, :ZH] = (mine[:, :ZH] + z_recv_r[0, :, :ZH].astype(F32)).astype(BF16)
-            z_send_r[1, :, ZH:] = mine[:, ZH:].astype(BF16)
-        else:
-            received(z_recv_r.at[step - 1], ("zr", step - 1))
-            z_send_r[step] = (z_part(4 - step) + z_recv_r[step - 1].astype(F32)).astype(BF16)
-        send(lambda step=step: (z_send_r.at[step], z_recv_r.at[step]), ("zr", step), up)
-        if step == 1:
-            mine = z_part(-3)
-            received(z_recv_l.at[0, :, pl.ds(ZH, ZH)], ("zl", 0))
-            z_send_l[1, :, :ZH] = mine[:, :ZH].astype(BF16)
-            z_send_l[1, :, ZH:] = (mine[:, ZH:] + z_recv_l[0, :, ZH:].astype(F32)).astype(BF16)
-        else:
-            received(z_recv_l.at[step - 1], ("zl", step - 1))
-            z_send_l[step] = (z_part(step - 4) + z_recv_l[step - 1].astype(F32)).astype(BF16)
-        send(lambda step=step: (z_send_l.at[step], z_recv_l.at[step]), ("zl", step), down)
-
-    def y_step(step):
-        mine = y_part(4 - step)
-        if step == 1:
-            received(y_recv_r.at[0, pl.ds(0, YH)], ("yr", 0))
-            y_send_r[1, :YH] = (mine[:YH] + y_recv_r[0, :YH].astype(F32)).astype(BF16)
-            y_send_r[1, YH:] = mine[YH:].astype(BF16)
-        else:
-            received(y_recv_r.at[step - 1], ("yr", step - 1))
-            y_send_r[step] = (mine + y_recv_r[step - 1].astype(F32)).astype(BF16)
-        send(lambda step=step: (y_send_r.at[step], y_recv_r.at[step]), ("yr", step), up)
-        mine = y_part(step - 4)
-        if step == 1:
-            received(y_recv_l.at[0, pl.ds(YH, YH)], ("yl", 0))
-            y_send_l[1, :YH] = mine[:YH].astype(BF16)
-            y_send_l[1, YH:] = (mine[YH:] + y_recv_l[0, YH:].astype(F32)).astype(BF16)
-        else:
-            received(y_recv_l.at[step - 1], ("yl", step - 1))
-            y_send_l[step] = (mine + y_recv_l[step - 1].astype(F32)).astype(BF16)
-        send(lambda step=step: (y_send_l.at[step], y_recv_l.at[step]), ("yl", step), down)
+    def order(away):
+        return (4, 3, -3, 2, -2, 1, -1, 0).index(4 if away == -4 else away)
+
+    def pair_arrived(away):
+        pair_copy(order(away)).wait_recv()
+
+    def part(chain, away):
+        n = group(away)
+        if chain < 2:
+            return gq[n, chain, :ZF]
+        i = order(away)
+        start = (chain - 2) * YF // 2
+        pair = y_pair_recv[i, start:start + YF // 2].astype(F32)
+        return gq[n, yl, ZF + start:ZF + start + YF // 2] + pair
+
+    rings = (z_send, z_recv), (y_send, y_recv)
+
+    def slots(chain, way, step):
+        sends, recvs = rings[chain // 2]
+        return sends.at[chain % 2, way, step], recvs.at[chain % 2, way, step]
+
+    def come(chain, way, step):
+        received(slots(chain, way, step)[1], ("ring", chain, way, step))
+        return rings[chain // 2][1][chain % 2, way, step].astype(F32)
+
+    def ring_step(chain, way, step):
+        total = part(chain, 4 - step if way == 0 else step - 4)
+        if step > 1 or (step == 1 and chain % 2 == way):
+            total = total + come(chain, way, step - 1)
+        rings[chain // 2][0][chain % 2, way, step] = total.astype(BF16)
+        send(lambda: slots(chain, way, step), ("ring", chain, way, step), down if way else up)
+
+    def ring_steps(chains, step):
+        for chain in chains:
+            for way in (chain % 2, 1 - chain % 2):
+                ring_step(chain, way, step)
+
+    def ring_total(chain):
+        return part(chain, 0) + come(chain, 0, 3) + come(chain, 1, 3)
 
     def passage_part(core, to):
         to[...] = jnp.zeros_like(to)
@@ -467,14 +456,6 @@
     def x_total(h):
         return gp_of(h, SELF) + gp2_recv[0, h].astype(F32) + gp2_recv[1, h].astype(F32)
 
-    def z_last():
-        received(z_recv_r.at[3], ("zr", 3))
-        received(z_recv_l.at[3], ("zl", 3))
-        for y in range(NYL):
-            gq[z, y, :ZF] = gq[z, y, :ZF] + z_recv_r[3, y].astype(F32) + z_recv_l[3, y].astype(F32)
-        z_pair_send[...] = gq[z, 1 - yl, :ZF].astype(BF16)
-        send(lambda: (z_pair_send, z_pair_recv), "z pair", y_mate)
-
     form(0)
 
     def gradient_step(i, carry):
@@ -484,39 +465,63 @@
 
         @pl.when(i == 0)
         def _():
-            z_start()
+            ring_step(0, 0, 0)
+            ring_step(1, 1, 0)
+
+        @pl.when(i == 2)
+        def _():
+            ring_step(1, 0, 1)
+            ring_step(0, 1, 1)
 
         @pl.when(i == 5)
         def _():
-            z_step(1)
-            y_start()
+            ring_step(0, 0, 1)
+            ring_step(1, 1, 1)
+
+        @pl.when(i == 6)
+        def _():
+            pair_arrived(4)
+            ring_step(2, 0, 0)
+            ring_step(3, 1, 0)
+            pair_arrived(3)
+            ring_step(3, 0, 1)
+            pair_arrived(-3)
+            ring_step(2, 1, 1)
 
         return carry
 
     lax.fori_loop(0, NZ - 1, gradient_step, 0)
     query_part(NZ - 1)
     pair_copy(NZ - 1).start()
+    ring_steps((0, 1), 2)
     passage_part(1, gp)
     gps_send[...] = gp[...].astype(BF16)
     send(lambda: (gps_send, gps_recv), "gp sibling", sibling)
-    z_step(2)
-    y_step(1)
+    ring_step(2, 0, 1)
+    ring_step(3, 1, 1)
     passage_part(0, gp)
     gp_first()
-    z_step(3)
-    y_step(2)
+    ring_steps((0, 1), 3)
+    pair_arrived(2)
+    pair_arrived(-2)
+    ring_steps((2, 3), 2)
     gp_second()
     each_other(lambda m: res_copy(m, me).wait_send())
     lax.fori_loop(0, NZ, lambda i, carry: (pair_copy(i).wait_send(), carry)[1], 0)
-    z_last()
-    y_step(3)
+    pair_arrived(1)
+    pair_arrived(-1)
+    for y in range(NYL):
+        gq[z, y, :ZF] = ring_total(y)
+    z_pair_send[...] = gq[z, 1 - yl, :ZF].astype(BF16)
+    send(lambda: (z_pair_send, z_pair_recv), "z pair", y_mate)
+    ring_steps((2, 3), 3)
     gp_third()
     flush()
-
-    mine = y_part(0)
-    received(y_recv_r.at[3], ("yr", 3))
-    received(y_recv_l.at[3], ("yl", 3))
-    gq_out[:, ZF:] = (mine + y_recv_r[3].astype(F32) + y_recv_l[3].astype(F32)).T
+    pair_arrived(0)
+    for chain in (2, 3):
+        start = ZF + (chain - 2) * YF // 2
+        gq[z, yl, start:start + YF // 2] = ring_total(chain)
+    gq_out[:, ZF:] = gq[z, yl, ZF:].T
     received(z_pair_recv, "z pair")
     gq_out[:, :ZF] = (gq[z, yl, :ZF] + z_pair_recv[...].astype(F32)).T
     received(gp3_recv, "gp across")
@@ -567,18 +572,14 @@
             pltpu.VMEM((OWNERS, 8, ROWS), F32),
             pltpu.VMEM((OWNERS, 8, ROWS), F32),
             pltpu.VMEM((OWNERS, 8, ROWS), F32),
-            pltpu.VMEM((4, NYL, ZF, ROWS), BF16),
-            pltpu.VMEM((4, NYL, ZF, ROWS), BF16),
-            pltpu.VMEM((4, NYL, ZF, ROWS), BF16),
-            pltpu.VMEM((4, NYL, ZF, ROWS), BF16),
+            pltpu.VMEM((2, 2, 4, ZF, ROWS), BF16),
+            pltpu.VMEM((2, 2, 4, ZF, ROWS), BF16),
             pltpu.VMEM((ZF, ROWS), BF16),
             pltpu.VMEM((ZF, ROWS), BF16),
             pltpu.VMEM((NZ, YF, ROWS), BF16),
             pltpu.VMEM((NZ, YF, ROWS), BF16),
-            pltpu.VMEM((4, YF, ROWS), BF16),
-            pltpu.VMEM((4, YF, ROWS), BF16),
-            pltpu.VMEM((4, YF, ROWS), BF16),
-            pltpu.VMEM((4, YF, ROWS), BF16),
+            pltpu.VMEM((2, 2, 4, YF // 2, ROWS), BF16),
+            pltpu.VMEM((2, 2, 4, YF // 2, ROWS), BF16),
             pltpu.VMEM((BATCHES, 2, OWN, DS), F32),
             pltpu.VMEM((BATCHES, 2, OWN, DS), BF16),
             pltpu.VMEM((BATCHES, 2, OWN, DS), BF16),

time: 68.4 us -> 70.5 us (1.031)
  Pallas kernels: 67.3 us -> 69.8 us
    pallas_call x1, Pallas kernels: 65.6 us -> 68.1 us  [local(): pl.pallas_call(kernel, out_shape=outs, in_specs=[hbm] * 4, out_specs=(vme...]
where the time goes in v3:
time: 70.5 us; the launch traced here: 70.4 us
  Pallas kernels  69.8 us (99%)
    pallas_call x1, Pallas kernels, local(): pl.pallas_call(kernel, out_shape=outs, in_specs=[hbm] * 4, out_specs=(vme...  68.1 us
    pallas_call x1, Pallas kernels, local(): pl.pallas_call(deliver, out_shape=outs, in_specs=[hbm] * 3, out_specs=(hb...  1.69 us

profile of v3, /device:TPU:2, one launch (start us, length us, event | category | flops | bytes accessed | tf_op | source)
XLA Modules:
  0.0 70.4 jit_solution(10177381457901326643)
XLA Ops:
  0.6 68.1 %shard_map.67 = (f32[128,384]{1,0:T(8,128)}, f32[64,384]{1,0:T(8,128)}, f32[1,128]{1,0:T(1,128)}) custom-call(bf16[2,8,2,128,1024]{4,3,2,1,0:T(8,128)(2,1)} %bitcast.3, bf16[2,8,2,128,384]{4,3,2,1,0:T(8,128)(2,1)} %bitcast.4, bf16[64,1024]{1,0:T(8,128)(2,1)} %tp_hbm.1, bf16[64,384]{1,0:T(8,128)(2,1)} %sp_hbm.1), custom_call_target="tpu_custom_call" | custom-call | tf_op jit(solution)/shard_map/pallas_call | solution.py:553
  68.7 1.7 %shard_map.68 = (f32[128,384]{1,0:T(8,128)}, f32[64,384]{1,0:T(8,128)}, f32[1,128]{1,0:T(1,128)}) custom-call(f32[128,384]{1,0:T(8,128)} %get-tuple-element.9.gq_in, f32[64,384]{1,0:T(8,128)} %get-tuple-element.10.gp_in, f32[1,128]{1,0:T(1,128)} %get-tuple-element.11.div_in), custom_call_target="tpu_custom_call" | custom-call | tf_op jit(solution)/shard_map/pallas_call | solution.py:611

commit v4 on v2

--- a/solution.py
+++ b/solution.py
@@ -13,6 +13,7 @@
 ROWS = 128
 DT, DS = 1024, 384
 BATCHES = 4
+SLOTS = 4
 BATCH = 256
 GROUP = NYL * ROWS
 OWNERS = NYL * NZ
@@ -35,6 +36,18 @@
     return 2 * h, core * 2 + (where - LEFT)
 
 
+def div(a, b):
+    return lax.div(a, jnp.int32(b))
+
+
+def rem(a, b):
+    return lax.rem(a, jnp.int32(b))
+
+
+def nt(a, b):
+    return lax.dot_general(a, b, (((1,), (1,)), ((), ())), preferred_element_type=F32)
+
+
 def nn(a, b):
     return lax.dot_general(a, b, (((1,), (0,)), ((), ())), preferred_element_type=F32)
 
@@ -54,43 +67,50 @@
 def kernel(
     tq_hbm, sq_hbm, tp_hbm, sp_hbm,
     gq_out, gp_out, div_out,
-    tq, sq, tqt, sqt, pbuf, spt, tw, sw, raw_a, raw_b, gt, stat, gq,
+    tq, sq, pbuf, spt, tw, sw, raw_a, raw_b, gt, stat, gq,
     stat_send, stat_recv, res_recv,
-    z_send_r, z_recv_r, z_send_l, z_recv_l, z_pair_send, z_pair_recv,
-    y_pair_send, y_pair_recv, y_send_r, y_recv_r, y_send_l, y_recv_l,
+    z_send, z_recv_r, z_recv_l, z_pair_send, z_pair_recv,
+    y_pair_send, y_pair_recv, y_send, y_recv_r, y_recv_l,
     gp, gps_send, gps_recv, gp1_send, gp1_recv, gp2_send, gp2_recv, gp3_send, gp3_recv,
-    load_sem, send_sem, recv_sem, yp_send_sem, yp_recv_sem, st_send_sem, st_recv_sem, rs_send_sem, rs_recv_sem,
+    load_sem, gather_sem, ring_sem, send_sem, recv_sem, yp_recv_sem, st_sem,
 ):
     t_scale = DT ** (-0.5) * LOG2E
     s_scale = DS ** (-0.5) * LOG2E
     factor = DS ** (-0.5)
     q = lax.axis_index("query")
     c = lax.axis_index("corpus")
-    x, yh = q // NYH, q % NYH
-    yl, z, k = c // (NZ * NCORE), (c // NCORE) % NZ, c % NCORE
+    x, yh = div(q, NYH), rem(q, NYH)
+    yl, z, k = div(c, NZ * NCORE), rem(div(c, NCORE), NZ), rem(c, NCORE)
     me = yl * NZ + z
 
     def at(x_, yh_, yl_, z_, k_):
         return (x_ * NYH + yh_, (yl_ * NZ + z_) * NCORE + k_)
 
-    right, left = at((x + 1) % NX, yh, yl, z, k), at((x + NX - 1) % NX, yh, yl, z, k)
+    right, left = at(rem(x + 1, NX), yh, yl, z, k), at(rem(x + NX - 1, NX), yh, yl, z, k)
     across = at(x, 1 - yh, 1 - yl, z, k)
     sibling = at(x, yh, yl, z, 1 - k)
-    up, down = at(x, yh, yl, (z + 1) % NZ, k), at(x, yh, yl, (z + NZ - 1) % NZ, k)
+    up, down = at(x, yh, yl, rem(z + 1, NZ), k), at(x, yh, yl, rem(z + NZ - 1, NZ), k)
     y_mate = at(x, yh, 1 - yl, z, k)
 
-    def owner(m):
-        return at(x, yh, m // NZ, m % NZ, k)
+    offsets = [(dy, dz) for dy in range(NYL) for dz in range(NZ) if (dy, dz) != (0, 0)]
+    y_of = [yl, 1 - yl]
+    z_of = [rem(z + dz, NZ) for dz in range(NZ)]
+
+    def offset_device(dy, dz):
+        return at(x, yh, y_of[dy], z_of[dz], k)
 
     def slot(h, where, core, half=None):
         b, s = place(h, where, core)
         if half is None:
-            return pbuf.at[b, s]
-        return pbuf.at[b, s, pl.ds(half * HALF, HALF)]
+            return pbuf.at[b * SLOTS + s]
+        return pbuf.at[b * SLOTS + s, pl.ds(half * HALF, HALF)]
+
+    def both(b, core):
+        return pbuf.at[pl.ds(b * SLOTS + core * 2, 2)]
 
     loads = [
-        pltpu.make_async_copy(tp_hbm, pbuf.at[1, 0, :, pl.ds(0, DT)], load_sem.at[0]),
-        pltpu.make_async_copy(sp_hbm, pbuf.at[1, 0, :, pl.ds(DT, DS)], load_sem.at[1]),
+        pltpu.make_async_copy(tp_hbm, pbuf.at[SLOTS, :, pl.ds(0, DT)], load_sem.at[0]),
+        pltpu.make_async_copy(sp_hbm, pbuf.at[SLOTS, :, pl.ds(DT, DS)], load_sem.at[1]),
     ]
     for y in range(NYL):
         loads.append(pltpu.make_async_copy(tq_hbm.at[y, :, k], tq.at[:, y], load_sem.at[2 + y]))
@@ -102,11 +122,8 @@
     for device in (right, left, across, sibling):
         pl.semaphore_signal(barrier, inc=1, device_id=device, device_id_type=MESH)
 
-    def greet(i, carry):
-        pl.semaphore_signal(barrier, inc=1, device_id=owner((me + i) % OWNERS), device_id_type=MESH)
-        return carry
-
-    lax.fori_loop(1, OWNERS, greet, 0)
+    for offset in offsets:
+        pl.semaphore_signal(barrier, inc=1, device_id=offset_device(*offset), device_id_type=MESH)
     pl.semaphore_wait(barrier, 4 + OWNERS - 1)
     loads[0].wait()
     loads[1].wait()
@@ -114,11 +131,11 @@
     number = Messages()
     sent = []
 
-    def message(refs, name, device):
+    def message(refs, name, device, out=None):
         i = number(name)
         src, dst = refs()
         return pltpu.make_async_remote_copy(
-            src_ref=src, dst_ref=dst, send_sem=send_sem.at[i], recv_sem=recv_sem.at[i],
+            src_ref=src, dst_ref=dst, send_sem=send_sem.at[i] if out is None else out, recv_sem=recv_sem.at[i],
             device_id=device, device_id_type=MESH,
         )
 
@@ -134,57 +151,65 @@
     def received(ref, name):
         message(lambda: (ref, ref), name, sibling).wait_recv()
 
-    def to_sides(h):
-        for first in (0, 1):
-            half = first
-            send(lambda half=half, h=h: (slot(h, SELF, 0, half), slot(h, LEFT, 0, half)), ("p", h, LEFT, half), right)
-            half = 1 - first
-            send(lambda half=half, h=h: (slot(h, SELF, 0, half), slot(h, RIGHT, 0, half)), ("p", h, RIGHT, half), left)
-
-    def to_sibling(h, where):
-        send(lambda h=h, where=where: (slot(h, where, 0), slot(h, where, 1)), ("sib", h, where), sibling)
-
-    def side_halves_on():
-        received(slot(0, LEFT, 0, 0), ("p", 0, LEFT, 0))
-        send(lambda: (slot(0, LEFT, 0, 0), slot(0, FAR, 0, 0)), ("p", 0, FAR, 0), right)
-        received(slot(0, RIGHT, 0, 1), ("p", 0, RIGHT, 1))
-        send(lambda: (slot(0, RIGHT, 0, 1), slot(0, FAR, 0, 1)), ("p", 0, FAR, 1), left)
-
-    def sides_to_sibling(h, rest):
-        for half in rest:
-            received(slot(h, LEFT, 0, half), ("p", h, LEFT, half))
-        to_sibling(h, LEFT)
-        for half in rest:
-            received(slot(h, RIGHT, 0, 1 - half), ("p", h, RIGHT, 1 - half))
-        to_sibling(h, RIGHT)
+    def spread(refs, name, device):
+        message(refs, name, device, gather_sem).start()
+
+    def spread_wait():
+        everything = pbuf.at[pl.ds(0, BATCHES * SLOTS - 1)]
+        message(lambda: (everything, everything), "gather", sibling, gather_sem).wait_send()
+
+    def half_to(where, half, device):
+        spread(lambda: (slot(0, SELF, 0, half), slot(0, where, 0, half)), ("p", where, half), device)
+
+    def sides_to_sibling(h):
+        if h == 0:
+            received(slot(0, LEFT, 0, 1), ("p", LEFT, 1))
+            received(slot(0, RIGHT, 0, 0), ("p", RIGHT, 0))
+        else:
+            received(slot(1, LEFT, 0), ("p1", LEFT))
+            received(slot(1, RIGHT, 0), ("p1", RIGHT))
+        to_sibling(2 * h)
+
+    def to_sibling(b):
+        spread(lambda: (both(b, 0), both(b, 1)), ("sib", b), sibling)
+
+    def from_sibling(b):
+        received(both(b, 1), ("sib", b))
+
+    def far_on():
+        received(slot(0, LEFT, 0, 0), ("p", LEFT, 0))
+        spread(lambda: (slot(0, LEFT, 0, 0), slot(0, FAR, 0, 0)), ("far",), right)
+        received(slot(0, RIGHT, 0, 1), ("p", RIGHT, 1))
+        spread(lambda: (slot(0, RIGHT, 0, 1), slot(0, FAR, 0, 1)), ("far",), left)
+
+    def across_on():
+        received(slot(1, SELF, 0), ("across",))
+        spread(lambda: (slot(1, SELF, 0), slot(1, LEFT, 0)), ("p1", LEFT), right)
+        spread(lambda: (slot(1, SELF, 0), slot(1, RIGHT, 0)), ("p1", RIGHT), left)
+        to_sibling(1)
 
     def far_across():
-        for half in (0, 1):
-            received(slot(0, FAR, 0, half), ("p", 0, FAR, half))
-            send(lambda half=half: (slot(0, FAR, 0, half), slot(1, FAR, 0, half)), ("p", 1, FAR, half), across)
-        to_sibling(0, FAR)
+        received(slot(0, FAR, 0), ("far",))
+        spread(lambda: (slot(0, FAR, 0), slot(1, FAR, 0)), ("far across",), across)
 
     def far_from_across():
-        for half in (0, 1):
-            received(slot(1, FAR, 0, half), ("p", 1, FAR, half))
-        to_sibling(1, FAR)
-
-    def from_sibling(h, where):
-        received(slot(h, where, 1), ("sib", h, where))
-
-    for half in (0, 1):
-        send(lambda half=half: (slot(0, SELF, 0, half), slot(1, SELF, 0, half)), ("p", 1, SELF, half), across)
-    to_sides(0)
-    to_sibling(0, SELF)
+        received(slot(1, FAR, 0), ("far across",))
+        to_sibling(3)
+
+    half_to(LEFT, 0, right)
+    half_to(RIGHT, 1, left)
+    spread(lambda: (slot(0, SELF, 0), slot(1, SELF, 0)), ("across",), across)
+    half_to(LEFT, 1, right)
+    half_to(RIGHT, 0, left)
 
     def product(i, raw):
-        b, n = i // NZ, i % NZ
-        passages = pbuf[b].reshape(BATCH, DT + DS)
-        raw[0] = nn(passages[:, :DT], tqt[n])
-        raw[1] = nn(passages[:, DT:], sqt[n])
+        b, n = div(i, NZ), rem(i, NZ)
+        batch = pbuf[pl.ds(b * SLOTS, SLOTS)].reshape(BATCH, DT + DS)
+        raw[0] = nt(batch[:, :DT], tq[n].reshape(GROUP, DT))
+        raw[1] = nt(batch[:, DT:], sq[n].reshape(GROUP, DS))
 
     def weights(i, raw):
-        b, n = i // NZ, i % NZ
+        b, n = div(i, NZ), rem(i, NZ)
         t = raw[0] * t_scale
         s = raw[1] * s_scale
         t_max = jnp.max(t, axis=0, keepdims=True)
@@ -199,30 +224,19 @@
         stat[n, b] = jnp.concatenate([t_max, t_sum, s_max, s_sum, cross, cross, cross, cross], axis=0)
 
     def turn(b):
-        turned = pbuf[b].reshape(BATCH, DT + DS)[:, DT:].T
+        turned = pbuf[b * SLOTS:(b + 1) * SLOTS].reshape(BATCH, DT + DS)[:, DT:].T
         part = BATCH // NCORE
         for core in range(NCORE):
             start = (core * BATCHES + b) * part
             spt[:, start:start + part] = turned[:, core * part:(core + 1) * part]
 
-    def turn_queries(first, count):
-        def body(n, carry):
-            tqt[n] = tq[n].reshape(GROUP, DT).T
-            sqt[n] = sq[n].reshape(GROUP, DS).T
-            return carry
-
-        lax.fori_loop(first, first + count, body, 0)
-
+    far_on()
+    across_on()
+    sides_to_sibling(0)
+    far_across()
     for load in loads[2:]:
         load.wait()
-    turn_queries(0, 4)
-    side_halves_on()
-    turn_queries(4, 4)
-    for half in (0, 1):
-        received(slot(1, SELF, 0, half), ("p", 1, SELF, half))
-    to_sides(1)
-    to_sibling(1, SELF)
-    sides_to_sibling(0, (1,))
+
     def joined(parts):
         t_max = functools.reduce(jnp.maximum, [p[0:1] for p in parts])
         s_max = functools.reduce(jnp.maximum, [p[2:3] for p in parts])
@@ -233,26 +247,26 @@
         cross = functools.reduce(jnp.add, [p[4:5] * w for p, w in zip(parts, t_in)])
         return t_max, t_sum, s_max, s_sum, cross
 
-    def stat_copy(m_to, m_slot):
+    def stat_copy(dy, dz):
         return pltpu.make_async_remote_copy(
-            src_ref=stat_send.at[m_to], dst_ref=stat_recv.at[m_slot],
-            send_sem=st_send_sem.at[m_to], recv_sem=st_recv_sem.at[m_slot],
-            device_id=owner(m_to), device_id_type=MESH,
+            src_ref=stat_send.at[y_of[dy] * NZ + z_of[dz]], dst_ref=stat_recv.at[dy * NZ + (NZ - dz) % NZ],
+            send_sem=st_sem.at[0], recv_sem=st_sem.at[1],
+            device_id=offset_device(dy, dz), device_id_type=MESH,
         )
 
-    def res_copy(m_to, m_slot):
+    def res_copy(dy, dz):
         return pltpu.make_async_remote_copy(
-            src_ref=res_recv.at[m_slot], dst_ref=res_recv.at[m_slot],
-            send_sem=rs_send_sem.at[m_to], recv_sem=rs_recv_sem.at[m_slot],
-            device_id=owner(m_to), device_id_type=MESH,
+            src_ref=res_recv.at[me], dst_ref=res_recv.at[me],
+            send_sem=st_sem.at[2], recv_sem=st_sem.at[3],
+            device_id=offset_device(dy, dz), device_id_type=MESH,
         )
 
-    def each_other(step):
-        def body(i, carry):
-            step((me + i) % OWNERS)
-            return carry
-
-        lax.fori_loop(1, OWNERS, body, 0)
+    def all_copies(ref, first):
+        others = ref.at[pl.ds(0, OWNERS - 1)]
+        return pltpu.make_async_remote_copy(
+            src_ref=others, dst_ref=others, send_sem=st_sem.at[first], recv_sem=st_sem.at[first + 1],
+            device_id=sibling, device_id_type=MESH,
+        )
 
     def leave(first):
         for n in range(first, first + 4):
@@ -261,48 +275,26 @@
             for y in range(NYL):
                 stat_send[y * NZ + n] = whole[:, y * ROWS:(y + 1) * ROWS]
 
-        def body(i, carry):
-            m = (i // 4) * NZ + first + i % 4
-
-            @pl.when(m != me)
-            def _():
-                stat_copy(m, me).start()
-
-            return carry
-
-        lax.fori_loop(0, 8, body, 0)
-
-    from_sibling(0, LEFT)
-    from_sibling(0, RIGHT)
+    from_sibling(0)
     product(0, raw_a)
 
     def score_step(j, carry):
-        @pl.when(j == 1)
-        def _():
-            far_across()
-
         @pl.when(j == 3)
         def _():
-            from_sibling(0, SELF)
-            from_sibling(1, SELF)
-
-        @pl.when(j == 6)
+            from_sibling(1)
+
+        @pl.when(j == 5)
         def _():
-            sides_to_sibling(1, (0, 1))
+            sides_to_sibling(1)
 
         @pl.when(j == 7)
         def _():
-            from_sibling(1, LEFT)
-            from_sibling(1, RIGHT)
-
-        @pl.when(j == 9)
-        def _():
             far_from_across()
+            from_sibling(2)
 
         @pl.when(j == 11)
         def _():
-            from_sibling(0, FAR)
-            from_sibling(1, FAR)
+            from_sibling(3)
 
         @pl.when(j == 14)
         def _():
@@ -316,25 +308,28 @@
 
     lax.fori_loop(0, BATCHES * NZ // 2, score_step, 0)
     leave(4)
-    stat_recv[me] = stat_send[me]
+    for offset in offsets:
+        stat_copy(*offset).start()
+    stat_recv[0] = stat_send[me]
     for b in range(BATCHES):
         turn(b)
-    flush()
-    each_other(lambda m: stat_copy(m, m).wait_recv())
+    spread_wait()
+    all_copies(stat_recv, 0).wait_recv()
     t_max, t_sum, s_max, s_sum, cross = joined([stat_recv[m] for m in range(OWNERS)])
     t_in, s_in = factor / t_sum, factor / s_sum
     res_recv[me] = jnp.concatenate([t_max, t_in, s_max, s_in, t_in, t_in, t_in, t_in], axis=0)
-    each_other(lambda m: res_copy(m, me).start())
+    for offset in offsets:
+        res_copy(*offset).start()
     div_out[...] = cross * LN2 / t_sum - (t_max * LN2 + jnp.log(t_sum)) + (s_max * LN2 + jnp.log(s_sum))
-    each_other(lambda m: stat_copy(m, me).wait_send())
-    each_other(lambda m: res_copy(m, m).wait_recv())
+    all_copies(stat_send, 0).wait_send()
+    all_copies(res_recv, 2).wait_recv()
 
     def group(away):
-        return (z + NZ + away) % NZ
+        return rem(z + NZ + away, NZ)
 
     def sequence(i):
-        size = 4 - (i + 1) // 2
-        return group(size * (2 * (i % 2) - 1))
+        size = 4 - div(i + 1, 2)
+        return group(size * (2 * rem(i, 2) - 1))
 
     def lanes(n):
         return pl.ds(pl.multiple_of(n * GROUP, GROUP), GROUP)
@@ -353,7 +348,7 @@
     def pair_copy(i):
         return pltpu.make_async_remote_copy(
             src_ref=y_pair_send.at[i], dst_ref=y_pair_recv.at[i],
-            send_sem=yp_send_sem.at[i], recv_sem=yp_recv_sem.at[i],
+            send_sem=ring_sem.at[2], recv_sem=yp_recv_sem.at[i],
             device_id=y_mate, device_id_type=MESH,
         )
 
@@ -376,54 +371,54 @@
 
     def z_start():
         far = z_part(4).astype(BF16)
-        z_send_r[0] = far
-        send(lambda: (z_send_r.at[0, :, pl.ds(0, ZH)], z_recv_r.at[0, :, pl.ds(0, ZH)]), ("zr", 0), up)
-        send(lambda: (z_send_r.at[0, :, pl.ds(ZH, ZH)], z_recv_l.at[0, :, pl.ds(ZH, ZH)]), ("zl", 0), down)
+        z_send[0] = far
+        message(lambda: (z_send.at[0, :, pl.ds(0, ZH)], z_recv_r.at[0, :, pl.ds(0, ZH)]), ("zr", 0), up, ring_sem.at[0]).start()
+        message(lambda: (z_send.at[0, :, pl.ds(ZH, ZH)], z_recv_l.at[0, :, pl.ds(ZH, ZH)]), ("zl", 0), down, ring_sem.at[0]).start()
 
     def y_start():
-        y_send_r[0] = y_part(4).astype(BF16)
-        send(lambda: (y_send_r.at[0, pl.ds(0, YH)], y_recv_r.at[0, pl.ds(0, YH)]), ("yr", 0), up)
-        send(lambda: (y_send_r.at[0, pl.ds(YH, YH)], y_recv_l.at[0, pl.ds(YH, YH)]), ("yl", 0), down)
+        y_send[0] = y_part(4).astype(BF16)
+        message(lambda: (y_send.at[0, pl.ds(0, YH)], y_recv_r.at[0, pl.ds(0, YH)]), ("yr", 0), up, ring_sem.at[1]).start()
+        message(lambda: (y_send.at[0, pl.ds(YH, YH)], y_recv_l.at[0, pl.ds(YH, YH)]), ("yl", 0), down, ring_sem.at[1]).start()
 
     def z_step(step):
         if step == 1:
             mine = z_part(3)
             received(z_recv_r.at[0, :, pl.ds(0, ZH)], ("zr", 0))
-            z_send_r[1, :, :ZH] = (mine[:, :ZH] + z_recv_r[0, :, :ZH].astype(F32)).astype(BF16)
-            z_send_r[1, :, ZH:] = mine[:, ZH:].astype(BF16)
+            z_send[1, :, :ZH] = (mine[:, :ZH] + z_recv_r[0, :, :ZH].astype(F32)).astype(BF16)
+            z_send[1, :, ZH:] = mine[:, ZH:].astype(BF16)
         else:
             received(z_recv_r.at[step - 1], ("zr", step - 1))
-            z_send_r[step] = (z_part(4 - step) + z_recv_r[step - 1].astype(F32)).astype(BF16)
-        send(lambda step=step: (z_send_r.at[step], z_recv_r.at[step]), ("zr", step), up)
+            z_send[step] = (z_part(4 - step) + z_recv_r[step - 1].astype(F32)).astype(BF16)
+        message(lambda step=step: (z_send.at[step], z_recv_r.at[step]), ("zr", step), up, ring_sem.at[0]).start()
         if step == 1:
             mine = z_part(-3)
             received(z_recv_l.at[0, :, pl.ds(ZH, ZH)], ("zl", 0))
-            z_send_l[1, :, :ZH] = mine[:, :ZH].astype(BF16)
-            z_send_l[1, :, ZH:] = (mine[:, ZH:] + z_recv_l[0, :, ZH:].astype(F32)).astype(BF16)
+            z_send[5, :, :ZH] = mine[:, :ZH].astype(BF16)
+            z_send[5, :, ZH:] = (mine[:, ZH:] + z_recv_l[0, :, ZH:].astype(F32)).astype(BF16)
         else:
             received(z_recv_l.at[step - 1], ("zl", step - 1))
-            z_send_l[step] = (z_part(step - 4) + z_recv_l[step - 1].astype(F32)).astype(BF16)
-        send(lambda step=step: (z_send_l.at[step], z_recv_l.at[step]), ("zl", step), down)
+            z_send[4 + step] = (z_part(step - 4) + z_recv_l[step - 1].astype(F32)).astype(BF16)
+        message(lambda step=step: (z_send.at[4 + step], z_recv_l.at[step]), ("zl", step), down, ring_sem.at[0]).start()
 
     def y_step(step):
         mine = y_part(4 - step)
         if step == 1:
             received(y_recv_r.at[0, pl.ds(0, YH)], ("yr", 0))
-            y_send_r[1, :YH] = (mine[:YH] + y_recv_r[0, :YH].astype(F32)).astype(BF16)
-            y_send_r[1, YH:] = mine[YH:].astype(BF16)
+            y_send[1, :YH] = (mine[:YH] + y_recv_r[0, :YH].astype(F32)).astype(BF16)
+            y_send[1, YH:] = mine[YH:].astype(BF16)
         else:
             received(y_recv_r.at[step - 1], ("yr", step - 1))
-            y_send_r[step] = (mine + y_recv_r[step - 1].astype(F32)).astype(BF16)
-        send(lambda step=step: (y_send_r.at[step], y_recv_r.at[step]), ("yr", step), up)
+            y_send[step] = (mine + y_recv_r[step - 1].astype(F32)).astype(BF16)
+        message(lambda step=step: (y_send.at[step], y_recv_r.at[step]), ("yr", step), up, ring_sem.at[1]).start()
         mine = y_part(step - 4)
         if step == 1:
             received(y_recv_l.at[0, pl.ds(YH, YH)], ("yl", 0))
-            y_send_l[1, :YH] = mine[:YH].astype(BF16)
-            y_send_l[1, YH:] = (mine[YH:] + y_recv_l[0, YH:].astype(F32)).astype(BF16)
+            y_send[5, :YH] = mine[:YH].astype(BF16)
+            y_send[5, YH:] = (mine[YH:] + y_recv_l[0, YH:].astype(F32)).astype(BF16)
         else:
             received(y_recv_l.at[step - 1], ("yl", step - 1))
-            y_send_l[step] = (mine + y_recv_l[step - 1].astype(F32)).astype(BF16)
-        send(lambda step=step: (y_send_l.at[step], y_recv_l.at[step]), ("yl", step), down)
+            y_send[4 + step] = (mine + y_recv_l[step - 1].astype(F32)).astype(BF16)
+        message(lambda step=step: (y_send.at[4 + step], y_recv_l.at[step]), ("yl", step), down, ring_sem.at[1]).start()
 
     def passage_part(core, to):
         to[...] = jnp.zeros_like(to)
@@ -506,11 +501,12 @@
     z_step(3)
     y_step(2)
     gp_second()
-    each_other(lambda m: res_copy(m, me).wait_send())
-    lax.fori_loop(0, NZ, lambda i, carry: (pair_copy(i).wait_send(), carry)[1], 0)
+    all_copies(res_recv, 2).wait_send()
     z_last()
     y_step(3)
     gp_third()
+    for i, ref in enumerate((z_send.at[pl.ds(0, 7)], y_send.at[pl.ds(0, 7)], y_pair_send)):
+        message(lambda: (ref, ref), "ring", sibling, ring_sem.at[i]).wait_send()
     flush()
 
     mine = y_part(0)
@@ -553,9 +549,7 @@
         scratch_shapes=[
             pltpu.VMEM((NZ, NYL, ROWS, DT), BF16),
             pltpu.VMEM((NZ, NYL, ROWS, DS), BF16),
-            pltpu.VMEM((NZ, DT, GROUP), BF16),
-            pltpu.VMEM((NZ, DS, GROUP), BF16),
-            pltpu.VMEM((BATCHES, BATCH // OWN, OWN, DT + DS), BF16),
+            pltpu.VMEM((BATCHES * SLOTS, OWN, DT + DS), BF16),
             pltpu.VMEM((DS, BATCHES * BATCH), BF16),
             pltpu.VMEM((NZ, BATCHES, BATCH, GROUP), F32),
             pltpu.VMEM((NZ, BATCHES, BATCH, GROUP), F32),
@@ -567,16 +561,14 @@
             pltpu.VMEM((OWNERS, 8, ROWS), F32),
             pltpu.VMEM((OWNERS, 8, ROWS), F32),
             pltpu.VMEM((OWNERS, 8, ROWS), F32),
-            pltpu.VMEM((4, NYL, ZF, ROWS), BF16),
-            pltpu.VMEM((4, NYL, ZF, ROWS), BF16),
+            pltpu.VMEM((8, NYL, ZF, ROWS), BF16),
             pltpu.VMEM((4, NYL, ZF, ROWS), BF16),
             pltpu.VMEM((4, NYL, ZF, ROWS), BF16),
             pltpu.VMEM((ZF, ROWS), BF16),
             pltpu.VMEM((ZF, ROWS), BF16),
             pltpu.VMEM((NZ, YF, ROWS), BF16),
             pltpu.VMEM((NZ, YF, ROWS), BF16),
-            pltpu.VMEM((4, YF, ROWS), BF16),
-            pltpu.VMEM((4, YF, ROWS), BF16),
+            pltpu.VMEM((8, YF, ROWS), BF16),
             pltpu.VMEM((4, YF, ROWS), BF16),
             pltpu.VMEM((4, YF, ROWS), BF16),
             pltpu.VMEM((BATCHES, 2, OWN, DS), F32),
@@ -589,14 +581,12 @@
             pltpu.VMEM((OWN, DS), BF16),
             pltpu.VMEM((OWN, DS), BF16),
             pltpu.SemaphoreType.DMA((6,)),
+            pltpu.SemaphoreType.DMA,
+            pltpu.SemaphoreType.DMA((3,)),
             pltpu.SemaphoreType.DMA((MESSAGES,)),
             pltpu.SemaphoreType.DMA((MESSAGES,)),
             pltpu.SemaphoreType.DMA((NZ,)),
-            pltpu.SemaphoreType.DMA((NZ,)),
-            pltpu.SemaphoreType.DMA((OWNERS,)),
-            pltpu.SemaphoreType.DMA((OWNERS,)),
-            pltpu.SemaphoreType.DMA((OWNERS,)),
-            pltpu.SemaphoreType.DMA((OWNERS,)),
+            pltpu.SemaphoreType.DMA((4,)),
         ],
         compiler_params=pltpu.CompilerParams(
             collective_id=0, has_side_effects=True, vmem_limit_bytes=VMEM_BYTES

time: 68.4 us -> 69.4 us (1.015)
  Pallas kernels: 67.3 us -> 68.7 us
    pallas_call x1, Pallas kernels: 65.6 us -> 67 us  [local(): pl.pallas_call(kernel, out_shape=outs, in_specs=[hbm] * 4, out_specs=(vme...]
where the time goes in v4:
time: 69.4 us; the launch traced here: 69.3 us
  Pallas kernels  68.7 us (99%)
    pallas_call x1, Pallas kernels, local(): pl.pallas_call(kernel, out_shape=outs, in_specs=[hbm] * 4, out_specs=(vme...  67 us
    pallas_call x1, Pallas kernels, local(): pl.pallas_call(deliver, out_shape=outs, in_specs=[hbm] * 3, out_specs=(hb...  1.69 us

profile of v4, /device:TPU:2, one launch (start us, length us, event | category | flops | bytes accessed | tf_op | source)
XLA Modules:
  0.0 69.3 jit_solution(1335533539073082227)
XLA Ops:
  0.6 67.0 %shard_map.67 = (f32[128,384]{1,0:T(8,128)}, f32[64,384]{1,0:T(8,128)}, f32[1,128]{1,0:T(1,128)}) custom-call(bf16[2,8,2,128,1024]{4,3,2,1,0:T(8,128)(2,1)} %bitcast.3, bf16[2,8,2,128,384]{4,3,2,1,0:T(8,128)(2,1)} %bitcast.4, bf16[64,1024]{1,0:T(8,128)(2,1)} %tp_hbm.1, bf16[64,384]{1,0:T(8,128)(2,1)} %sp_hbm.1), custom_call_target="tpu_custom_call" | custom-call | tf_op jit(solution)/shard_map/pallas_call | solution.py:544
  67.6 1.7 %shard_map.68 = (f32[128,384]{1,0:T(8,128)}, f32[64,384]{1,0:T(8,128)}, f32[1,128]{1,0:T(1,128)}) custom-call(f32[128,384]{1,0:T(8,128)} %get-tuple-element.9.gq_in, f32[64,384]{1,0:T(8,128)} %get-tuple-element.10.gp_in, f32[1,128]{1,0:T(1,128)} %get-tuple-element.11.div_in), custom_call_target="tpu_custom_call" | custom-call | tf_op jit(solution)/shard_map/pallas_call | solution.py:600

commit v5 on v4

--- a/solution.py
+++ b/solution.py
@@ -72,7 +72,7 @@
     z_send, z_recv_r, z_recv_l, z_pair_send, z_pair_recv,
     y_pair_send, y_pair_recv, y_send, y_recv_r, y_recv_l,
     gp, gps_send, gps_recv, gp1_send, gp1_recv, gp2_send, gp2_recv, gp3_send, gp3_recv,
-    load_sem, gather_sem, ring_sem, send_sem, recv_sem, yp_recv_sem, st_sem,
+    load_sem, known_sem, gather_sem, ring_sem, send_sem, recv_sem, yp_recv_sem, st_sem,
 ):
     t_scale = DT ** (-0.5) * LOG2E
     s_scale = DS ** (-0.5) * LOG2E
@@ -119,12 +119,9 @@
         load.start()
 
     barrier = pltpu.get_barrier_semaphore()
-    for device in (right, left, across, sibling):
+    for device in (right, left, across, sibling, up, down, y_mate):
         pl.semaphore_signal(barrier, inc=1, device_id=device, device_id_type=MESH)
-
-    for offset in offsets:
-        pl.semaphore_signal(barrier, inc=1, device_id=offset_device(*offset), device_id_type=MESH)
-    pl.semaphore_wait(barrier, 4 + OWNERS - 1)
+    pl.semaphore_wait(barrier, 7)
     loads[0].wait()
     loads[1].wait()
 
@@ -182,11 +179,10 @@
         received(slot(0, RIGHT, 0, 1), ("p", RIGHT, 1))
         spread(lambda: (slot(0, RIGHT, 0, 1), slot(0, FAR, 0, 1)), ("far",), left)
 
-    def across_on():
-        received(slot(1, SELF, 0), ("across",))
-        spread(lambda: (slot(1, SELF, 0), slot(1, LEFT, 0)), ("p1", LEFT), right)
-        spread(lambda: (slot(1, SELF, 0), slot(1, RIGHT, 0)), ("p1", RIGHT), left)
-        to_sibling(1)
+    def across_on(half):
+        received(slot(1, SELF, 0, half), ("across", half))
+        spread(lambda: (slot(1, SELF, 0, half), slot(1, LEFT, 0, half)), ("p1", LEFT), right)
+        spread(lambda: (slot(1, SELF, 0, half), slot(1, RIGHT, 0, half)), ("p1", RIGHT), left)
 
     def far_across():
         received(slot(0, FAR, 0), ("far",))
@@ -198,9 +194,10 @@
 
     half_to(LEFT, 0, right)
     half_to(RIGHT, 1, left)
-    spread(lambda: (slot(0, SELF, 0), slot(1, SELF, 0)), ("across",), across)
+    spread(lambda: (slot(0, SELF, 0, 0), slot(1, SELF, 0, 0)), ("across", 0), across)
     half_to(LEFT, 1, right)
     half_to(RIGHT, 0, left)
+    spread(lambda: (slot(0, SELF, 0, 1), slot(1, SELF, 0, 1)), ("across", 1), across)
 
     def product(i, raw):
         b, n = div(i, NZ), rem(i, NZ)
@@ -230,10 +227,21 @@
             start = (core * BATCHES + b) * part
             spt[:, start:start + part] = turned[:, core * part:(core + 1) * part]
 
+    def know(i):
+        for device in (up, down, y_mate):
+            pl.semaphore_signal(known_sem.at[i], inc=1, device_id=device, device_id_type=MESH)
+        pl.semaphore_wait(known_sem.at[i], 3)
+
+    know(0)
     far_on()
-    across_on()
+    across_on(0)
+    across_on(1)
+    to_sibling(1)
+    know(1)
     sides_to_sibling(0)
+    know(2)
     far_across()
+    know(3)
     for load in loads[2:]:
         load.wait()
 
@@ -273,7 +281,10 @@
             t_max, t_sum, s_max, s_sum, cross = joined([stat[n, b] for b in range(BATCHES)])
             whole = jnp.concatenate([t_max, t_sum, s_max, s_sum, cross, cross, cross, cross], axis=0)
             for y in range(NYL):
-                stat_send[y * NZ + n] = whole[:, y * ROWS:(y + 1) * ROWS]
+                stat_send[y * NZ + n, 0] = whole[:, y * ROWS:(y + 1) * ROWS]
+            four = jnp.concatenate([whole[0:4, :ROWS], whole[0:4, ROWS:]], axis=0)
+            for y in range(NYL):
+                stat_send[y * NZ + (n + 4) % NZ, 1] = four
 
     from_sibling(0)
     product(0, raw_a)
@@ -315,14 +326,21 @@
         turn(b)
     spread_wait()
     all_copies(stat_recv, 0).wait_recv()
-    t_max, t_sum, s_max, s_sum, cross = joined([stat_recv[m] for m in range(OWNERS)])
-    t_in, s_in = factor / t_sum, factor / s_sum
-    res_recv[me] = jnp.concatenate([t_max, t_in, s_max, s_in, t_in, t_in, t_in, t_in], axis=0)
+    def totals(parts):
+        t_max, t_sum, s_max, s_sum, cross = joined(parts)
+        t_in, s_in = factor / t_sum, factor / s_sum
+        result = jnp.concatenate([t_max, t_in, s_max, s_in, t_in, t_in, t_in, t_in], axis=0)
+        return result, (t_max, t_sum, s_max, s_sum, cross)
+
+    result, (t_max, t_sum, s_max, s_sum, cross) = totals([stat_recv[m, 0] for m in range(OWNERS)])
+    res_recv[me] = result
     for offset in offsets:
         res_copy(*offset).start()
-    div_out[...] = cross * LN2 / t_sum - (t_max * LN2 + jnp.log(t_sum)) + (s_max * LN2 + jnp.log(s_sum))
-    all_copies(stat_send, 0).wait_send()
-    all_copies(res_recv, 2).wait_recv()
+    far = []
+    for y in range(NYL):
+        parts = [stat_recv[m, 1, 4 * y:4 * y + 4] for m in range(OWNERS)]
+        far.append(totals([jnp.concatenate([p, p], axis=0) for p in parts])[0])
+    far = jnp.concatenate(far, axis=1)
 
     def group(away):
         return rem(z + NZ + away, NZ)
@@ -334,9 +352,10 @@
     def lanes(n):
         return pl.ds(pl.multiple_of(n * GROUP, GROUP), GROUP)
 
-    def form(i):
+    def form(i, res=None):
         n = sequence(i)
-        res = jnp.concatenate([res_recv[n], res_recv[NZ + n]], axis=1)
+        if res is None:
+            res = jnp.concatenate([res_recv[n], res_recv[NZ + n]], axis=1)
         for b in range(BATCHES):
             st = stat[n, b]
             t_in = jnp.exp2(st[0:1] - res[0:1]) * res[1:2]
@@ -470,25 +489,31 @@
         z_pair_send[...] = gq[z, 1 - yl, :ZF].astype(BF16)
         send(lambda: (z_pair_send, z_pair_recv), "z pair", y_mate)
 
-    form(0)
+    form(0, far)
+    query_part(0)
+    pair_copy(0).start()
+    z_start()
+    div_out[...] = cross * LN2 / t_sum - (t_max * LN2 + jnp.log(t_sum)) + (s_max * LN2 + jnp.log(s_sum))
+    all_copies(stat_send, 0).wait_send()
+    all_copies(res_recv, 2).wait_recv()
+    form(1)
 
     def gradient_step(i, carry):
         query_part(i)
         form(i + 1)
         pair_copy(i).start()
 
-        @pl.when(i == 0)
-        def _():
-            z_start()
-
-        @pl.when(i == 5)
+        @pl.when(i == 3)
         def _():
             z_step(1)
+
+        @pl.when(i == 4)
+        def _():
             y_start()
 
         return carry
 
-    lax.fori_loop(0, NZ - 1, gradient_step, 0)
+    lax.fori_loop(1, NZ - 1, gradient_step, 0)
     query_part(NZ - 1)
     pair_copy(NZ - 1).start()
     passage_part(1, gp)
@@ -558,8 +583,8 @@
             pltpu.VMEM((NCORE, BATCHES, BATCH // 2, NZ * GROUP), BF16),
             pltpu.VMEM((NZ, BATCHES, 8, GROUP), F32),
             pltpu.VMEM((NZ, NYL, DS, ROWS), F32),
-            pltpu.VMEM((OWNERS, 8, ROWS), F32),
-            pltpu.VMEM((OWNERS, 8, ROWS), F32),
+            pltpu.VMEM((OWNERS, 2, 8, ROWS), F32),
+            pltpu.VMEM((OWNERS, 2, 8, ROWS), F32),
             pltpu.VMEM((OWNERS, 8, ROWS), F32),
             pltpu.VMEM((8, NYL, ZF, ROWS), BF16),
             pltpu.VMEM((4, NYL, ZF, ROWS), BF16),
@@ -581,6 +606,7 @@
             pltpu.VMEM((OWN, DS), BF16),
             pltpu.VMEM((OWN, DS), BF16),
             pltpu.SemaphoreType.DMA((6,)),
+            pltpu.SemaphoreType.REGULAR((4,)),
             pltpu.SemaphoreType.DMA,
             pltpu.SemaphoreType.DMA((3,)),
             pltpu.SemaphoreType.DMA((MESSAGES,)),

time: 69.4 us -> 68 us (0.980)
  Pallas kernels: 68.7 us -> 67.3 us
    pallas_call x1, Pallas kernels: 67 us -> 65.6 us  [local(): pl.pallas_call(kernel, out_shape=outs, in_specs=[hbm] * 4, out_specs=(vme...]
where the time goes in v5:
time: 68 us; the launch traced here: 67.9 us
  Pallas kernels  67.3 us (99%)
    pallas_call x1, Pallas kernels, local(): pl.pallas_call(kernel, out_shape=outs, in_specs=[hbm] * 4, out_specs=(vme...  65.6 us
    pallas_call x1, Pallas kernels, local(): pl.pallas_call(deliver, out_shape=outs, in_specs=[hbm] * 3, out_specs=(hb...  1.69 us

profile of v5, /device:TPU:2, one launch (start us, length us, event | category | flops | bytes accessed | tf_op | source)
XLA Modules:
  0.0 67.9 jit_solution(3643725096600973309)
XLA Ops:
  0.6 65.6 %shard_map.67 = (f32[128,384]{1,0:T(8,128)}, f32[64,384]{1,0:T(8,128)}, f32[1,128]{1,0:T(1,128)}) custom-call(bf16[2,8,2,128,1024]{4,3,2,1,0:T(8,128)(2,1)} %bitcast.3, bf16[2,8,2,128,384]{4,3,2,1,0:T(8,128)(2,1)} %bitcast.4, bf16[64,1024]{1,0:T(8,128)(2,1)} %tp_hbm.1, bf16[64,384]{1,0:T(8,128)(2,1)} %sp_hbm.1), custom_call_target="tpu_custom_call" | custom-call | tf_op jit(solution)/shard_map/pallas_call | solution.py:569
  66.2 1.7 %shard_map.68 = (f32[128,384]{1,0:T(8,128)}, f32[64,384]{1,0:T(8,128)}, f32[1,128]{1,0:T(1,128)}) custom-call(f32[128,384]{1,0:T(8,128)} %get-tuple-element.9.gq_in, f32[64,384]{1,0:T(8,128)} %get-tuple-element.10.gp_in, f32[1,128]{1,0:T(1,128)} %get-tuple-element.11.div_in), custom_call_target="tpu_custom_call" | custom-call | tf_op jit(solution)/shard_map/pallas_call | solution.py:626

commit v6 on v5

--- a/solution.py
+++ b/solution.py
@@ -12,8 +12,6 @@
 OWN = 64
 ROWS = 128
 DT, DS = 1024, 384
-BATCHES = 4
-SLOTS = 4
 BATCH = 256
 GROUP = NYL * ROWS
 OWNERS = NYL * NZ
@@ -28,12 +26,24 @@
 SELF, LEFT, RIGHT, FAR = 0, 1, 2, 3
 
 
-def place(h, where, core):
-    if where == SELF:
-        return 1, core * 2 + h
-    if where == FAR:
-        return 3, core * 2 + h
-    return 2 * h, core * 2 + (where - LEFT)
+BATCH_SLOTS = (0, 2), (2, 4), (6, 4), (10, 4), (14, 2)
+BATCHES = len(BATCH_SLOTS)
+SLOTS = 16
+PLACES = 8
+
+
+def place(h, where):
+    if h == 0:
+        return {SELF: 0, LEFT: 1, RIGHT: 2, FAR: 4}[where]
+    return {SELF: 3, LEFT: 5, RIGHT: 6, FAR: 7}[where]
+
+
+def slot_of(h, where, core):
+    p = place(h, where)
+    for first, count in BATCH_SLOTS:
+        if p < count // 2:
+            return first + p + core * (count // 2)
+        p -= count // 2
 
 
 def div(a, b):
@@ -100,17 +110,18 @@
         return at(x, yh, y_of[dy], z_of[dz], k)
 
     def slot(h, where, core, half=None):
-        b, s = place(h, where, core)
+        i = slot_of(h, where, core)
         if half is None:
-            return pbuf.at[b * SLOTS + s]
-        return pbuf.at[b * SLOTS + s, pl.ds(half * HALF, HALF)]
+            return pbuf.at[i]
+        return pbuf.at[i, pl.ds(half * HALF, HALF)]
 
     def both(b, core):
-        return pbuf.at[pl.ds(b * SLOTS + core * 2, 2)]
+        first, count = BATCH_SLOTS[b]
+        return pbuf.at[pl.ds(first + core * (count // 2), count // 2)]
 
     loads = [
-        pltpu.make_async_copy(tp_hbm, pbuf.at[SLOTS, :, pl.ds(0, DT)], load_sem.at[0]),
-        pltpu.make_async_copy(sp_hbm, pbuf.at[SLOTS, :, pl.ds(DT, DS)], load_sem.at[1]),
+        pltpu.make_async_copy(tp_hbm, pbuf.at[0, :, pl.ds(0, DT)], load_sem.at[0]),
+        pltpu.make_async_copy(sp_hbm, pbuf.at[0, :, pl.ds(DT, DS)], load_sem.at[1]),
     ]
     for y in range(NYL):
         loads.append(pltpu.make_async_copy(tq_hbm.at[y, :, k], tq.at[:, y], load_sem.at[2 + y]))
@@ -152,7 +163,7 @@
         message(refs, name, device, gather_sem).start()
 
     def spread_wait():
-        everything = pbuf.at[pl.ds(0, BATCHES * SLOTS - 1)]
+        everything = pbuf.at[pl.ds(0, SLOTS - 1)]
         message(lambda: (everything, everything), "gather", sibling, gather_sem).wait_send()
 
     def half_to(where, half, device):
@@ -165,7 +176,7 @@
         else:
             received(slot(1, LEFT, 0), ("p1", LEFT))
             received(slot(1, RIGHT, 0), ("p1", RIGHT))
-        to_sibling(2 * h)
+        to_sibling(3 if h else 1)
 
     def to_sibling(b):
         spread(lambda: (both(b, 0), both(b, 1)), ("sib", b), sibling)
@@ -187,10 +198,11 @@
     def far_across():
         received(slot(0, FAR, 0), ("far",))
         spread(lambda: (slot(0, FAR, 0), slot(1, FAR, 0)), ("far across",), across)
+        to_sibling(2)
 
     def far_from_across():
         received(slot(1, FAR, 0), ("far across",))
-        to_sibling(3)
+        to_sibling(4)
 
     half_to(LEFT, 0, right)
     half_to(RIGHT, 1, left)
@@ -198,34 +210,51 @@
     half_to(LEFT, 1, right)
     half_to(RIGHT, 0, left)
     spread(lambda: (slot(0, SELF, 0, 1), slot(1, SELF, 0, 1)), ("across", 1), across)
-
-    def product(i, raw):
-        b, n = div(i, NZ), rem(i, NZ)
-        batch = pbuf[pl.ds(b * SLOTS, SLOTS)].reshape(BATCH, DT + DS)
+    to_sibling(0)
+
+    def product(slots, n, raw):
+        first, count = slots
+        batch = pbuf[pl.ds(first, count)].reshape(count * OWN, DT + DS)
         raw[0] = nt(batch[:, :DT], tq[n].reshape(GROUP, DT))
         raw[1] = nt(batch[:, DT:], sq[n].reshape(GROUP, DS))
 
-    def weights(i, raw):
-        b, n = div(i, NZ), rem(i, NZ)
+    def weights(b, row, n, raw, size):
         t = raw[0] * t_scale
         s = raw[1] * s_scale
         t_max = jnp.max(t, axis=0, keepdims=True)
         s_max = jnp.max(s, axis=0, keepdims=True)
         t_weight = jnp.exp2(t - t_max)
         s_weight = jnp.exp2(s - s_max)
-        tw[n, b] = t_weight
-        sw[n, b] = s_weight
+        tw[n, pl.ds(row, size)] = t_weight
+        sw[n, pl.ds(row, size)] = s_weight
         t_sum = jnp.sum(t_weight, axis=0, keepdims=True)
         s_sum = jnp.sum(s_weight, axis=0, keepdims=True)
         cross = jnp.sum(t_weight * (t - s), axis=0, keepdims=True)
         stat[n, b] = jnp.concatenate([t_max, t_sum, s_max, s_sum, cross, cross, cross, cross], axis=0)
 
-    def turn(b):
-        turned = pbuf[b * SLOTS:(b + 1) * SLOTS].reshape(BATCH, DT + DS)[:, DT:].T
-        part = BATCH // NCORE
+    def small_scores(b, first):
+        slots = BATCH_SLOTS[b]
+        row, size = slots[0] * OWN, slots[1] * OWN
+        half_a, half_b = raw_a.at[:, pl.ds(0, size)], raw_b.at[:, pl.ds(0, size)]
+
+        def body(i, carry):
+            n = first + 2 * i
+            product(slots, n, half_a)
+            product(slots, n + 1, half_b)
+            weights(b, row, n, half_a, size)
+            weights(b, row, n + 1, half_b, size)
+            return carry
+
+        lax.fori_loop(0, 2, body, 0)
+
+    def turn():
         for core in range(NCORE):
-            start = (core * BATCHES + b) * part
-            spt[:, start:start + part] = turned[:, core * part:(core + 1) * part]
+            rows = [
+                pbuf[first + core * (count // 2):first + (core + 1) * (count // 2)].reshape(-1, DT + DS)[:, DT:]
+                for first, count in BATCH_SLOTS
+            ]
+            size = PLACES * OWN
+            spt[:, core * size:(core + 1) * size] = jnp.concatenate(rows, axis=0).T
 
     def know(i):
         for device in (up, down, y_mate):
@@ -233,17 +262,18 @@
         pl.semaphore_wait(known_sem.at[i], 3)
 
     know(0)
+    for load in loads[2:]:
+        load.wait()
+    from_sibling(0)
+    small_scores(0, 0)
     far_on()
     across_on(0)
+    know(1)
+    small_scores(0, 4)
     across_on(1)
-    to_sibling(1)
-    know(1)
     sides_to_sibling(0)
     know(2)
-    far_across()
     know(3)
-    for load in loads[2:]:
-        load.wait()
 
     def joined(parts):
         t_max = functools.reduce(jnp.maximum, [p[0:1] for p in parts])
@@ -286,44 +316,55 @@
             for y in range(NYL):
                 stat_send[y * NZ + (n + 4) % NZ, 1] = four
 
-    from_sibling(0)
-    product(0, raw_a)
+    large = 3 * NZ
+    size = 4 * OWN
+
+    def large_product(i, raw):
+        product((2 + 4 * div(i, NZ), 4), rem(i, NZ), raw)
+
+    def large_weights(i, raw):
+        b = div(i, NZ)
+        weights(1 + b, pl.multiple_of(2 * OWN + b * size, 2 * OWN), rem(i, NZ), raw, size)
+
+    from_sibling(1)
+    large_product(0, raw_a)
 
     def score_step(j, carry):
+        @pl.when(j == 1)
+        def _():
+            far_across()
+
         @pl.when(j == 3)
         def _():
-            from_sibling(1)
-
-        @pl.when(j == 5)
+            from_sibling(2)
+
+        @pl.when(j == 6)
         def _():
             sides_to_sibling(1)
 
         @pl.when(j == 7)
         def _():
+            from_sibling(3)
+
+        @pl.when(j == 10)
+        def _():
             far_from_across()
-            from_sibling(2)
-
-        @pl.when(j == 11)
-        def _():
-            from_sibling(3)
-
-        @pl.when(j == 14)
-        def _():
-            leave(0)
-
-        product(2 * j + 1, raw_b)
-        weights(2 * j, raw_a)
-        product(jnp.minimum(2 * j + 2, BATCHES * NZ - 1), raw_a)
-        weights(2 * j + 1, raw_b)
+
+        large_product(2 * j + 1, raw_b)
+        large_weights(2 * j, raw_a)
+        large_product(jnp.minimum(2 * j + 2, large - 1), raw_a)
+        large_weights(2 * j + 1, raw_b)
         return carry
 
-    lax.fori_loop(0, BATCHES * NZ // 2, score_step, 0)
-    leave(4)
+    lax.fori_loop(0, large // 2, score_step, 0)
+    from_sibling(4)
+    for first in (0, 4):
+        small_scores(4, first)
+        leave(first)
     for offset in offsets:
         stat_copy(*offset).start()
     stat_recv[0] = stat_send[me]
-    for b in range(BATCHES):
-        turn(b)
+    turn()
     spread_wait()
     all_copies(stat_recv, 0).wait_recv()
     def totals(parts):
@@ -356,13 +397,16 @@
         n = sequence(i)
         if res is None:
             res = jnp.concatenate([res_recv[n], res_recv[NZ + n]], axis=1)
-        for b in range(BATCHES):
+        for b, (first, count) in enumerate(BATCH_SLOTS):
             st = stat[n, b]
             t_in = jnp.exp2(st[0:1] - res[0:1]) * res[1:2]
             s_in = jnp.exp2(st[2:3] - res[2:3]) * res[3:4]
-            grad = (sw[n, b] * s_in - tw[n, b] * t_in).astype(BF16)
-            gt[0, b, :, lanes(n)] = grad[:BATCH // 2]
-            gt[1, b, :, lanes(n)] = grad[BATCH // 2:]
+            rows = pl.ds(first * OWN, count * OWN)
+            grad = (sw[n, rows] * s_in - tw[n, rows] * t_in).astype(BF16)
+            half = count * OWN // 2
+            rows = pl.ds(first * OWN // 2, half)
+            gt[0, rows, lanes(n)] = grad[:half]
+            gt[1, rows, lanes(n)] = grad[half:]
 
     def pair_copy(i):
         return pltpu.make_async_remote_copy(
@@ -373,7 +417,7 @@
 
     def query_part(i):
         n = sequence(i)
-        total = nn(spt[...], gt[:, :, :, lanes(n)].reshape(NCORE * BATCHES * BATCH // 2, GROUP))
+        total = nn(spt[...], gt[:, :, lanes(n)].reshape(NCORE * PLACES * OWN, GROUP))
         gq[n, 0] = total[:, :ROWS]
         gq[n, 1] = total[:, ROWS:]
         y_pair_send[i] = gq[n, 1 - yl, ZF:].astype(BF16)
@@ -443,16 +487,14 @@
         to[...] = jnp.zeros_like(to)
 
         def body(n, carry):
-            grads = gt[core, :, :, lanes(n)].reshape(BATCHES * BATCH // 2, GROUP)
-            term = nn(grads, sq[n].reshape(GROUP, DS))
-            to[...] = to[...] + term.reshape(BATCHES, 2, OWN, DS)
+            term = nn(gt[core, :, lanes(n)], sq[n].reshape(GROUP, DS))
+            to[...] = to[...] + term.reshape(PLACES, OWN, DS)
             return carry
 
         lax.fori_loop(0, NZ, body, 0)
 
     def gp_of(h, where):
-        b, s = place(h, where, 0)
-        return gp[b, s]
+        return gp[place(h, where)]
 
     def gp_first():
         received(gps_recv, "gp sibling")
@@ -574,13 +616,13 @@
         scratch_shapes=[
             pltpu.VMEM((NZ, NYL, ROWS, DT), BF16),
             pltpu.VMEM((NZ, NYL, ROWS, DS), BF16),
-            pltpu.VMEM((BATCHES * SLOTS, OWN, DT + DS), BF16),
-            pltpu.VMEM((DS, BATCHES * BATCH), BF16),
-            pltpu.VMEM((NZ, BATCHES, BATCH, GROUP), F32),
-            pltpu.VMEM((NZ, BATCHES, BATCH, GROUP), F32),
+            pltpu.VMEM((SLOTS, OWN, DT + DS), BF16),
+            pltpu.VMEM((DS, SLOTS * OWN), BF16),
+            pltpu.VMEM((NZ, SLOTS * OWN, GROUP), F32),
+            pltpu.VMEM((NZ, SLOTS * OWN, GROUP), F32),
             pltpu.VMEM((2, BATCH, GROUP), F32),
             pltpu.VMEM((2, BATCH, GROUP), F32),
-            pltpu.VMEM((NCORE, BATCHES, BATCH // 2, NZ * GROUP), BF16),
+            pltpu.VMEM((NCORE, PLACES * OWN, NZ * GROUP), BF16),
             pltpu.VMEM((NZ, BATCHES, 8, GROUP), F32),
             pltpu.VMEM((NZ, NYL, DS, ROWS), F32),
             pltpu.VMEM((OWNERS, 2, 8, ROWS), F32),
@@ -596,9 +638,9 @@
             pltpu.VMEM((8, YF, ROWS), BF16),
             pltpu.VMEM((4, YF, ROWS), BF16),
             pltpu.VMEM((4, YF, ROWS), BF16),
-            pltpu.VMEM((BATCHES, 2, OWN, DS), F32),
-            pltpu.VMEM((BATCHES, 2, OWN, DS), BF16),
-            pltpu.VMEM((BATCHES, 2, OWN, DS), BF16),
+            pltpu.VMEM((PLACES, OWN, DS), F32),
+            pltpu.VMEM((PLACES, OWN, DS), BF16),
+            pltpu.VMEM((PLACES, OWN, DS), BF16),
             pltpu.VMEM((NYH, OWN, DS), BF16),
             pltpu.VMEM((NYH, OWN, DS), BF16),
             pltpu.VMEM((2, NYH, OWN, DS), BF16),

time: 68 us -> 69 us (1.015)
  Pallas kernels: 67.3 us -> 68.3 us
    pallas_call x1, Pallas kernels: 65.6 us -> 66.6 us  [local(): pl.pallas_call(kernel, out_shape=outs, in_specs=[hbm] * 4, out_specs=(vme...]
where the time goes in v6:
time: 69 us; the launch traced here: 68.9 us
  Pallas kernels  68.3 us (99%)
    pallas_call x1, Pallas kernels, local(): pl.pallas_call(kernel, out_shape=outs, in_specs=[hbm] * 4, out_specs=(vme...  66.6 us
    pallas_call x1, Pallas kernels, local(): pl.pallas_call(deliver, out_shape=outs, in_specs=[hbm] * 3, out_specs=(hb...  1.69 us

profile of v6, /device:TPU:2, one launch (start us, length us, event | category | flops | bytes accessed | tf_op | source)
XLA Modules:
  0.0 68.9 jit_solution(9607923855619120914)
XLA Ops:
  0.6 66.6 %shard_map.67 = (f32[128,384]{1,0:T(8,128)}, f32[64,384]{1,0:T(8,128)}, f32[1,128]{1,0:T(1,128)}) custom-call(bf16[2,8,2,128,1024]{4,3,2,1,0:T(8,128)(2,1)} %bitcast.3, bf16[2,8,2,128,384]{4,3,2,1,0:T(8,128)(2,1)} %bitcast.4, bf16[64,1024]{1,0:T(8,128)(2,1)} %tp_hbm.1, bf16[64,384]{1,0:T(8,128)(2,1)} %sp_hbm.1), custom_call_target="tpu_custom_call" | custom-call | tf_op jit(solution)/shard_map/pallas_call | solution.py:611
  67.2 1.7 %shard_map.68 = (f32[128,384]{1,0:T(8,128)}, f32[64,384]{1,0:T(8,128)}, f32[1,128]{1,0:T(1,128)}) custom-call(f32[128,384]{1,0:T(8,128)} %get-tuple-element.9.gq_in, f32[64,384]{1,0:T(8,128)} %get-tuple-element.10.gp_in, f32[1,128]{1,0:T(1,128)} %get-tuple-element.11.div_in), custom_call_target="tpu_custom_call" | custom-call | tf_op jit(solution)/shard_map/pallas_call | solution.py:668

commit v7 on v6

--- a/solution.py
+++ b/solution.py
@@ -79,8 +79,8 @@
     gq_out, gp_out, div_out,
     tq, sq, pbuf, spt, tw, sw, raw_a, raw_b, gt, stat, gq,
     stat_send, stat_recv, res_recv,
-    z_send, z_recv_r, z_recv_l, z_pair_send, z_pair_recv,
-    y_pair_send, y_pair_recv, y_send, y_recv_r, y_recv_l,
+    z_send, z_recv, z_pair_send, z_pair_recv,
+    y_pair_send, y_pair_recv, y_send, y_recv,
     gp, gps_send, gps_recv, gp1_send, gp1_recv, gp2_send, gp2_recv, gp3_send, gp3_recv,
     load_sem, known_sem, gather_sem, ring_sem, send_sem, recv_sem, yp_recv_sem, st_sem,
 ):
@@ -262,17 +262,17 @@
         pl.semaphore_wait(known_sem.at[i], 3)
 
     know(0)
+    far_on()
+    across_on(0)
+    know(1)
     for load in loads[2:]:
         load.wait()
     from_sibling(0)
     small_scores(0, 0)
-    far_on()
-    across_on(0)
-    know(1)
+    across_on(1)
+    know(2)
     small_scores(0, 4)
-    across_on(1)
     sides_to_sibling(0)
-    know(2)
     know(3)
 
     def joined(parts):
@@ -411,7 +411,7 @@
     def pair_copy(i):
         return pltpu.make_async_remote_copy(
             src_ref=y_pair_send.at[i], dst_ref=y_pair_recv.at[i],
-            send_sem=ring_sem.at[2], recv_sem=yp_recv_sem.at[i],
+            send_sem=ring_sem.at[3], recv_sem=yp_recv_sem.at[i],
             device_id=y_mate, device_id_type=MESH,
         )
 
@@ -422,66 +422,63 @@
         gq[n, 1] = total[:, ROWS:]
         y_pair_send[i] = gq[n, 1 - yl, ZF:].astype(BF16)
 
-    def z_part(away):
-        return gq[group(away), :, :ZF]
-
-    def y_part(away):
-        i = (4, 3, -3, 2, -2, 1, -1, 0).index(away)
-        pair_copy(i).wait_recv()
-        return gq[group(away), yl, ZF:] + y_pair_recv[i].astype(F32)
-
-    ZH, YH = ZF // 2, YF // 2
-
-    def z_start():
-        far = z_part(4).astype(BF16)
-        z_send[0] = far
-        message(lambda: (z_send.at[0, :, pl.ds(0, ZH)], z_recv_r.at[0, :, pl.ds(0, ZH)]), ("zr", 0), up, ring_sem.at[0]).start()
-        message(lambda: (z_send.at[0, :, pl.ds(ZH, ZH)], z_recv_l.at[0, :, pl.ds(ZH, ZH)]), ("zl", 0), down, ring_sem.at[0]).start()
-
-    def y_start():
-        y_send[0] = y_part(4).astype(BF16)
-        message(lambda: (y_send.at[0, pl.ds(0, YH)], y_recv_r.at[0, pl.ds(0, YH)]), ("yr", 0), up, ring_sem.at[1]).start()
-        message(lambda: (y_send.at[0, pl.ds(YH, YH)], y_recv_l.at[0, pl.ds(YH, YH)]), ("yl", 0), down, ring_sem.at[1]).start()
-
-    def z_step(step):
-        if step == 1:
-            mine = z_part(3)
-            received(z_recv_r.at[0, :, pl.ds(0, ZH)], ("zr", 0))
-            z_send[1, :, :ZH] = (mine[:, :ZH] + z_recv_r[0, :, :ZH].astype(F32)).astype(BF16)
-            z_send[1, :, ZH:] = mine[:, ZH:].astype(BF16)
+    ORDER = (4, 3, -3, 2, -2, 1, -1, 0)
+
+    rings = (z_send.at[0], z_recv.at[0]), (z_send.at[1], z_recv.at[1]), (y_send, y_recv)
+
+    def part(chain, away):
+        n = group(away)
+        if chain < 2:
+            return gq[n, chain, :ZF]
+        return gq[n, yl, ZF:] + y_pair_recv[ORDER.index(away)].astype(F32)
+
+    def pair_arrived(away):
+        pair_copy(ORDER.index(away)).wait_recv()
+
+    def ring_message(chain, way, step, rows):
+        sends, recvs = rings[chain]
+        return message(
+            lambda: (sends.at[4 * way + step, rows], recvs.at[4 * way + step, rows]), ("ring", chain, way, step),
+            down if way else up, ring_sem.at[chain],
+        )
+
+    def rows_of(chain, way, step):
+        if chain == 2 and step == 0:
+            return pl.ds(way * (YF // 2), YF // 2)
+        return pl.ds(0, ZF)
+
+    def come(chain, way, step):
+        rows = rows_of(chain, way, step)
+        ring_message(chain, way, step, rows).wait_recv()
+        return rings[chain][1][4 * way + step, rows].astype(F32)
+
+    def ring_start(chain, way):
+        rows = rows_of(chain, way, 0)
+        rings[chain][0][4 * way, rows] = part(chain, 4)[rows.start:rows.start + rows.size].astype(BF16)
+        ring_message(chain, way, 0, rows).start()
+
+    def ring_step(chain, way, step):
+        total = part(chain, 4 - step if way == 0 else step - 4)
+        to = rings[chain][0]
+        if step == 1 and chain == 2:
+            h = YF // 2
+            halves = [total[:h], total[h:]]
+            halves[way] = halves[way] + come(chain, way, 0)
+            to[4 * way + step, :h] = halves[0].astype(BF16)
+            to[4 * way + step, h:] = halves[1].astype(BF16)
         else:
-            received(z_recv_r.at[step - 1], ("zr", step - 1))
-            z_send[step] = (z_part(4 - step) + z_recv_r[step - 1].astype(F32)).astype(BF16)
-        message(lambda step=step: (z_send.at[step], z_recv_r.at[step]), ("zr", step), up, ring_sem.at[0]).start()
-        if step == 1:
-            mine = z_part(-3)
-            received(z_recv_l.at[0, :, pl.ds(ZH, ZH)], ("zl", 0))
-            z_send[5, :, :ZH] = mine[:, :ZH].astype(BF16)
-            z_send[5, :, ZH:] = (mine[:, ZH:] + z_recv_l[0, :, ZH:].astype(F32)).astype(BF16)
-        else:
-            received(z_recv_l.at[step - 1], ("zl", step - 1))
-            z_send[4 + step] = (z_part(step - 4) + z_recv_l[step - 1].astype(F32)).astype(BF16)
-        message(lambda step=step: (z_send.at[4 + step], z_recv_l.at[step]), ("zl", step), down, ring_sem.at[0]).start()
-
-    def y_step(step):
-        mine = y_part(4 - step)
-        if step == 1:
-            received(y_recv_r.at[0, pl.ds(0, YH)], ("yr", 0))
-            y_send[1, :YH] = (mine[:YH] + y_recv_r[0, :YH].astype(F32)).astype(BF16)
-            y_send[1, YH:] = mine[YH:].astype(BF16)
-        else:
-            received(y_recv_r.at[step - 1], ("yr", step - 1))
-            y_send[step] = (mine + y_recv_r[step - 1].astype(F32)).astype(BF16)
-        message(lambda step=step: (y_send.at[step], y_recv_r.at[step]), ("yr", step), up, ring_sem.at[1]).start()
-        mine = y_part(step - 4)
-        if step == 1:
-            received(y_recv_l.at[0, pl.ds(YH, YH)], ("yl", 0))
-            y_send[5, :YH] = mine[:YH].astype(BF16)
-            y_send[5, YH:] = (mine[YH:] + y_recv_l[0, YH:].astype(F32)).astype(BF16)
-        else:
-            received(y_recv_l.at[step - 1], ("yl", step - 1))
-            y_send[4 + step] = (mine + y_recv_l[step - 1].astype(F32)).astype(BF16)
-        message(lambda step=step: (y_send.at[4 + step], y_recv_l.at[step]), ("yl", step), down, ring_sem.at[1]).start()
+            if step > 1 or chain == way:
+                total = total + come(chain, way, step - 1)
+            to[4 * way + step] = total.astype(BF16)
+        ring_message(chain, way, step, pl.ds(0, ZF)).start()
+
+    def ring_steps(chains, step):
+        for chain in chains:
+            for way in (0, 1):
+                ring_step(chain, way, step)
+
+    def ring_total(chain):
+        return part(chain, 0) + come(chain, 0, 3) + come(chain, 1, 3)
 
     def passage_part(core, to):
         to[...] = jnp.zeros_like(to)
@@ -523,18 +520,11 @@
     def x_total(h):
         return gp_of(h, SELF) + gp2_recv[0, h].astype(F32) + gp2_recv[1, h].astype(F32)
 
-    def z_last():
-        received(z_recv_r.at[3], ("zr", 3))
-        received(z_recv_l.at[3], ("zl", 3))
-        for y in range(NYL):
-            gq[z, y, :ZF] = gq[z, y, :ZF] + z_recv_r[3, y].astype(F32) + z_recv_l[3, y].astype(F32)
-        z_pair_send[...] = gq[z, 1 - yl, :ZF].astype(BF16)
-        send(lambda: (z_pair_send, z_pair_recv), "z pair", y_mate)
-
     form(0, far)
     query_part(0)
+    ring_start(0, 0)
+    ring_start(1, 1)
     pair_copy(0).start()
-    z_start()
     div_out[...] = cross * LN2 / t_sum - (t_max * LN2 + jnp.log(t_sum)) + (s_max * LN2 + jnp.log(s_sum))
     all_copies(stat_send, 0).wait_send()
     all_copies(res_recv, 2).wait_recv()
@@ -543,43 +533,61 @@
     def gradient_step(i, carry):
         query_part(i)
         form(i + 1)
+
+        @pl.when(i == 1)
+        def _():
+            ring_step(1, 0, 1)
+
+        @pl.when(i == 2)
+        def _():
+            ring_step(0, 1, 1)
+            ring_step(0, 0, 1)
+            ring_step(1, 1, 1)
+
         pair_copy(i).start()
 
         @pl.when(i == 3)
         def _():
-            z_step(1)
-
-        @pl.when(i == 4)
-        def _():
-            y_start()
+            pair_arrived(4)
+            ring_start(2, 0)
+            ring_start(2, 1)
+
+        @pl.when(i == 6)
+        def _():
+            pair_arrived(3)
+            pair_arrived(-3)
+            ring_steps((2,), 1)
 
         return carry
 
     lax.fori_loop(1, NZ - 1, gradient_step, 0)
     query_part(NZ - 1)
     pair_copy(NZ - 1).start()
+    ring_steps((0, 1), 2)
     passage_part(1, gp)
     gps_send[...] = gp[...].astype(BF16)
     send(lambda: (gps_send, gps_recv), "gp sibling", sibling)
-    z_step(2)
-    y_step(1)
+    pair_arrived(2)
+    pair_arrived(-2)
+    ring_steps((2,), 2)
     passage_part(0, gp)
     gp_first()
-    z_step(3)
-    y_step(2)
+    ring_steps((0, 1), 3)
+    pair_arrived(1)
+    pair_arrived(-1)
+    ring_steps((2,), 3)
     gp_second()
     all_copies(res_recv, 2).wait_send()
-    z_last()
-    y_step(3)
+    for y in range(NYL):
+        gq[z, y, :ZF] = ring_total(y)
+    z_pair_send[...] = gq[z, 1 - yl, :ZF].astype(BF16)
+    send(lambda: (z_pair_send, z_pair_recv), "z pair", y_mate)
     gp_third()
-    for i, ref in enumerate((z_send.at[pl.ds(0, 7)], y_send.at[pl.ds(0, 7)], y_pair_send)):
+    pair_arrived(0)
+    gq_out[:, ZF:] = ring_total(2).T
+    for i, ref in enumerate((z_send.at[0, pl.ds(0, 7)], z_send.at[1, pl.ds(0, 7)], y_send.at[pl.ds(0, 7)], y_pair_send)):
         message(lambda: (ref, ref), "ring", sibling, ring_sem.at[i]).wait_send()
     flush()
-
-    mine = y_part(0)
-    received(y_recv_r.at[3], ("yr", 3))
-    received(y_recv_l.at[3], ("yl", 3))
-    gq_out[:, ZF:] = (mine + y_recv_r[3].astype(F32) + y_recv_l[3].astype(F32)).T
     received(z_pair_recv, "z pair")
     gq_out[:, :ZF] = (gq[z, yl, :ZF] + z_pair_recv[...].astype(F32)).T
     received(gp3_recv, "gp across")
@@ -628,16 +636,14 @@
             pltpu.VMEM((OWNERS, 2, 8, ROWS), F32),
             pltpu.VMEM((OWNERS, 2, 8, ROWS), F32),
             pltpu.VMEM((OWNERS, 8, ROWS), F32),
-            pltpu.VMEM((8, NYL, ZF, ROWS), BF16),
-            pltpu.VMEM((4, NYL, ZF, ROWS), BF16),
-            pltpu.VMEM((4, NYL, ZF, ROWS), BF16),
+            pltpu.VMEM((2, 8, ZF, ROWS), BF16),
+            pltpu.VMEM((2, 8, ZF, ROWS), BF16),
             pltpu.VMEM((ZF, ROWS), BF16),
             pltpu.VMEM((ZF, ROWS), BF16),
             pltpu.VMEM((NZ, YF, ROWS), BF16),
             pltpu.VMEM((NZ, YF, ROWS), BF16),
             pltpu.VMEM((8, YF, ROWS), BF16),
-            pltpu.VMEM((4, YF, ROWS), BF16),
-            pltpu.VMEM((4, YF, ROWS), BF16),
+            pltpu.VMEM((8, YF, ROWS), BF16),
             pltpu.VMEM((PLACES, OWN, DS), F32),
             pltpu.VMEM((PLACES, OWN, DS), BF16),
             pltpu.VMEM((PLACES, OWN, DS), BF16),
@@ -650,7 +656,7 @@
             pltpu.SemaphoreType.DMA((6,)),
             pltpu.SemaphoreType.REGULAR((4,)),
             pltpu.SemaphoreType.DMA,
-            pltpu.SemaphoreType.DMA((3,)),
+            pltpu.SemaphoreType.DMA((4,)),
             pltpu.SemaphoreType.DMA((MESSAGES,)),
             pltpu.SemaphoreType.DMA((MESSAGES,)),
             pltpu.SemaphoreType.DMA((NZ,)),

time: 69 us -> 73 us (1.058)
  Pallas kernels: 68.3 us -> 72.2 us
    pallas_call x1, Pallas kernels: 66.6 us -> 70.6 us  [local(): pl.pallas_call(kernel, out_shape=outs, in_specs=[hbm] * 4, out_specs=(vme...]
where the time goes in v7:
time: 73 us; the launch traced here: 72.9 us
  Pallas kernels  72.2 us (99%)
    pallas_call x1, Pallas kernels, local(): pl.pallas_call(kernel, out_shape=outs, in_specs=[hbm] * 4, out_specs=(vme...  70.6 us
    pallas_call x1, Pallas kernels, local(): pl.pallas_call(deliver, out_shape=outs, in_specs=[hbm] * 3, out_specs=(hb...  1.69 us

profile of v7, /device:TPU:2, one launch (start us, length us, event | category | flops | bytes accessed | tf_op | source)
XLA Modules:
  0.0 72.9 jit_solution(14843727247823211398)
XLA Ops:
  0.6 70.6 %shard_map.67 = (f32[128,384]{1,0:T(8,128)}, f32[64,384]{1,0:T(8,128)}, f32[1,128]{1,0:T(1,128)}) custom-call(bf16[2,8,2,128,1024]{4,3,2,1,0:T(8,128)(2,1)} %bitcast.3, bf16[2,8,2,128,384]{4,3,2,1,0:T(8,128)(2,1)} %bitcast.4, bf16[64,1024]{1,0:T(8,128)(2,1)} %tp_hbm.1, bf16[64,384]{1,0:T(8,128)(2,1)} %sp_hbm.1), custom_call_target="tpu_custom_call" | custom-call | tf_op jit(solution)/shard_map/pallas_call | solution.py:619
  71.2 1.7 %shard_map.68 = (f32[128,384]{1,0:T(8,128)}, f32[64,384]{1,0:T(8,128)}, f32[1,128]{1,0:T(1,128)}) custom-call(f32[128,384]{1,0:T(8,128)} %get-tuple-element.9.gq_in, f32[64,384]{1,0:T(8,128)} %get-tuple-element.10.gp_in, f32[1,128]{1,0:T(1,128)} %get-tuple-element.11.div_in), custom_call_target="tpu_custom_call" | custom-call | tf_op jit(solution)/shard_map/pallas_call | solution.py:674

commit v8 on v5

--- a/solution.py
+++ b/solution.py
@@ -18,7 +18,7 @@
 GROUP = NYL * ROWS
 OWNERS = NYL * NZ
 HALF = OWN // 2
-ZF = 192
+ZF = 128
 YF = DS - ZF
 LOG2E = math.log2(math.e)
 LN2 = math.log(2.0)
@@ -440,15 +440,19 @@
         message(lambda step=step: (y_send.at[4 + step], y_recv_l.at[step]), ("yl", step), down, ring_sem.at[1]).start()
 
     def passage_part(core, to):
-        to[...] = jnp.zeros_like(to)
-
-        def body(n, carry):
-            grads = gt[core, :, :, lanes(n)].reshape(BATCHES * BATCH // 2, GROUP)
-            term = nn(grads, sq[n].reshape(GROUP, DS))
-            to[...] = to[...] + term.reshape(BATCHES, 2, OWN, DS)
+        def term(i):
+            wide = pl.ds(pl.multiple_of(i * 2 * GROUP, 2 * GROUP), 2 * GROUP)
+            grads = gt[core, :, :, wide].reshape(BATCHES * BATCH // 2, 2 * GROUP)
+            queries = sq[pl.ds(2 * i, 2)].reshape(2 * GROUP, DS)
+            return nn(grads, queries).reshape(BATCHES, 2, OWN, DS)
+
+        to[...] = term(0)
+
+        def body(i, carry):
+            to[...] = to[...] + term(i)
             return carry
 
-        lax.fori_loop(0, NZ, body, 0)
+        lax.fori_loop(1, NZ // 2, body, 0)
 
     def gp_of(h, where):
         b, s = place(h, where, 0)
@@ -491,8 +495,8 @@
 
     form(0, far)
     query_part(0)
+    z_start()
     pair_copy(0).start()
-    z_start()
     div_out[...] = cross * LN2 / t_sum - (t_max * LN2 + jnp.log(t_sum)) + (s_max * LN2 + jnp.log(s_sum))
     all_copies(stat_send, 0).wait_send()
     all_copies(res_recv, 2).wait_recv()
@@ -501,11 +505,12 @@
     def gradient_step(i, carry):
         query_part(i)
         form(i + 1)
-        pair_copy(i).start()
-
-        @pl.when(i == 3)
+
+        @pl.when(i == 2)
         def _():
             z_step(1)
+
+        pair_copy(i).start()
 
         @pl.when(i == 4)
         def _():

time: 68 us -> 67.8 us (level)
  no operation moved by 1% of the time
where the time goes in v8:
time: 67.8 us; the launch traced here: 67.6 us
  Pallas kernels  66.9 us (99%)
    pallas_call x1, Pallas kernels, local(): pl.pallas_call(kernel, out_shape=outs, in_specs=[hbm] * 4, out_specs=(vme...  65.3 us
    pallas_call x1, Pallas kernels, local(): pl.pallas_call(deliver, out_shape=outs, in_specs=[hbm] * 3, out_specs=(hb...  1.69 us

profile of v8, /device:TPU:2, one launch (start us, length us, event | category | flops | bytes accessed | tf_op | source)
XLA Modules:
  0.0 67.6 jit_solution(3162485036619011451)
XLA Ops:
  0.6 65.3 %shard_map.67 = (f32[128,384]{1,0:T(8,128)}, f32[64,384]{1,0:T(8,128)}, f32[1,128]{1,0:T(1,128)}) custom-call(bf16[2,8,2,128,1024]{4,3,2,1,0:T(8,128)(2,1)} %bitcast.3, bf16[2,8,2,128,384]{4,3,2,1,0:T(8,128)(2,1)} %bitcast.4, bf16[64,1024]{1,0:T(8,128)(2,1)} %tp_hbm.1, bf16[64,384]{1,0:T(8,128)(2,1)} %sp_hbm.1), custom_call_target="tpu_custom_call" | custom-call | tf_op jit(solution)/shard_map/pallas_call | solution.py:574
  65.9 1.7 %shard_map.68 = (f32[128,384]{1,0:T(8,128)}, f32[64,384]{1,0:T(8,128)}, f32[1,128]{1,0:T(1,128)}) custom-call(f32[128,384]{1,0:T(8,128)} %get-tuple-element.9.gq_in, f32[64,384]{1,0:T(8,128)} %get-tuple-element.10.gp_in, f32[1,128]{1,0:T(1,128)} %get-tuple-element.11.div_in), custom_call_target="tpu_custom_call" | custom-call | tf_op jit(solution)/shard_map/pallas_call | solution.py:631

commit v9 on v8

--- a/solution.py
+++ b/solution.py
@@ -14,6 +14,7 @@
 DT, DS = 1024, 384
 BATCHES = 4
 SLOTS = 4
+WIDE = 2
 BATCH = 256
 GROUP = NYL * ROWS
 OWNERS = NYL * NZ
@@ -71,7 +72,7 @@
     stat_send, stat_recv, res_recv,
     z_send, z_recv_r, z_recv_l, z_pair_send, z_pair_recv,
     y_pair_send, y_pair_recv, y_send, y_recv_r, y_recv_l,
-    gp, gps_send, gps_recv, gp1_send, gp1_recv, gp2_send, gp2_recv, gp3_send, gp3_recv,
+    gp2, gps_send, gps_recv, gp1_send, gp1_recv, gp2_send, gp2_recv, gp3_send, gp3_recv,
     load_sem, known_sem, gather_sem, ring_sem, send_sem, recv_sem, yp_recv_sem, st_sem,
 ):
     t_scale = DT ** (-0.5) * LOG2E
@@ -201,7 +202,7 @@
 
     def product(i, raw):
         b, n = div(i, NZ), rem(i, NZ)
-        batch = pbuf[pl.ds(b * SLOTS, SLOTS)].reshape(BATCH, DT + DS)
+        batch = pbuf[pl.ds(b * WIDE * SLOTS, WIDE * SLOTS)].reshape(WIDE * BATCH, DT + DS)
         raw[0] = nt(batch[:, :DT], tq[n].reshape(GROUP, DT))
         raw[1] = nt(batch[:, DT:], sq[n].reshape(GROUP, DS))
 
@@ -213,8 +214,8 @@
         s_max = jnp.max(s, axis=0, keepdims=True)
         t_weight = jnp.exp2(t - t_max)
         s_weight = jnp.exp2(s - s_max)
-        tw[n, b] = t_weight
-        sw[n, b] = s_weight
+        tw[n, b] = t_weight.reshape(WIDE, BATCH, GROUP)
+        sw[n, b] = s_weight.reshape(WIDE, BATCH, GROUP)
         t_sum = jnp.sum(t_weight, axis=0, keepdims=True)
         s_sum = jnp.sum(s_weight, axis=0, keepdims=True)
         cross = jnp.sum(t_weight * (t - s), axis=0, keepdims=True)
@@ -278,7 +279,7 @@
 
     def leave(first):
         for n in range(first, first + 4):
-            t_max, t_sum, s_max, s_sum, cross = joined([stat[n, b] for b in range(BATCHES)])
+            t_max, t_sum, s_max, s_sum, cross = joined([stat[n, b] for b in range(BATCHES // WIDE)])
             whole = jnp.concatenate([t_max, t_sum, s_max, s_sum, cross, cross, cross, cross], axis=0)
             for y in range(NYL):
                 stat_send[y * NZ + n, 0] = whole[:, y * ROWS:(y + 1) * ROWS]
@@ -286,38 +287,33 @@
             for y in range(NYL):
                 stat_send[y * NZ + (n + 4) % NZ, 1] = four
 
+    tiles = BATCHES // WIDE * NZ
     from_sibling(0)
+    from_sibling(1)
     product(0, raw_a)
 
     def score_step(j, carry):
-        @pl.when(j == 3)
-        def _():
-            from_sibling(1)
-
-        @pl.when(j == 5)
+        @pl.when(j == 2)
         def _():
             sides_to_sibling(1)
 
-        @pl.when(j == 7)
+        @pl.when(j == 3)
         def _():
             far_from_across()
             from_sibling(2)
-
-        @pl.when(j == 11)
-        def _():
             from_sibling(3)
 
-        @pl.when(j == 14)
+        @pl.when(j == 6)
         def _():
             leave(0)
 
         product(2 * j + 1, raw_b)
         weights(2 * j, raw_a)
-        product(jnp.minimum(2 * j + 2, BATCHES * NZ - 1), raw_a)
+        product(jnp.minimum(2 * j + 2, tiles - 1), raw_a)
         weights(2 * j + 1, raw_b)
         return carry
 
-    lax.fori_loop(0, BATCHES * NZ // 2, score_step, 0)
+    lax.fori_loop(0, tiles // 2, score_step, 0)
     leave(4)
     for offset in offsets:
         stat_copy(*offset).start()
@@ -357,10 +353,10 @@
         if res is None:
             res = jnp.concatenate([res_recv[n], res_recv[NZ + n]], axis=1)
         for b in range(BATCHES):
-            st = stat[n, b]
+            st = stat[n, b // WIDE]
             t_in = jnp.exp2(st[0:1] - res[0:1]) * res[1:2]
             s_in = jnp.exp2(st[2:3] - res[2:3]) * res[3:4]
-            grad = (sw[n, b] * s_in - tw[n, b] * t_in).astype(BF16)
+            grad = (sw[n, b // WIDE, b % WIDE] * s_in - tw[n, b // WIDE, b % WIDE] * t_in).astype(BF16)
             gt[0, b, :, lanes(n)] = grad[:BATCH // 2]
             gt[1, b, :, lanes(n)] = grad[BATCH // 2:]
 
@@ -439,20 +435,22 @@
             y_send[4 + step] = (mine + y_recv_l[step - 1].astype(F32)).astype(BF16)
         message(lambda step=step: (y_send.at[4 + step], y_recv_l.at[step]), ("yl", step), down, ring_sem.at[1]).start()
 
-    def passage_part(core, to):
+    def passage_products():
         def term(i):
             wide = pl.ds(pl.multiple_of(i * 2 * GROUP, 2 * GROUP), 2 * GROUP)
-            grads = gt[core, :, :, wide].reshape(BATCHES * BATCH // 2, 2 * GROUP)
+            grads = gt[:, :, :, wide].reshape(BATCHES * BATCH, 2 * GROUP)
             queries = sq[pl.ds(2 * i, 2)].reshape(2 * GROUP, DS)
-            return nn(grads, queries).reshape(BATCHES, 2, OWN, DS)
-
-        to[...] = term(0)
+            return nn(grads, queries).reshape(NCORE, BATCHES, 2, OWN, DS)
+
+        gp2[...] = term(0)
 
         def body(i, carry):
-            to[...] = to[...] + term(i)
+            gp2[...] = gp2[...] + term(i)
             return carry
 
         lax.fori_loop(1, NZ // 2, body, 0)
+
+    gp = gp2.at[0]
 
     def gp_of(h, where):
         b, s = place(h, where, 0)
@@ -521,12 +519,11 @@
     lax.fori_loop(1, NZ - 1, gradient_step, 0)
     query_part(NZ - 1)
     pair_copy(NZ - 1).start()
-    passage_part(1, gp)
-    gps_send[...] = gp[...].astype(BF16)
+    passage_products()
+    gps_send[...] = gp2[1].astype(BF16)
     send(lambda: (gps_send, gps_recv), "gp sibling", sibling)
     z_step(2)
     y_step(1)
-    passage_part(0, gp)
     gp_first()
     z_step(3)
     y_step(2)
@@ -581,12 +578,12 @@
             pltpu.VMEM((NZ, NYL, ROWS, DS), BF16),
             pltpu.VMEM((BATCHES * SLOTS, OWN, DT + DS), BF16),
             pltpu.VMEM((DS, BATCHES * BATCH), BF16),
-            pltpu.VMEM((NZ, BATCHES, BATCH, GROUP), F32),
-            pltpu.VMEM((NZ, BATCHES, BATCH, GROUP), F32),
-            pltpu.VMEM((2, BATCH, GROUP), F32),
-            pltpu.VMEM((2, BATCH, GROUP), F32),
+            pltpu.VMEM((NZ, BATCHES // WIDE, WIDE, BATCH, GROUP), F32),
+            pltpu.VMEM((NZ, BATCHES // WIDE, WIDE, BATCH, GROUP), F32),
+            pltpu.VMEM((2, WIDE * BATCH, GROUP), F32),
+            pltpu.VMEM((2, WIDE * BATCH, GROUP), F32),
             pltpu.VMEM((NCORE, BATCHES, BATCH // 2, NZ * GROUP), BF16),
-            pltpu.VMEM((NZ, BATCHES, 8, GROUP), F32),
+            pltpu.VMEM((NZ, BATCHES // WIDE, 8, GROUP), F32),
             pltpu.VMEM((NZ, NYL, DS, ROWS), F32),
             pltpu.VMEM((OWNERS, 2, 8, ROWS), F32),
             pltpu.VMEM((OWNERS, 2, 8, ROWS), F32),
@@ -601,7 +598,7 @@
             pltpu.VMEM((8, YF, ROWS), BF16),
             pltpu.VMEM((4, YF, ROWS), BF16),
             pltpu.VMEM((4, YF, ROWS), BF16),
-            pltpu.VMEM((BATCHES, 2, OWN, DS), F32),
+            pltpu.VMEM((NCORE, BATCHES, 2, OWN, DS), F32),
             pltpu.VMEM((BATCHES, 2, OWN, DS), BF16),
             pltpu.VMEM((BATCHES, 2, OWN, DS), BF16),
             pltpu.VMEM((NYH, OWN, DS), BF16),

time: 67.8 us -> 68.5 us (1.010)
  Pallas kernels: 66.9 us -> 67.7 us
    pallas_call x1, Pallas kernels: 65.3 us -> 66 us  [local(): pl.pallas_call(kernel, out_shape=outs, in_specs=[hbm] * 4, out_specs=(vme...]
where the time goes in v9:
time: 68.5 us; the launch traced here: 68.3 us
  Pallas kernels  67.7 us (99%)
    pallas_call x1, Pallas kernels, local(): pl.pallas_call(kernel, out_shape=outs, in_specs=[hbm] * 4, out_specs=(vme...  66 us
    pallas_call x1, Pallas kernels, local(): pl.pallas_call(deliver, out_shape=outs, in_specs=[hbm] * 3, out_specs=(hb...  1.69 us

profile of v9, /device:TPU:2, one launch (start us, length us, event | category | flops | bytes accessed | tf_op | source)
XLA Modules:
  0.0 68.3 jit_solution(9149523068675223559)
XLA Ops:
  0.6 66.0 %shard_map.67 = (f32[128,384]{1,0:T(8,128)}, f32[64,384]{1,0:T(8,128)}, f32[1,128]{1,0:T(1,128)}) custom-call(bf16[2,8,2,128,1024]{4,3,2,1,0:T(8,128)(2,1)} %bitcast.3, bf16[2,8,2,128,384]{4,3,2,1,0:T(8,128)(2,1)} %bitcast.4, bf16[64,1024]{1,0:T(8,128)(2,1)} %tp_hbm.1, bf16[64,384]{1,0:T(8,128)(2,1)} %sp_hbm.1), custom_call_target="tpu_custom_call" | custom-call | tf_op jit(solution)/shard_map/pallas_call | solution.py:571
  66.6 1.7 %shard_map.68 = (f32[128,384]{1,0:T(8,128)}, f32[64,384]{1,0:T(8,128)}, f32[1,128]{1,0:T(1,128)}) custom-call(f32[128,384]{1,0:T(8,128)} %get-tuple-element.9.gq_in, f32[64,384]{1,0:T(8,128)} %get-tuple-element.10.gp_in, f32[1,128]{1,0:T(1,128)} %get-tuple-element.11.div_in), custom_call_target="tpu_custom_call" | custom-call | tf_op jit(solution)/shard_map/pallas_call | solution.py:628

commit v10 on v8

--- a/solution.py
+++ b/solution.py
@@ -67,7 +67,7 @@
 def kernel(
     tq_hbm, sq_hbm, tp_hbm, sp_hbm,
     gq_out, gp_out, div_out,
-    tq, sq, pbuf, spt, tw, sw, raw_a, raw_b, gt, stat, gq,
+    tq, sq, pbuf, spt, tw, sw, raw_a, raw_b, top_a, top_b, gt_a, gt_b, stat, gq,
     stat_send, stat_recv, res_recv,
     z_send, z_recv_r, z_recv_l, z_pair_send, z_pair_recv,
     y_pair_send, y_pair_recv, y_send, y_recv_r, y_recv_l,
@@ -199,18 +199,20 @@
     half_to(RIGHT, 0, left)
     spread(lambda: (slot(0, SELF, 0, 1), slot(1, SELF, 0, 1)), ("across", 1), across)
 
-    def product(i, raw):
+    def product(i, raw, top):
         b, n = div(i, NZ), rem(i, NZ)
         batch = pbuf[pl.ds(b * SLOTS, SLOTS)].reshape(BATCH, DT + DS)
-        raw[0] = nt(batch[:, :DT], tq[n].reshape(GROUP, DT))
-        raw[1] = nt(batch[:, DT:], sq[n].reshape(GROUP, DS))
-
-    def weights(i, raw):
+        t = nt(batch[:, :DT], tq[n].reshape(GROUP, DT)) * t_scale
+        raw[0] = t
+        top[0:1] = jnp.max(t, axis=0, keepdims=True)
+        s = nt(batch[:, DT:], sq[n].reshape(GROUP, DS)) * s_scale
+        raw[1] = s
+        top[1:2] = jnp.max(s, axis=0, keepdims=True)
+
+    def weights(i, raw, top):
         b, n = div(i, NZ), rem(i, NZ)
-        t = raw[0] * t_scale
-        s = raw[1] * s_scale
-        t_max = jnp.max(t, axis=0, keepdims=True)
-        s_max = jnp.max(s, axis=0, keepdims=True)
+        t, s = raw[0], raw[1]
+        t_max, s_max = top[0:1], top[1:2]
         t_weight = jnp.exp2(t - t_max)
         s_weight = jnp.exp2(s - s_max)
         tw[n, b] = t_weight
@@ -287,7 +289,7 @@
                 stat_send[y * NZ + (n + 4) % NZ, 1] = four
 
     from_sibling(0)
-    product(0, raw_a)
+    product(0, raw_a, top_a)
 
     def score_step(j, carry):
         @pl.when(j == 3)
@@ -311,10 +313,10 @@
         def _():
             leave(0)
 
-        product(2 * j + 1, raw_b)
-        weights(2 * j, raw_a)
-        product(jnp.minimum(2 * j + 2, BATCHES * NZ - 1), raw_a)
-        weights(2 * j + 1, raw_b)
+        product(2 * j + 1, raw_b, top_b)
+        weights(2 * j, raw_a, top_a)
+        product(jnp.minimum(2 * j + 2, BATCHES * NZ - 1), raw_a, top_a)
+        weights(2 * j + 1, raw_b, top_b)
         return carry
 
     lax.fori_loop(0, BATCHES * NZ // 2, score_step, 0)
@@ -352,7 +354,7 @@
     def lanes(n):
         return pl.ds(pl.multiple_of(n * GROUP, GROUP), GROUP)
 
-    def form(i, res=None):
+    def form(i, gt, p, res=None):
         n = sequence(i)
         if res is None:
             res = jnp.concatenate([res_recv[n], res_recv[NZ + n]], axis=1)
@@ -361,8 +363,8 @@
             t_in = jnp.exp2(st[0:1] - res[0:1]) * res[1:2]
             s_in = jnp.exp2(st[2:3] - res[2:3]) * res[3:4]
             grad = (sw[n, b] * s_in - tw[n, b] * t_in).astype(BF16)
-            gt[0, b, :, lanes(n)] = grad[:BATCH // 2]
-            gt[1, b, :, lanes(n)] = grad[BATCH // 2:]
+            gt[0, b, :, lanes(p)] = grad[:BATCH // 2]
+            gt[1, b, :, lanes(p)] = grad[BATCH // 2:]
 
     def pair_copy(i):
         return pltpu.make_async_remote_copy(
@@ -371,9 +373,9 @@
             device_id=y_mate, device_id_type=MESH,
         )
 
-    def query_part(i):
+    def query_part(i, gt, p):
         n = sequence(i)
-        total = nn(spt[...], gt[:, :, :, lanes(n)].reshape(NCORE * BATCHES * BATCH // 2, GROUP))
+        total = nn(spt[...], gt[:, :, :, lanes(p)].reshape(NCORE * BATCHES * BATCH // 2, GROUP))
         gq[n, 0] = total[:, :ROWS]
         gq[n, 1] = total[:, ROWS:]
         y_pair_send[i] = gq[n, 1 - yl, ZF:].astype(BF16)
@@ -440,16 +442,15 @@
         message(lambda step=step: (y_send.at[4 + step], y_recv_l.at[step]), ("yl", step), down, ring_sem.at[1]).start()
 
     def passage_part(core, to):
-        def term(i):
-            wide = pl.ds(pl.multiple_of(i * 2 * GROUP, 2 * GROUP), 2 * GROUP)
-            grads = gt[core, :, :, wide].reshape(BATCHES * BATCH // 2, 2 * GROUP)
-            queries = sq[pl.ds(2 * i, 2)].reshape(2 * GROUP, DS)
-            return nn(grads, queries).reshape(BATCHES, 2, OWN, DS)
+        def term(p):
+            grads = [gt[core, :, :, lanes(p)].reshape(BATCHES * BATCH // 2, GROUP) for gt in (gt_a, gt_b)]
+            queries = [sq[sequence(2 * p + i)].reshape(GROUP, DS) for i in (0, 1)]
+            return (nn(grads[0], queries[0]) + nn(grads[1], queries[1])).reshape(BATCHES, 2, OWN, DS)
 
         to[...] = term(0)
 
-        def body(i, carry):
-            to[...] = to[...] + term(i)
+        def body(p, carry):
+            to[...] = to[...] + term(p)
             return carry
 
         lax.fori_loop(1, NZ // 2, body, 0)
@@ -493,33 +494,35 @@
         z_pair_send[...] = gq[z, 1 - yl, :ZF].astype(BF16)
         send(lambda: (z_pair_send, z_pair_recv), "z pair", y_mate)
 
-    form(0, far)
-    query_part(0)
+    form(0, gt_a, 0, far)
+    query_part(0, gt_a, 0)
     z_start()
     pair_copy(0).start()
     div_out[...] = cross * LN2 / t_sum - (t_max * LN2 + jnp.log(t_sum)) + (s_max * LN2 + jnp.log(s_sum))
     all_copies(stat_send, 0).wait_send()
     all_copies(res_recv, 2).wait_recv()
-    form(1)
-
-    def gradient_step(i, carry):
-        query_part(i)
-        form(i + 1)
-
-        @pl.when(i == 2)
+    form(1, gt_b, 0)
+
+    def gradient_step(p, carry):
+        query_part(2 * p + 1, gt_b, p)
+        form(2 * p + 2, gt_a, p + 1)
+        pair_copy(2 * p + 1).start()
+        query_part(2 * p + 2, gt_a, p + 1)
+        form(2 * p + 3, gt_b, p + 1)
+
+        @pl.when(p == 0)
         def _():
             z_step(1)
 
-        pair_copy(i).start()
-
-        @pl.when(i == 4)
+        @pl.when(p == 1)
         def _():
             y_start()
 
+        pair_copy(2 * p + 2).start()
         return carry
 
-    lax.fori_loop(1, NZ - 1, gradient_step, 0)
-    query_part(NZ - 1)
+    lax.fori_loop(0, NZ // 2 - 1, gradient_step, 0)
+    query_part(NZ - 1, gt_b, NZ // 2 - 1)
     pair_copy(NZ - 1).start()
     passage_part(1, gp)
     gps_send[...] = gp[...].astype(BF16)
@@ -585,7 +588,10 @@
             pltpu.VMEM((NZ, BATCHES, BATCH, GROUP), F32),
             pltpu.VMEM((2, BATCH, GROUP), F32),
             pltpu.VMEM((2, BATCH, GROUP), F32),
-            pltpu.VMEM((NCORE, BATCHES, BATCH // 2, NZ * GROUP), BF16),
+            pltpu.VMEM((8, GROUP), F32),
+            pltpu.VMEM((8, GROUP), F32),
+            pltpu.VMEM((NCORE, BATCHES, BATCH // 2, NZ // 2 * GROUP), BF16),
+            pltpu.VMEM((NCORE, BATCHES, BATCH // 2, NZ // 2 * GROUP), BF16),
             pltpu.VMEM((NZ, BATCHES, 8, GROUP), F32),
             pltpu.VMEM((NZ, NYL, DS, ROWS), F32),
             pltpu.VMEM((OWNERS, 2, 8, ROWS), F32),

time: 67.8 us -> 68.5 us (1.010)
  Pallas kernels: 66.9 us -> 67.8 us
    pallas_call x1, Pallas kernels: 65.3 us -> 66.1 us  [local(): pl.pallas_call(kernel, out_shape=outs, in_specs=[hbm] * 4, out_specs=(vme...]
where the time goes in v10:
time: 68.5 us; the launch traced here: 68.4 us
  Pallas kernels  67.8 us (99%)
    pallas_call x1, Pallas kernels, local(): pl.pallas_call(kernel, out_shape=outs, in_specs=[hbm] * 4, out_specs=(vme...  66.1 us
    pallas_call x1, Pallas kernels, local(): pl.pallas_call(deliver, out_shape=outs, in_specs=[hbm] * 3, out_specs=(hb...  1.69 us

profile of v10, /device:TPU:2, one launch (start us, length us, event | category | flops | bytes accessed | tf_op | source)
XLA Modules:
  0.0 68.4 jit_solution(5338627363881675078)
XLA Ops:
  0.6 66.1 %shard_map.67 = (f32[128,384]{1,0:T(8,128)}, f32[64,384]{1,0:T(8,128)}, f32[1,128]{1,0:T(1,128)}) custom-call(bf16[2,8,2,128,1024]{4,3,2,1,0:T(8,128)(2,1)} %bitcast.3, bf16[2,8,2,128,384]{4,3,2,1,0:T(8,128)(2,1)} %bitcast.4, bf16[64,1024]{1,0:T(8,128)(2,1)} %tp_hbm.1, bf16[64,384]{1,0:T(8,128)(2,1)} %sp_hbm.1), custom_call_target="tpu_custom_call" | custom-call | tf_op jit(solution)/shard_map/pallas_call | solution.py:577
  66.7 1.7 %shard_map.68 = (f32[128,384]{1,0:T(8,128)}, f32[64,384]{1,0:T(8,128)}, f32[1,128]{1,0:T(1,128)}) custom-call(f32[128,384]{1,0:T(8,128)} %get-tuple-element.9.gq_in, f32[64,384]{1,0:T(8,128)} %get-tuple-element.10.gp_in, f32[1,128]{1,0:T(1,128)} %get-tuple-element.11.div_in), custom_call_target="tpu_custom_call" | custom-call | tf_op jit(solution)/shard_map/pallas_call | solution.py:637

commit v11 on v8

--- a/solution.py
+++ b/solution.py
@@ -92,7 +92,8 @@
     up, down = at(x, yh, yl, rem(z + 1, NZ), k), at(x, yh, yl, rem(z + NZ - 1, NZ), k)
     y_mate = at(x, yh, 1 - yl, z, k)
 
-    offsets = [(dy, dz) for dy in range(NYL) for dz in range(NZ) if (dy, dz) != (0, 0)]
+    offsets = [(dy, dz) for dz in (4, 3, 5, 2, 6, 1, 7, 0) for dy in (1, 0) if (dy, dz) != (0, 0)]
+    results_to = [offset for offset in offsets if offset[1] != 4]
     y_of = [yl, 1 - yl]
     z_of = [rem(z + dz, NZ) for dz in range(NZ)]
 
@@ -270,7 +271,7 @@
         )
 
     def all_copies(ref, first):
-        others = ref.at[pl.ds(0, OWNERS - 1)]
+        others = ref.at[pl.ds(0, len(offsets) if first == 0 else len(results_to))]
         return pltpu.make_async_remote_copy(
             src_ref=others, dst_ref=others, send_sem=st_sem.at[first], recv_sem=st_sem.at[first + 1],
             device_id=sibling, device_id_type=MESH,
@@ -334,7 +335,7 @@
 
     result, (t_max, t_sum, s_max, s_sum, cross) = totals([stat_recv[m, 0] for m in range(OWNERS)])
     res_recv[me] = result
-    for offset in offsets:
+    for offset in results_to:
         res_copy(*offset).start()
     far = []
     for y in range(NYL):

time: 67.8 us -> 65.8 us (0.971)
  Pallas kernels: 66.9 us -> 65.1 us
    pallas_call x1, Pallas kernels: 65.3 us -> 63.4 us  [local(): pl.pallas_call(kernel, out_shape=outs, in_specs=[hbm] * 4, out_specs=(vme...]
where the time goes in v11:
time: 65.8 us; the launch traced here: 65.7 us
  Pallas kernels  65.1 us (99%)
    pallas_call x1, Pallas kernels, local(): pl.pallas_call(kernel, out_shape=outs, in_specs=[hbm] * 4, out_specs=(vme...  63.4 us
    pallas_call x1, Pallas kernels, local(): pl.pallas_call(deliver, out_shape=outs, in_specs=[hbm] * 3, out_specs=(hb...  1.69 us

profile of v11, /device:TPU:2, one launch (start us, length us, event | category | flops | bytes accessed | tf_op | source)
XLA Modules:
  0.0 65.7 jit_solution(3170908647711352573)
XLA Ops:
  0.6 63.4 %shard_map.67 = (f32[128,384]{1,0:T(8,128)}, f32[64,384]{1,0:T(8,128)}, f32[1,128]{1,0:T(1,128)}) custom-call(bf16[2,8,2,128,1024]{4,3,2,1,0:T(8,128)(2,1)} %bitcast.3, bf16[2,8,2,128,384]{4,3,2,1,0:T(8,128)(2,1)} %bitcast.4, bf16[64,1024]{1,0:T(8,128)(2,1)} %tp_hbm.1, bf16[64,384]{1,0:T(8,128)(2,1)} %sp_hbm.1), custom_call_target="tpu_custom_call" | custom-call | tf_op jit(solution)/shard_map/pallas_call | solution.py:575
  64.0 1.7 %shard_map.68 = (f32[128,384]{1,0:T(8,128)}, f32[64,384]{1,0:T(8,128)}, f32[1,128]{1,0:T(1,128)}) custom-call(f32[128,384]{1,0:T(8,128)} %get-tuple-element.9.gq_in, f32[64,384]{1,0:T(8,128)} %get-tuple-element.10.gp_in, f32[1,128]{1,0:T(1,128)} %get-tuple-element.11.div_in), custom_call_target="tpu_custom_call" | custom-call | tf_op jit(solution)/shard_map/pallas_call | solution.py:632

commit v12 on v11

--- a/solution.py
+++ b/solution.py
@@ -200,14 +200,17 @@
     half_to(RIGHT, 0, left)
     spread(lambda: (slot(0, SELF, 0, 1), slot(1, SELF, 0, 1)), ("across", 1), across)
 
+    def group_of(i):
+        return rem(i, 2) * 4 + div(rem(i, NZ), 2)
+
     def product(i, raw):
-        b, n = div(i, NZ), rem(i, NZ)
+        b, n = div(i, NZ), group_of(i)
         batch = pbuf[pl.ds(b * SLOTS, SLOTS)].reshape(BATCH, DT + DS)
         raw[0] = nt(batch[:, :DT], tq[n].reshape(GROUP, DT))
         raw[1] = nt(batch[:, DT:], sq[n].reshape(GROUP, DS))
 
     def weights(i, raw):
-        b, n = div(i, NZ), rem(i, NZ)
+        b, n = div(i, NZ), group_of(i)
         t = raw[0] * t_scale
         s = raw[1] * s_scale
         t_max = jnp.max(t, axis=0, keepdims=True)
@@ -266,19 +269,19 @@
     def res_copy(dy, dz):
         return pltpu.make_async_remote_copy(
             src_ref=res_recv.at[me], dst_ref=res_recv.at[me],
-            send_sem=st_sem.at[2], recv_sem=st_sem.at[3],
+            send_sem=st_sem.at[2], recv_sem=st_sem.at[3 if dz in (3, 5) else 4],
             device_id=offset_device(dy, dz), device_id_type=MESH,
         )
 
-    def all_copies(ref, first):
-        others = ref.at[pl.ds(0, len(offsets) if first == 0 else len(results_to))]
+    def all_copies(ref, count, out, into):
+        others = ref.at[pl.ds(0, count)]
         return pltpu.make_async_remote_copy(
-            src_ref=others, dst_ref=others, send_sem=st_sem.at[first], recv_sem=st_sem.at[first + 1],
+            src_ref=others, dst_ref=others, send_sem=st_sem.at[out], recv_sem=st_sem.at[into],
             device_id=sibling, device_id_type=MESH,
         )
 
     def leave(first):
-        for n in range(first, first + 4):
+        for n in (first, first + 4, first + 1, first + 5):
             t_max, t_sum, s_max, s_sum, cross = joined([stat[n, b] for b in range(BATCHES)])
             whole = jnp.concatenate([t_max, t_sum, s_max, s_sum, cross, cross, cross, cross], axis=0)
             for y in range(NYL):
@@ -287,6 +290,11 @@
             for y in range(NYL):
                 stat_send[y * NZ + (n + 4) % NZ, 1] = four
 
+        for offset in offsets:
+            @pl.when(div(rem(z_of[offset[1]], 4), 2) == first // 2)
+            def _():
+                stat_copy(*offset).start()
+
     from_sibling(0)
     product(0, raw_a)
 
@@ -319,14 +327,12 @@
         return carry
 
     lax.fori_loop(0, BATCHES * NZ // 2, score_step, 0)
-    leave(4)
-    for offset in offsets:
-        stat_copy(*offset).start()
+    leave(2)
     stat_recv[0] = stat_send[me]
     for b in range(BATCHES):
         turn(b)
     spread_wait()
-    all_copies(stat_recv, 0).wait_recv()
+    all_copies(stat_recv, 15, 0, 1).wait_recv()
     def totals(parts):
         t_max, t_sum, s_max, s_sum, cross = joined(parts)
         t_in, s_in = factor / t_sum, factor / s_sum
@@ -365,10 +371,11 @@
             gt[0, b, :, lanes(n)] = grad[:BATCH // 2]
             gt[1, b, :, lanes(n)] = grad[BATCH // 2:]
 
-    def pair_copy(i):
+    def pair_copy(i, count):
+        slots = pl.ds(i, count)
         return pltpu.make_async_remote_copy(
-            src_ref=y_pair_send.at[i], dst_ref=y_pair_recv.at[i],
-            send_sem=ring_sem.at[2], recv_sem=yp_recv_sem.at[i],
+            src_ref=y_pair_send.at[slots], dst_ref=y_pair_recv.at[slots],
+            send_sem=ring_sem.at[2], recv_sem=yp_recv_sem.at[div(i + 1, 2)],
             device_id=y_mate, device_id_type=MESH,
         )
 
@@ -384,7 +391,8 @@
 
     def y_part(away):
         i = (4, 3, -3, 2, -2, 1, -1, 0).index(away)
-        pair_copy(i).wait_recv()
+        if away >= 0:
+            pair_copy(i, 1 if away in (4, 0) else 2).wait_recv()
         return gq[group(away), yl, ZF:] + y_pair_recv[i].astype(F32)
 
     ZH, YH = ZF // 2, YF // 2
@@ -497,13 +505,17 @@
     form(0, far)
     query_part(0)
     z_start()
-    pair_copy(0).start()
+    pair_copy(0, 1).start()
     div_out[...] = cross * LN2 / t_sum - (t_max * LN2 + jnp.log(t_sum)) + (s_max * LN2 + jnp.log(s_sum))
-    all_copies(stat_send, 0).wait_send()
-    all_copies(res_recv, 2).wait_recv()
+    all_copies(stat_send, 15, 0, 1).wait_send()
+    all_copies(res_recv, 4, 2, 3).wait_recv()
     form(1)
 
     def gradient_step(i, carry):
+        @pl.when(i == 2)
+        def _():
+            all_copies(res_recv, 9, 2, 4).wait_recv()
+
         query_part(i)
         form(i + 1)
 
@@ -511,7 +523,10 @@
         def _():
             z_step(1)
 
-        pair_copy(i).start()
+        @pl.when(rem(i, 2) == 0)
+        def _():
+            pair_copy(i - 1, 2).start()
+
 
         @pl.when(i == 4)
         def _():
@@ -521,7 +536,7 @@
 
     lax.fori_loop(1, NZ - 1, gradient_step, 0)
     query_part(NZ - 1)
-    pair_copy(NZ - 1).start()
+    pair_copy(NZ - 1, 1).start()
     passage_part(1, gp)
     gps_send[...] = gp[...].astype(BF16)
     send(lambda: (gps_send, gps_recv), "gp sibling", sibling)
@@ -532,7 +547,7 @@
     z_step(3)
     y_step(2)
     gp_second()
-    all_copies(res_recv, 2).wait_send()
+    all_copies(res_recv, 13, 2, 3).wait_send()
     z_last()
     y_step(3)
     gp_third()
@@ -618,7 +633,7 @@
             pltpu.SemaphoreType.DMA((MESSAGES,)),
             pltpu.SemaphoreType.DMA((MESSAGES,)),
             pltpu.SemaphoreType.DMA((NZ,)),
-            pltpu.SemaphoreType.DMA((4,)),
+            pltpu.SemaphoreType.DMA((5,)),
         ],
         compiler_params=pltpu.CompilerParams(
             collective_id=0, has_side_effects=True, vmem_limit_bytes=VMEM_BYTES

time: 65.8 us -> 65.3 us (level)
  no operation moved by 1% of the time
where the time goes in v12:
time: 65.3 us; the launch traced here: 65.2 us
  Pallas kernels  64.6 us (99%)
    pallas_call x1, Pallas kernels, local(): pl.pallas_call(kernel, out_shape=outs, in_specs=[hbm] * 4, out_specs=(vme...  62.9 us
    pallas_call x1, Pallas kernels, local(): pl.pallas_call(deliver, out_shape=outs, in_specs=[hbm] * 3, out_specs=(hb...  1.69 us

profile of v12, /device:TPU:2, one launch (start us, length us, event | category | flops | bytes accessed | tf_op | source)
XLA Modules:
  0.0 65.2 jit_solution(14906914762190756232)
XLA Ops:
  0.6 62.9 %shard_map.67 = (f32[128,384]{1,0:T(8,128)}, f32[64,384]{1,0:T(8,128)}, f32[1,128]{1,0:T(1,128)}) custom-call(bf16[2,8,2,128,1024]{4,3,2,1,0:T(8,128)(2,1)} %bitcast.3, bf16[2,8,2,128,384]{4,3,2,1,0:T(8,128)(2,1)} %bitcast.4, bf16[64,1024]{1,0:T(8,128)(2,1)} %tp_hbm.1, bf16[64,384]{1,0:T(8,128)(2,1)} %sp_hbm.1), custom_call_target="tpu_custom_call" | custom-call | tf_op jit(solution)/shard_map/pallas_call | solution.py:590
  63.5 1.7 %shard_map.68 = (f32[128,384]{1,0:T(8,128)}, f32[64,384]{1,0:T(8,128)}, f32[1,128]{1,0:T(1,128)}) custom-call(f32[128,384]{1,0:T(8,128)} %get-tuple-element.9.gq_in, f32[64,384]{1,0:T(8,128)} %get-tuple-element.10.gp_in, f32[1,128]{1,0:T(1,128)} %get-tuple-element.11.div_in), custom_call_target="tpu_custom_call" | custom-call | tf_op jit(solution)/shard_map/pallas_call | solution.py:647

commit v13 on v12

--- a/solution.py
+++ b/solution.py
@@ -244,7 +244,6 @@
     know(1)
     sides_to_sibling(0)
     know(2)
-    far_across()
     know(3)
     for load in loads[2:]:
         load.wait()
@@ -299,6 +298,10 @@
     product(0, raw_a)
 
     def score_step(j, carry):
+        @pl.when(j == 1)
+        def _():
+            far_across()
+
         @pl.when(j == 3)
         def _():
             from_sibling(1)
@@ -309,8 +312,11 @@
 
         @pl.when(j == 7)
         def _():
+            from_sibling(2)
+
+        @pl.when(j == 8)
+        def _():
             far_from_across()
-            from_sibling(2)
 
         @pl.when(j == 11)
         def _():

time: 65.3 us -> 65.1 us (level)
  no operation moved by 1% of the time
where the time goes in v13:
time: 65.1 us; the launch traced here: 65 us
  Pallas kernels  64.3 us (99%)
    pallas_call x1, Pallas kernels, local(): pl.pallas_call(kernel, out_shape=outs, in_specs=[hbm] * 4, out_specs=(vme...  62.6 us
    pallas_call x1, Pallas kernels, local(): pl.pallas_call(deliver, out_shape=outs, in_specs=[hbm] * 3, out_specs=(hb...  1.69 us

profile of v13, /device:TPU:2, one launch (start us, length us, event | category | flops | bytes accessed | tf_op | source)
XLA Modules:
  0.0 65.0 jit_solution(3107258426831856826)
XLA Ops:
  0.6 62.6 %shard_map.67 = (f32[128,384]{1,0:T(8,128)}, f32[64,384]{1,0:T(8,128)}, f32[1,128]{1,0:T(1,128)}) custom-call(bf16[2,8,2,128,1024]{4,3,2,1,0:T(8,128)(2,1)} %bitcast.3, bf16[2,8,2,128,384]{4,3,2,1,0:T(8,128)(2,1)} %bitcast.4, bf16[64,1024]{1,0:T(8,128)(2,1)} %tp_hbm.1, bf16[64,384]{1,0:T(8,128)(2,1)} %sp_hbm.1), custom_call_target="tpu_custom_call" | custom-call | tf_op jit(solution)/shard_map/pallas_call | solution.py:596
  63.3 1.7 %shard_map.68 = (f32[128,384]{1,0:T(8,128)}, f32[64,384]{1,0:T(8,128)}, f32[1,128]{1,0:T(1,128)}) custom-call(f32[128,384]{1,0:T(8,128)} %get-tuple-element.9.gq_in, f32[64,384]{1,0:T(8,128)} %get-tuple-element.10.gp_in, f32[1,128]{1,0:T(1,128)} %get-tuple-element.11.div_in), custom_call_target="tpu_custom_call" | custom-call | tf_op jit(solution)/shard_map/pallas_call | solution.py:653
